TPU v7x, 32 devices: a whole 2x2x4 slice. The times are simulated.
32 devices in a mesh: space: 8 (over y, x, core), tm: 2 (over z_hi), op: 2 (over z_lo).
Axes of the slice: x: 2, y: 2, z: 4 (z_hi: 2, z_lo: 2; z = z_hi * 2 + z_lo), core: 2. Of those that a mesh axis runs over, the one named last changes fastest.
Arguments:
- eigvecs: bfloat16 [2, 2, 256, 3, 16, 256], P('tm', None, None, None, 'space'), may hold values from -6 to 6
- links: float32 [2, 3, 3, 3, 2, 16, 256], P('tm', None, None, None, None, 'space'), may hold values from -2.5 to 2.5
- momenta: int32 [4, 3], P('op'), may hold values from -2 to 2
- coef_num: int32 [4, 4, 3], P(None, 'op'), may hold values from -3 to 3
- coef_den: int32 [4], replicated, may hold values from 1 to 6
- peram: bfloat16 [2, 256, 4, 4, 2, 256], P('tm'), may hold values from -0.25 to 0.25
Outputs:
- quark_lines: float32 [2, 4, 4, 4, 2, 256, 256], P('tm', 'op', None, None, None, 'space')
All inputs are finite; a program needn't handle non-finite values.
Results may differ from a plain program's by a relative error of at most 0.0053.
Values may be sent and summed in bfloat16 or wider, within the bound.
No kernel may reach another device: no remote copies, remote signals or barrier semaphores. Data moves between devices by JAX's collectives and lax.ppermute only.
A program may use at most 128 MiB of HBM per device.

v0:
```python
import functools
import itertools
import math

import jax
import jax.numpy as jnp
from jax import lax
from jax.experimental import pallas as pl
from jax.experimental.pallas import tpu as pltpu
from jax.sharding import PartitionSpec as P

LY = 32
LZ = 8
NDIR = 3
SPINS = 16
ROWS = 16
HALF = 128
VMEM_BYTES = 20 * 2**20


def from_behind(value, axis, steps):
    count = lax.axis_size(axis)
    pairs = [(source, (source + steps) % count) for source in range(count)]
    return lax.ppermute(value, axis, pairs)


def across(value, axis, mask):
    pairs = [(source, source ^ mask) for source in range(lax.axis_size(axis))]
    return lax.ppermute(value, axis, pairs)


def dot_nt(left, right):
    return lax.dot_general(
        left, right, (((1,), (1,)), ((), ())), preferred_element_type=jnp.float32
    )


def shift_y(arr):
    return pltpu.roll(arr, arr.shape[1] - LZ, 1)


def shift_z(arr):
    width = arr.shape[1]
    lane = lax.broadcasted_iota(jnp.int32, arr.shape, 1)
    near = pltpu.roll(arr, width - 1, 1)
    far = pltpu.roll(arr, LZ - 1, 1)
    return jnp.where((lane & (LZ - 1)) == LZ - 1, far, near)


def weighted_links(u_ref, phi_ref, shifted, dirs, plane, n_h, store):
    width = u_ref.shape[-1]
    for half in range(width // HALF):
        lanes = pl.ds(half * HALF, HALF)
        for col in range(3):
            acc = {}
            for slot, direc in enumerate(dirs):
                f_r = None
                f_i = None
                for col_two in range(3):
                    u_r = u_ref[direc, col, col_two, 0, pl.ds(plane, 1), lanes]
                    u_i = u_ref[direc, col, col_two, 1, pl.ds(plane, 1), lanes]
                    v_r = shifted[slot, 0, col_two, :, lanes]
                    v_i = shifted[slot, 1, col_two, :, lanes]
                    term_r = u_r * v_r - u_i * v_i
                    term_i = u_r * v_i + u_i * v_r
                    f_r = term_r if f_r is None else f_r + term_r
                    f_i = term_i if f_i is None else f_i + term_i
                for kind in range(2):
                    for hel in range(n_h):
                        p_r = phi_ref[kind, hel, direc, 0, pl.ds(plane, 1), lanes]
                        p_i = phi_ref[kind, hel, direc, 1, pl.ds(plane, 1), lanes]
                        g_r = p_r * f_r - p_i * f_i
                        g_i = p_r * f_i + p_i * f_r
                        if (kind, hel) in acc:
                            old_r, old_i = acc[kind, hel]
                            g_r, g_i = old_r + g_r, old_i + g_i
                        acc[kind, hel] = (g_r, g_i)
            for (kind, hel), (g_r, g_i) in acc.items():
                store(kind, hel, col, half, (g_r, g_i))


def plane_kernel(plane, dirs, has_part, n_out, *refs):
    refs = list(refs)
    v_ref = refs.pop(0)
    next_ref = refs.pop(0) if 0 in dirs else None
    u_ref, phi_ref = refs.pop(0), refs.pop(0)
    part_ref = refs.pop(0) if has_part else None
    out_ref = refs.pop(0)
    give_ref = refs.pop(0) if n_out else None
    g_ref, h_ref, sh_ref = refs
    n_h = phi_ref.shape[1]
    _, _, n_b, width = v_ref.shape
    kinds = (g_ref, h_ref)

    def block(step, carry):
        row = pl.multiple_of(step * ROWS, ROWS)
        rows = pl.ds(row, ROWS)
        for slot, direc in enumerate(dirs):
            for part in range(2):
                for col in range(3):
                    source = next_ref if direc == 0 else v_ref
                    field = source[part, col, rows, :].astype(jnp.float32)
                    if direc == 1:
                        field = shift_y(field)
                    elif direc == 2:
                        field = shift_z(field)
                    sh_ref[slot, part, col] = field

        def store(kind, hel, col, half, both):
            for part in range(2):
                there = pl.ds(pl.multiple_of(part * n_b + row, ROWS), ROWS)
                lanes = pl.ds(col * width + half * HALF, HALF)
                kinds[kind][hel, there, lanes] = both[part].astype(jnp.bfloat16)

        weighted_links(u_ref, phi_ref, sh_ref, dirs, plane, n_h, store)
        return carry

    lax.fori_loop(0, n_b // ROWS, block, 0)

    def multiply(hel, carry):
        mat = jnp.concatenate([v_ref[:, col].reshape(2 * n_b, width) for col in range(3)], 1)
        one = dot_nt(mat, g_ref[hel])
        two = dot_nt(h_ref[hel], mat)
        real = one[:n_b, :n_b] + one[n_b:, n_b:] + two[:n_b, :n_b] + two[n_b:, n_b:]
        imag = one[:n_b, n_b:] - one[n_b:, :n_b] + two[:n_b, n_b:] - two[n_b:, :n_b]
        for part, total in enumerate((real, imag)):
            if has_part:
                total = total + part_ref[hel, part]
            if n_out:
                core = lax.axis_index("space") & 1
                halves = total.reshape(n_out // 2, 2, n_b // n_out, n_b)
                out_ref[:, hel, part] = jnp.where(core == 0, halves[:, 0], halves[:, 1])
                give_ref[:, hel, part] = jnp.where(core == 0, halves[:, 1], halves[:, 0]).astype(jnp.bfloat16)
            else:
                out_ref[hel, part] = total
        return carry

    lax.fori_loop(0, n_h, multiply, 0)


def plane_call(plane, dirs, vec, ahead, link, phi, part=None, n_out=0):
    n_h = phi.shape[1]
    _, _, n_b, width = vec.shape
    vmem = pl.BlockSpec(memory_space=pltpu.VMEM)
    args = [vec] + ([ahead] if 0 in dirs else []) + [link, phi]
    args += [part] if part is not None else []
    specs = [vmem] * len(args)
    scratch = [
        pltpu.VMEM((n_h, 2 * n_b, 3 * width), jnp.bfloat16),
        pltpu.VMEM((n_h, 2 * n_b, 3 * width), jnp.bfloat16),
        pltpu.VMEM((len(dirs), 2, 3, ROWS, width), jnp.float32),
    ]
    if n_out:
        blocks = (n_out // 2, n_h, 2, n_b // n_out, n_b)
        out_shape = [
            jax.ShapeDtypeStruct(blocks, jnp.float32),
            jax.ShapeDtypeStruct(blocks, jnp.bfloat16),
        ]
        out_specs = [vmem, vmem]
    else:
        out_shape = jax.ShapeDtypeStruct((n_h, 2, n_b, n_b), jnp.float32)
        out_specs = vmem
    return pl.pallas_call(
        functools.partial(plane_kernel, plane, dirs, part is not None, n_out),
        in_specs=specs,
        out_specs=out_specs,
        out_shape=out_shape,
        scratch_shapes=scratch,
        compiler_params=pltpu.CompilerParams(vmem_limit_bytes=VMEM_BYTES),
        cost_estimate=pl.CostEstimate(
            flops=(16 + 8 * len(dirs)) * n_h * n_b * n_b * 3 * width,
            bytes_accessed=2**22,
            transcendentals=0,
        ),
        name="plane%d_%s" % (plane, "".join(str(direc) for direc in dirs)),
    )(*args)


def merge_kernel(keep_ref, got_ref, own_ref, *out_refs):
    chip = lax.axis_index("space") >> 1
    shape = own_ref.shape
    own_ref[...] = (keep_ref[chip] + got_ref[chip].astype(jnp.float32)).reshape(shape)
    for mask, out_ref in enumerate(out_refs, 1):
        total = keep_ref[chip ^ mask] + got_ref[chip ^ mask].astype(jnp.float32)
        out_ref[...] = total.reshape(shape).astype(jnp.bfloat16)


def merge_call(keep, got):
    chips, n_h, _, own, n_b = keep.shape
    shape = (n_h * 2 * own, n_b)
    vmem = pl.BlockSpec(memory_space=pltpu.VMEM)
    return pl.pallas_call(
        merge_kernel,
        in_specs=[vmem, vmem],
        out_specs=[vmem] * chips,
        out_shape=[jax.ShapeDtypeStruct(shape, jnp.float32)]
        + [jax.ShapeDtypeStruct(shape, jnp.bfloat16)] * (chips - 1),
        compiler_params=pltpu.CompilerParams(vmem_limit_bytes=8 * 2**20),
        name="merge_cores",
    )(keep, got)


def quark_kernel(masks, n_op, n_got, n_h, *refs):
    n_tau = len(masks)
    got_refs = refs[:n_got]
    tau_refs = refs[n_got : n_got + n_tau]
    out_ref, left_ref = refs[n_got + n_tau :]
    my_space, my_op = lax.axis_index("space"), lax.axis_index("op")
    _, n_pair, _, own, n_b = out_ref.shape
    row = lax.broadcasted_iota(jnp.int32, (n_b, 2 * n_b), 0)
    col = lax.broadcasted_iota(jnp.int32, (n_b, 2 * n_b), 1)
    even = (col == 2 * row).astype(jnp.bfloat16)
    odd = (col == 2 * row + 1).astype(jnp.bfloat16)
    total = got_refs[0][...]
    for ref in got_refs[1:]:
        total = total + ref[...].astype(jnp.float32)
    swap = []
    for hel in range(n_h):
        start = hel * 2 * own
        swap += [-total[start + own : start + 2 * own], total[start : start + own]]
    left = jnp.dot(total.astype(jnp.bfloat16), even, preferred_element_type=jnp.float32)
    left += jnp.dot(
        jnp.concatenate(swap, 0).astype(jnp.bfloat16), odd, preferred_element_type=jnp.float32
    )
    left_ref[...] = left.astype(jnp.bfloat16)
    depth = tau_refs[0].shape[0]
    whole = depth == 2 * n_b
    if not whole:
        out_ref[...] = jnp.zeros_like(out_ref)
    for which, (mask, mask_op) in enumerate(masks):
        first = ((my_space ^ mask) * n_op + (my_op ^ mask_op)) * depth
        pair = first // (2 * n_b)
        if whole:
            lhs = left_ref[...]
        else:
            lhs = left_ref[:, pl.ds(pl.multiple_of(first - pair * 2 * n_b, depth), depth)]
        res = jnp.dot(lhs, tau_refs[which][...], preferred_element_type=jnp.float32)
        for hel in range(n_h):
            for part in range(2):
                start = (hel * 2 + part) * own
                if whole:
                    out_ref[hel, pair, part] = res[start : start + own]
                else:
                    out_ref[hel, pair, part] += res[start : start + own]


def phase_kernel(n_op, n_x, planes, *refs):
    mom_refs = refs[:n_op]
    num_refs = refs[n_op : 2 * n_op]
    den_ref, out_ref = refs[2 * n_op :]
    my_space, my_op = lax.axis_index("space"), lax.axis_index("op")
    _, n_h, _, _, _, width = out_ref.shape
    n_mom = mom_refs[0].shape[0]
    moms = [(op, k) for op in range(n_op) for k in range(n_mom)]
    scale = 1.0 / math.sqrt(3.0 * n_x * LY * LZ)
    shape = (planes * len(moms), width)
    row = lax.broadcasted_iota(jnp.int32, shape, 0)
    lane = lax.broadcasted_iota(jnp.int32, shape, 1)
    yy = lane // LZ
    zz = lane & (LZ - 1)

    def spread(values):
        res = jnp.full(shape, values[0], jnp.int32)
        for which in range(1, len(values)):
            res = jnp.where(row == which, values[which], res)
        return res

    comps = [[mom_refs[op][k, axis] for _ in range(planes) for op, k in moms] for axis in range(3)]
    mom_x, mom_y, mom_z = [spread(comp) for comp in comps]
    pos_x = my_space * planes + row // len(moms)
    steps = ((0, 0, 0), (1, 0, 0), (0, 1, 0), (0, 0, 1))
    waves = []
    for step_x, step_y, step_z in steps:
        turn_x = lax.rem(mom_x * (pos_x + step_x), n_x).astype(jnp.float32) * (1.0 / n_x)
        turn_y = ((mom_y * (yy + step_y)) & (LY - 1)).astype(jnp.float32) * (1.0 / LY)
        turn_z = ((mom_z * (zz + step_z)) & (LZ - 1)).astype(jnp.float32) * (1.0 / LZ)
        turn = turn_x + turn_y + turn_z
        theta = (2.0 * math.pi) * (turn - jnp.floor(turn))
        waves.append((jnp.cos(theta), jnp.sin(theta)))
    for hel in range(n_h):
        which_h = my_op * n_h + hel
        den = jnp.full((1, width), den_ref[which_h], jnp.int32).astype(jnp.float32)
        for direc in range(NDIR):
            wts = []
            for op, k in moms:
                num = num_refs[op][direc, k, which_h]
                wts.append(jnp.full((1, width), num, jnp.int32).astype(jnp.float32) / den * scale)
            for kind, wave in ((0, waves[0]), (1, waves[1 + direc])):
                for plane in range(planes):
                    start = plane * len(moms)
                    real = sum(wt * wave[0][start + at : start + at + 1] for at, wt in enumerate(wts))
                    imag = sum(wt * wave[1][start + at : start + at + 1] for at, wt in enumerate(wts))
                    out_ref[kind, hel, direc, 0, plane : plane + 1, :] = -real if kind else real
                    out_ref[kind, hel, direc, 1, plane : plane + 1, :] = -imag


def shards(eigvecs, links, momenta, coef_num, coef_den, peram):
    n_space = lax.axis_size("space")
    n_op = lax.axis_size("op")
    n_tm = lax.axis_size("tm")
    _, _, n_b, _, planes, width = eigvecs.shape
    n_x = planes * n_space
    own = n_b // n_space
    n_h = coef_num.shape[0] // n_op
    my_op = lax.axis_index("op")
    my_space = lax.axis_index("space")

    nums = jnp.transpose(coef_num, (2, 1, 0))
    both = [(momenta, nums)]
    both += [(across(momenta, "op", mask), across(nums, "op", mask)) for mask in range(1, n_op)]

    group = n_space * n_op
    depth = n_b * SPINS // group
    first = (my_space * n_op + my_op) * depth
    piece = lax.dynamic_slice(
        peram.reshape(n_b, SPINS, 2, n_b), (first % n_b, first // n_b, 0, 0), (depth, 1, 2, n_b)
    ).reshape(depth * 2, n_b)
    eigvecs, piece, both = lax.optimization_barrier((eigvecs, piece, both))
    own_piece = from_behind(piece, "tm", n_tm - 1)

    vecs = [jnp.transpose(eigvecs[0, :, :, :, plane, :], (0, 2, 1, 3)) for plane in range(planes)]
    upper = from_behind(vecs[0], "space", -1)

    smem = pl.BlockSpec(memory_space=pltpu.SMEM)
    vmem = pl.BlockSpec(memory_space=pltpu.VMEM)
    phi = pl.pallas_call(
        functools.partial(phase_kernel, n_op, n_x, planes),
        in_specs=[smem] * (2 * n_op + 1),
        out_specs=vmem,
        out_shape=jax.ShapeDtypeStruct((2, n_h, NDIR, 2, planes, width), jnp.float32),
        compiler_params=pltpu.CompilerParams(vmem_limit_bytes=4 * 2**20),
        name="phases",
    )(*[mom for mom, _ in both], *[num for _, num in both], coef_den)

    dims = [("op", 1 << bit) for bit in range(n_op.bit_length() - 1)]
    dims += [("space", 1 << bit) for bit in range(1, n_space.bit_length() - 1)]
    load = [0] * len(dims)

    def stage(held, size):
        for group_dims in itertools.combinations(range(len(dims)), size):
            dim = min(group_dims, key=lambda at: load[at])
            load[dim] += 1
            before = held[tuple(at for at in group_dims if at != dim)]
            held[group_dims] = across(before, *dims[dim])

    def hold(held, other):
        arrs, other = lax.optimization_barrier((list(held.values()), other))
        return dict(zip(held.keys(), arrs)), other

    link = links[0]
    last = planes - 1
    partial = plane_call(last, (1, 2), vecs[last], None, link, phi)
    held, partial = hold({(): own_piece}, partial)
    stage(held, 1)
    for plane in range(last):
        partial = plane_call(plane, (1, 2, 0), vecs[plane], vecs[plane + 1], link, phi, partial)
    held, partial = hold(held, partial)
    ready = dict(held)
    stage(held, 2)
    keep, give = plane_call(last, (0,), vecs[last], upper, link, phi, partial, n_space)
    swapped = across(give, "space", 1)
    held, keep = hold(held, keep)
    for size in range(3, len(dims) + 1):
        stage(held, size)
    merged = merge_call(keep, swapped)
    got = [merged[0]] + [across(arr, "space", 2 * mask) for mask, arr in enumerate(merged[1:], 1)]
    tau, masks = [], []
    for flip in range(2):
        for group_dims, arr in held.items():
            mask = {"space": flip, "op": 0}
            for at in group_dims:
                mask[dims[at][0]] ^= dims[at][1]
            tau.append(across(ready.get(group_dims, arr), "space", 1) if flip else arr)
            masks.append((mask["space"], mask["op"]))

    lines = pl.pallas_call(
        functools.partial(quark_kernel, masks, n_op, len(got), n_h),
        in_specs=[vmem] * (len(got) + len(tau)),
        out_specs=vmem,
        out_shape=jax.ShapeDtypeStruct((n_h, SPINS, 2, own, n_b), jnp.float32),
        scratch_shapes=[
            pltpu.VMEM((n_h * 2 * own, 2 * n_b), jnp.bfloat16),
        ],
        compiler_params=pltpu.CompilerParams(vmem_limit_bytes=VMEM_BYTES),
        cost_estimate=pl.CostEstimate(
            flops=2 * SPINS * n_h * 2 * own * 2 * n_b * n_b, bytes_accessed=7 * 2**20, transcendentals=0
        ),
        name="quark_products",
    )(*got, *tau)
    return lines.reshape(1, n_h, 4, 4, 2, own, n_b)


def solution(mesh):
    return jax.shard_map(
        shards,
        mesh=mesh,
        in_specs=(
            P("tm", None, None, None, "space", None),
            P("tm", None, None, None, None, "space", None),
            P("op", None),
            P(None, "op", None),
            P(),
            P("tm", None, None, None, None, None),
        ),
        out_specs=P("tm", "op", None, None, None, "space", None),
        check_vma=False,
    )
```

profile of v0, /device:TPU:0, one launch (start us, length us, event | category | flops | bytes accessed | tf_op | source)
XLA Modules:
  0.0 60.1 jit_solution(3196848626632174272)
XLA Ops:
  0.0 3.0 %collective-permute-start = (s32[2,3]{1,0:T(2,128)}, s32[2,3]{1,0:T(2,128)S(1)}, u32[]{:S(2)}, u32[]{:S(2)}) collective-permute-start(s32[2,3]{1,0:T(2,128)} %refs_0_), channel_id=1, source_target_pairs={{0,1},{1,0},{2,3},{3,2},{4,5},{5,4},{6,7},{7,6},{8,9},{9,8},{10,11... | collective-permute-start | bytes 80 | tf_op jit(solution)/shard_map/ppermute | solution.py:29
  3.1 1.1 %dynamic-slice_bitcast_fusion = bf16[256,1,2,256]{3,2,0,1:T(2,128)(2,1)S(1)} fusion(bf16[256,16,2,256]{3,2,1,0:T(2,128)(2,1)} %bitcast.21, s32[]{:T(128)S(6)} %select_n.14), kind=kLoop, calls=%fused_computation.2 | loop fusion | bytes 524292
  4.3 0.5 collective-permute-done.refs_1_
  4.8 2.1 %collective-permute-done.1.refs_3_ = s32[3,2,4]{2,1,0:T(2,128)S(1)} collective-permute-done((s32[3,2,4]{2,1,0:T(2,128)}, s32[3,2,4]{2,1,0:T(2,128)S(1)}, u32[]{:S(2)}, u32[]{:S(2)}) %collective-permute-start.1) | collective-permute-done | bytes 128 | tf_op jit(solution)/shard_map/ppermute | solution.py:29
  6.8 2.6 %collective-permute-start.2 = (bf16[512,256]{1,0:T(8,128)(2,1)S(1)}, bf16[512,256]{1,0:T(8,128)(2,1)S(1)}, u32[]{:S(2)}, u32[]{:S(2)}) collective-permute-start(bf16[512,256]{1,0:T(8,128)(2,1)S(1)} %reshape.10), channel_id=1, source_target_pairs={{0,2},{2,0},{1,3},{3,1},{4,6},{6,4},{5,7},{7,5},{8,10},{10,8},{9,1... | collective-permute-start | bytes 786440 | tf_op jit(solution)/shard_map/ppermute | solution.py:24
  9.4 1.6 %copy.8 = bf16[1,2,256,3,2,256]{5,2,3,1,4,0:T(8,128)(2,1)S(1)} copy(bf16[1,2,256,3,2,256]{5,4,3,2,1,0:T(2,128)(2,1)} %param.6) | data formatting | bytes 3145728 | tf_op jit(solution)/shard_map/optimization_barrier | solution.py:318
  11.3 0.3 collective-permute-start.9
  11.6 0.2 copy-done
  11.8 0.9 %phases.1.refs_2_.refs_3_ = f32[2,2,3,2,2,256]{5,4,3,2,1,0:T(2,128)S(1)} custom-call(s32[2,3]{1,0:T(2,128)S(1)} %copy-done.1, s32[2,3]{1,0:T(2,128)S(1)} %collective-permute-done.refs_1_, s32[3,2,4]{2,1,0:T(2,128)S(1)} %bitcast.17, s32[3,2,4]{2,1,0:T(2,128)S(1)} %collective-permute-done.1.refs_3_, s32[4]{0:T(128)S(1)} %copy-done.2), custom_call_target="tpu_custom_call" | custom-call | tf_op jit(solution)/shard_map/phases/pallas_call | solution.py:326
  12.7 6.7 %plane1_12.1.refs_4_ = f32[2,2,256,256]{3,2,1,0:T(8,128)S(1)} custom-call(bf16[2,3,256,256]{3,2,1,0:T(8,128)(2,1)S(1)} %get-tuple-element.60.refs_0_.refs_1_, f32[3,3,3,2,2,256]{5,4,3,2,1,0:T(2,128)S(1)} %bitcast.18, f32[2,2,3,2,2,256]{5,4,3,2,1,0:T(2,128)S(1)} %phases.1.refs_2_.refs_3_), custom_call_target="tpu_custom_call" | custom-call | flops 3221225472 | bytes 4194304 | tf_op jit(solution)/shard_map/plane1_12/pallas_call | solution.py:163
  19.5 0.3 collective-permute-done.2.refs_4_
  19.8 1.6 %collective-permute-start.5 = (bf16[512,256]{1,0:T(8,128)(2,1)S(1)}, bf16[512,256]{1,0:T(8,128)(2,1)S(1)}, u32[]{:S(2)}, u32[]{:S(2)}) collective-permute-start(bf16[512,256]{1,0:T(8,128)(2,1)S(1)} %collective-permute-done.2.refs_4_), channel_id=1, source_target_pairs={{0,16},{4,20},{8,24},{12,28},{16,0},{20,4},{24,8},{28,12},{1,17},{... | collective-permute-start | bytes 786440 | tf_op jit(solution)/shard_map/ppermute | solution.py:29
  21.4 1.5 %collective-permute-start.4 = (bf16[512,256]{1,0:T(8,128)(2,1)S(1)}, bf16[512,256]{1,0:T(8,128)(2,1)S(1)}, u32[]{:S(2)}, u32[]{:S(2)}) collective-permute-start(bf16[512,256]{1,0:T(8,128)(2,1)S(1)} %collective-permute-done.2.refs_4_), channel_id=1, source_target_pairs={{0,8},{4,12},{8,0},{12,4},{16,24},{20,28},{24,16},{28,20},{1,9},{5... | collective-permute-start | bytes 786440 | tf_op jit(solution)/shard_map/ppermute | solution.py:29
  23.0 8.3 %plane0_120.1.refs_4_ = f32[2,2,256,256]{3,2,1,0:T(8,128)S(1)} custom-call(bf16[2,3,256,256]{3,2,1,0:T(8,128)(2,1)S(1)} %get-tuple-element.59.refs_0_, bf16[2,3,256,256]{3,2,1,0:T(8,128)(2,1)S(1)} %get-tuple-element.60.refs_0_.refs_1_, f32[3,3,3,2,2,256]{5,4,3,2,1,0:T(2,128)S(1)} %bitcast.19, f32[2,2,3,2,2,256]{5,4,3,2,1,0:T(2,128)S(1)} %phases.1.refs_2_.refs_3_, ...), custom_call_target="tpu_custom_call" | custom-call | flops 4026531840 | bytes 4194304 | tf_op jit(solution)/shard_map/plane0_120/pallas_call | solution.py:163
  31.3 0.6 collective-permute-start.7
  31.9 1.9 %collective-permute-start.6 = (bf16[512,256]{1,0:T(8,128)(2,1)S(1)}, bf16[512,256]{1,0:T(8,128)(2,1)S(1)}, u32[]{:S(2)}, u32[]{:S(2)}) collective-permute-start(bf16[512,256]{1,0:T(8,128)(2,1)S(1)} %collective-permute-done.4.refs_6_), channel_id=1, source_target_pairs={{0,1},{1,0},{2,3},{3,2},{4,5},{5,4},{6,7},{7,6},{8,9},{9,8},{10,11... | collective-permute-start | bytes 786440 | tf_op jit(solution)/shard_map/ppermute | solution.py:29
  33.8 0.5 collective-permute-start.8
  34.3 0.5 collective-permute-start.17
  34.8 4.1 %collective-permute-done.7.refs_9_ = bf16[512,256]{1,0:T(8,128)(2,1)S(1)} collective-permute-done((bf16[512,256]{1,0:T(8,128)(2,1)S(1)}, bf16[512,256]{1,0:T(8,128)(2,1)S(1)}, u32[]{:S(2)}, u32[]{:S(2)}) %collective-permute-start.7) | collective-permute-done | bytes 262176 | tf_op jit(solution)/shard_map/ppermute | solution.py:29
  38.9 3.7 %plane1_0.1 = (f32[4,2,2,32,256]{4,3,2,1,0:T(8,128)S(1)}, bf16[4,2,2,32,256]{4,3,2,1,0:T(8,128)(2,1)S(1)}) custom-call(bf16[2,3,256,256]{3,2,1,0:T(8,128)(2,1)S(1)} %get-tuple-element.60.refs_0_.refs_1_, bf16[2,3,256,256]{3,2,1,0:T(8,128)(2,1)S(1)} %collective-permute-done.9.refs_1_, f32[3,3,3,2,2,256]{5,4,3,2,1,0:T(2,128)S(1)} %bitcast.20, ...), custom_call_target="tpu_custom_call" | custom-call | flops 2415919104 | bytes 4194304 | tf_op jit(solution)/shard_map/plane1_0/pallas_call | solution.py:163
  42.6 0.6 collective-permute-start.10
  43.2 1.7 %collective-permute-start.14 = (bf16[512,256]{1,0:T(8,128)(2,1)S(1)}, bf16[512,256]{1,0:T(8,128)(2,1)S(1)}, u32[]{:S(2)}, u32[]{:S(2)}) collective-permute-start(bf16[512,256]{1,0:T(8,128)(2,1)S(1)} %collective-permute-done.8.refs_10_), channel_id=1, source_target_pairs={{0,1},{1,0},{2,3},{3,2},{4,5},{5,4},{6,7},{7,6},{8,9},{9,8},{10,11... | collective-permute-start | bytes 786440 | tf_op jit(solution)/shard_map/ppermute | solution.py:29
  44.9 0.5 collective-permute-start.19
  45.5 0.4 collective-permute-start.21
  46.0 5.5 %collective-permute-done.14.refs_11_ = bf16[512,256]{1,0:T(8,128)(2,1)S(1)} collective-permute-done((bf16[512,256]{1,0:T(8,128)(2,1)S(1)}, bf16[512,256]{1,0:T(8,128)(2,1)S(1)}, u32[]{:S(2)}, u32[]{:S(2)}) %collective-permute-start.14) | collective-permute-done | bytes 262176 | tf_op jit(solution)/shard_map/ppermute | solution.py:29
  51.6 0.6 %collective-permute-start.11 = (bf16[128,256]{1,0:T(8,128)(2,1)S(1)}, bf16[128,256]{1,0:T(8,128)(2,1)S(1)}, u32[]{:S(2)}, u32[]{:S(2)}) collective-permute-start(bf16[128,256]{1,0:T(8,128)(2,1)S(1)} %get-tuple-element.49), channel_id=1, source_target_pairs={{0,8},{4,12},{8,0},{12,4},{16,24},{20,28},{24,16},{28,20},{1,9},{5... | collective-permute-start | bytes 196616 | tf_op jit(solution)/shard_map/ppermute | solution.py:29
  52.2 0.5 collective-permute-start.12
  52.7 2.5 %collective-permute-start.13 = (bf16[128,256]{1,0:T(8,128)(2,1)S(1)}, bf16[128,256]{1,0:T(8,128)(2,1)S(1)}, u32[]{:S(2)}, u32[]{:S(2)}) collective-permute-start(bf16[128,256]{1,0:T(8,128)(2,1)S(1)} %get-tuple-element.51), channel_id=1, source_target_pairs={{0,24},{4,28},{8,16},{12,20},{16,8},{20,12},{24,0},{28,4},{1,25},{... | collective-permute-start | bytes 196616 | tf_op jit(solution)/shard_map/ppermute | solution.py:29
  55.1 1.0 %collective-permute-done.11.refs_1_ = bf16[128,256]{1,0:T(8,128)(2,1)S(1)} collective-permute-done((bf16[128,256]{1,0:T(8,128)(2,1)S(1)}, bf16[128,256]{1,0:T(8,128)(2,1)S(1)}, u32[]{:S(2)}, u32[]{:S(2)}) %collective-permute-start.11) | collective-permute-done | bytes 65568 | tf_op jit(solution)/shard_map/ppermute | solution.py:29
  56.1 1.1 %collective-permute-done.12.refs_2_ = bf16[128,256]{1,0:T(8,128)(2,1)S(1)} collective-permute-done((bf16[128,256]{1,0:T(8,128)(2,1)S(1)}, bf16[128,256]{1,0:T(8,128)(2,1)S(1)}, u32[]{:S(2)}, u32[]{:S(2)}) %collective-permute-start.12) | collective-permute-done | bytes 65568 | tf_op jit(solution)/shard_map/ppermute | solution.py:29
  57.2 0.7 %collective-permute-done.13.refs_3_ = bf16[128,256]{1,0:T(8,128)(2,1)S(1)} collective-permute-done((bf16[128,256]{1,0:T(8,128)(2,1)S(1)}, bf16[128,256]{1,0:T(8,128)(2,1)S(1)}, u32[]{:S(2)}, u32[]{:S(2)}) %collective-permute-start.13) | collective-permute-done | bytes 65568 | tf_op jit(solution)/shard_map/ppermute | solution.py:29
  57.8 2.3 %quark_products.1 = f32[2,16,2,32,256]{4,3,2,1,0:T(8,128)} custom-call(f32[128,256]{1,0:T(8,128)S(1)} %get-tuple-element.48.refs_0_, bf16[128,256]{1,0:T(8,128)(2,1)S(1)} %collective-permute-done.11.refs_1_, bf16[128,256]{1,0:T(8,128)(2,1)S(1)} %collective-permute-done.12.refs_2_, bf16[128,256]{1,0:T(8,128)(2,1)S(1)} %collective-permute-done.13.refs_3_, ...), custom_call_target="tpu_custom_call" | custom-call | flops 536870912 | bytes 7340032 | tf_op jit(solution)/shard_map/quark_products/pallas_call | solution.py:376
  (32 shorter events, 0.6 us)
Async XLA Ops:
  0.0 4.8 %collective-permute-start = (s32[2,3]{1,0:T(2,128)}, s32[2,3]{1,0:T(2,128)S(1)}, u32[]{:S(2)}, u32[]{:S(2)}) collective-permute-start(s32[2,3]{1,0:T(2,128)} %refs_0_), channel_id=1, source_target_pairs={{0,1},{1,0},{2,3},{3,2},{4,5},{5,4},{6,7},{7,6},{8,9},{9,8},{10,11... | collective-permute-start | bytes 80 | tf_op jit(solution)/shard_map/ppermute | solution.py:29
  3.0 3.8 %collective-permute-start.1 = (s32[3,2,4]{2,1,0:T(2,128)}, s32[3,2,4]{2,1,0:T(2,128)S(1)}, u32[]{:S(2)}, u32[]{:S(2)}) collective-permute-start(s32[3,2,4]{2,1,0:T(2,128)} %bitcast.16), channel_id=1, source_target_pairs={{0,1},{1,0},{2,3},{3,2},{4,5},{5,4},{6,7},{7,6},{8,9},{9,8},{10,11... | collective-permute-start | bytes 296 | tf_op jit(solution)/shard_map/ppermute | solution.py:29
  6.8 13.0 %collective-permute-start.2 = (bf16[512,256]{1,0:T(8,128)(2,1)S(1)}, bf16[512,256]{1,0:T(8,128)(2,1)S(1)}, u32[]{:S(2)}, u32[]{:S(2)}) collective-permute-start(bf16[512,256]{1,0:T(8,128)(2,1)S(1)} %reshape.10), channel_id=1, source_target_pairs={{0,2},{2,0},{1,3},{3,1},{4,6},{6,4},{5,7},{7,5},{8,10},{10,8},{9,1... | collective-permute-start | bytes 786440 | tf_op jit(solution)/shard_map/ppermute | solution.py:24
  11.1 0.7 %copy-start = (s32[4,2,3]{0,1,2:T(2,128)S(1)}, s32[4,2,3]{0,1,2:T(2,128)}, u32[]{:S(2)}) copy-start(s32[4,2,3]{0,1,2:T(2,128)} %param.9) | copy-start | bytes 292
  11.1 0.7 %copy-start.1 = (s32[2,3]{1,0:T(2,128)S(1)}, s32[2,3]{1,0:T(2,128)}, u32[]{:S(2)}) copy-start(s32[2,3]{1,0:T(2,128)} %refs_0_) | copy-start | bytes 76
  11.1 0.7 %copy-start.2 = (s32[4]{0:T(128)S(1)}, s32[4]{0:T(128)}, u32[]{:S(2)}) copy-start(s32[4]{0:T(128)} %refs_4_.1) | copy-start | bytes 52
  11.1 1.6 %copy-start.3 = (f32[1,3,3,3,2,2,256]{6,5,4,3,2,1,0:T(2,128)S(1)}, f32[1,3,3,3,2,2,256]{6,5,4,3,2,1,0:T(2,128)}, u32[]{:S(2)}) copy-start(f32[1,3,3,3,2,2,256]{6,5,4,3,2,1,0:T(2,128)} %param.7) | copy-start | bytes 331780
  11.3 23.0 %collective-permute-start.9 = (bf16[2,3,256,256]{3,2,1,0:T(8,128)(2,1)S(1)}, bf16[2,3,256,256]{3,2,1,0:T(8,128)(2,1)S(1)}, u32[]{:S(2)}, u32[]{:S(2)}) collective-permute-start(bf16[2,3,256,256]{3,2,1,0:T(8,128)(2,1)S(1)} %get-tuple-element.59.refs_0_), channel_id=1, source_target_pairs={{0,28},{4,0},{8,4},{12,8},{16,12},{20,16},{24,20},{28,24},{1,29},{... | collective-permute-start | bytes 2359304 | tf_op jit(solution)/shard_map/ppermute | solution.py:24
  19.8 11.5 %collective-permute-start.5 = (bf16[512,256]{1,0:T(8,128)(2,1)S(1)}, bf16[512,256]{1,0:T(8,128)(2,1)S(1)}, u32[]{:S(2)}, u32[]{:S(2)}) collective-permute-start(bf16[512,256]{1,0:T(8,128)(2,1)S(1)} %collective-permute-done.2.refs_4_), channel_id=1, source_target_pairs={{0,16},{4,20},{8,24},{12,28},{16,0},{20,4},{24,8},{28,12},{1,17},{... | collective-permute-start | bytes 786440 | tf_op jit(solution)/shard_map/ppermute | solution.py:29
  21.4 9.9 %collective-permute-start.4 = (bf16[512,256]{1,0:T(8,128)(2,1)S(1)}, bf16[512,256]{1,0:T(8,128)(2,1)S(1)}, u32[]{:S(2)}, u32[]{:S(2)}) collective-permute-start(bf16[512,256]{1,0:T(8,128)(2,1)S(1)} %collective-permute-done.2.refs_4_), channel_id=1, source_target_pairs={{0,8},{4,12},{8,0},{12,4},{16,24},{20,28},{24,16},{28,20},{1,9},{5... | collective-permute-start | bytes 786440 | tf_op jit(solution)/shard_map/ppermute | solution.py:29
  22.9 8.4 %collective-permute-start.3 = (bf16[512,256]{1,0:T(8,128)(2,1)S(1)}, bf16[512,256]{1,0:T(8,128)(2,1)S(1)}, u32[]{:S(2)}, u32[]{:S(2)}) collective-permute-start(bf16[512,256]{1,0:T(8,128)(2,1)S(1)} %collective-permute-done.2.refs_4_), channel_id=1, source_target_pairs={{0,1},{1,0},{2,3},{3,2},{4,5},{5,4},{6,7},{7,6},{8,9},{9,8},{10,11... | collective-permute-start | bytes 786440 | tf_op jit(solution)/shard_map/ppermute | solution.py:29
  31.3 7.6 %collective-permute-start.7 = (bf16[512,256]{1,0:T(8,128)(2,1)S(1)}, bf16[512,256]{1,0:T(8,128)(2,1)S(1)}, u32[]{:S(2)}, u32[]{:S(2)}) collective-permute-start(bf16[512,256]{1,0:T(8,128)(2,1)S(1)} %collective-permute-done.3.refs_5_), channel_id=1, source_target_pairs={{0,16},{4,20},{8,24},{12,28},{16,0},{20,4},{24,8},{28,12},{1,17},{... | collective-permute-start | bytes 786440 | tf_op jit(solution)/shard_map/ppermute | solution.py:29
  31.9 10.7 %collective-permute-start.6 = (bf16[512,256]{1,0:T(8,128)(2,1)S(1)}, bf16[512,256]{1,0:T(8,128)(2,1)S(1)}, u32[]{:S(2)}, u32[]{:S(2)}) collective-permute-start(bf16[512,256]{1,0:T(8,128)(2,1)S(1)} %collective-permute-done.4.refs_6_), channel_id=1, source_target_pairs={{0,1},{1,0},{2,3},{3,2},{4,5},{5,4},{6,7},{7,6},{8,9},{9,8},{10,11... | collective-permute-start | bytes 786440 | tf_op jit(solution)/shard_map/ppermute | solution.py:29
  33.8 9.4 %collective-permute-start.8 = (bf16[512,256]{1,0:T(8,128)(2,1)S(1)}, bf16[512,256]{1,0:T(8,128)(2,1)S(1)}, u32[]{:S(2)}, u32[]{:S(2)}) collective-permute-start(bf16[512,256]{1,0:T(8,128)(2,1)S(1)} %collective-permute-done.5.refs_7_), channel_id=1, source_target_pairs={{0,8},{4,12},{8,0},{12,4},{16,24},{20,28},{24,16},{28,20},{1,9},{5... | collective-permute-start | bytes 786440 | tf_op jit(solution)/shard_map/ppermute | solution.py:29
  34.3 10.7 %collective-permute-start.16 = (bf16[512,256]{1,0:T(8,128)(2,1)S(1)}, bf16[512,256]{1,0:T(8,128)(2,1)S(1)}, u32[]{:S(2)}, u32[]{:S(2)}) collective-permute-start(bf16[512,256]{1,0:T(8,128)(2,1)S(1)} %collective-permute-done.3.refs_5_), channel_id=1, source_target_pairs={{0,4},{4,0},{8,12},{12,8},{16,20},{20,16},{24,28},{28,24},{1,5},{5... | collective-permute-start | bytes 786440 | tf_op jit(solution)/shard_map/ppermute | solution.py:29
  34.3 11.2 %collective-permute-start.17 = (bf16[512,256]{1,0:T(8,128)(2,1)S(1)}, bf16[512,256]{1,0:T(8,128)(2,1)S(1)}, u32[]{:S(2)}, u32[]{:S(2)}) collective-permute-start(bf16[512,256]{1,0:T(8,128)(2,1)S(1)} %collective-permute-done.4.refs_6_), channel_id=1, source_target_pairs={{0,4},{4,0},{8,12},{12,8},{16,20},{20,16},{24,28},{28,24},{1,5},{5... | collective-permute-start | bytes 786440 | tf_op jit(solution)/shard_map/ppermute | solution.py:29
  38.9 6.0 %collective-permute-start.15 = (bf16[512,256]{1,0:T(8,128)(2,1)S(1)}, bf16[512,256]{1,0:T(8,128)(2,1)S(1)}, u32[]{:S(2)}, u32[]{:S(2)}) collective-permute-start(bf16[512,256]{1,0:T(8,128)(2,1)S(1)} %collective-permute-done.2.refs_4_), channel_id=1, source_target_pairs={{0,4},{4,0},{8,12},{12,8},{16,20},{20,16},{24,28},{28,24},{1,5},{5... | collective-permute-start | bytes 786440 | tf_op jit(solution)/shard_map/ppermute | solution.py:29
  42.6 2.9 %collective-permute-start.10 = (bf16[4,2,2,32,256]{4,3,2,1,0:T(8,128)(2,1)S(1)}, bf16[4,2,2,32,256]{4,3,2,1,0:T(8,128)(2,1)S(1)}, u32[]{:S(2)}, u32[]{:S(2)}) collective-permute-start(bf16[4,2,2,32,256]{4,3,2,1,0:T(8,128)(2,1)S(1)} %get-tuple-element.47), channel_id=1, source_target_pairs={{0,4},{4,0},{8,12},{12,8},{16,20},{20,16},{24,28},{28,24},{1,5},{5... | collective-permute-start | bytes 786440 | tf_op jit(solution)/shard_map/ppermute | solution.py:29
  43.2 8.3 %collective-permute-start.14 = (bf16[512,256]{1,0:T(8,128)(2,1)S(1)}, bf16[512,256]{1,0:T(8,128)(2,1)S(1)}, u32[]{:S(2)}, u32[]{:S(2)}) collective-permute-start(bf16[512,256]{1,0:T(8,128)(2,1)S(1)} %collective-permute-done.8.refs_10_), channel_id=1, source_target_pairs={{0,1},{1,0},{2,3},{3,2},{4,5},{5,4},{6,7},{7,6},{8,9},{9,8},{10,11... | collective-permute-start | bytes 786440 | tf_op jit(solution)/shard_map/ppermute | solution.py:29
  44.9 6.6 %collective-permute-start.18 = (bf16[512,256]{1,0:T(8,128)(2,1)S(1)}, bf16[512,256]{1,0:T(8,128)(2,1)S(1)}, u32[]{:S(2)}, u32[]{:S(2)}) collective-permute-start(bf16[512,256]{1,0:T(8,128)(2,1)S(1)} %collective-permute-done.5.refs_7_), channel_id=1, source_target_pairs={{0,4},{4,0},{8,12},{12,8},{16,20},{20,16},{24,28},{28,24},{1,5},{5... | collective-permute-start | bytes 786440 | tf_op jit(solution)/shard_map/ppermute | solution.py:29
  44.9 7.2 %collective-permute-start.19 = (bf16[512,256]{1,0:T(8,128)(2,1)S(1)}, bf16[512,256]{1,0:T(8,128)(2,1)S(1)}, u32[]{:S(2)}, u32[]{:S(2)}) collective-permute-start(bf16[512,256]{1,0:T(8,128)(2,1)S(1)} %collective-permute-done.6.refs_8_), channel_id=1, source_target_pairs={{0,4},{4,0},{8,12},{12,8},{16,20},{20,16},{24,28},{28,24},{1,5},{5... | collective-permute-start | bytes 786440 | tf_op jit(solution)/shard_map/ppermute | solution.py:29
  45.4 7.2 %collective-permute-start.20 = (bf16[512,256]{1,0:T(8,128)(2,1)S(1)}, bf16[512,256]{1,0:T(8,128)(2,1)S(1)}, u32[]{:S(2)}, u32[]{:S(2)}) collective-permute-start(bf16[512,256]{1,0:T(8,128)(2,1)S(1)} %collective-permute-done.7.refs_9_), channel_id=1, source_target_pairs={{0,4},{4,0},{8,12},{12,8},{16,20},{20,16},{24,28},{28,24},{1,5},{5... | collective-permute-start | bytes 786440 | tf_op jit(solution)/shard_map/ppermute | solution.py:29
  45.5 9.6 %collective-permute-start.21 = (bf16[512,256]{1,0:T(8,128)(2,1)S(1)}, bf16[512,256]{1,0:T(8,128)(2,1)S(1)}, u32[]{:S(2)}, u32[]{:S(2)}) collective-permute-start(bf16[512,256]{1,0:T(8,128)(2,1)S(1)} %collective-permute-done.8.refs_10_), channel_id=1, source_target_pairs={{0,4},{4,0},{8,12},{12,8},{16,20},{20,16},{24,28},{28,24},{1,5},{5... | collective-permute-start | bytes 786440 | tf_op jit(solution)/shard_map/ppermute | solution.py:29
  51.5 6.4 %collective-permute-start.22 = (bf16[512,256]{1,0:T(8,128)(2,1)S(1)}, bf16[512,256]{1,0:T(8,128)(2,1)S(1)}, u32[]{:S(2)}, u32[]{:S(2)}) collective-permute-start(bf16[512,256]{1,0:T(8,128)(2,1)S(1)} %collective-permute-done.14.refs_11_), channel_id=1, source_target_pairs={{0,4},{4,0},{8,12},{12,8},{16,20},{20,16},{24,28},{28,24},{1,5},{5... | collective-permute-start | bytes 786440 | tf_op jit(solution)/shard_map/ppermute | solution.py:29
  51.6 4.6 %collective-permute-start.11 = (bf16[128,256]{1,0:T(8,128)(2,1)S(1)}, bf16[128,256]{1,0:T(8,128)(2,1)S(1)}, u32[]{:S(2)}, u32[]{:S(2)}) collective-permute-start(bf16[128,256]{1,0:T(8,128)(2,1)S(1)} %get-tuple-element.49), channel_id=1, source_target_pairs={{0,8},{4,12},{8,0},{12,4},{16,24},{20,28},{24,16},{28,20},{1,9},{5... | collective-permute-start | bytes 196616 | tf_op jit(solution)/shard_map/ppermute | solution.py:29
  52.2 5.0 %collective-permute-start.12 = (bf16[128,256]{1,0:T(8,128)(2,1)S(1)}, bf16[128,256]{1,0:T(8,128)(2,1)S(1)}, u32[]{:S(2)}, u32[]{:S(2)}) collective-permute-start(bf16[128,256]{1,0:T(8,128)(2,1)S(1)} %get-tuple-element.50), channel_id=1, source_target_pairs={{0,16},{4,20},{8,24},{12,28},{16,0},{20,4},{24,8},{28,12},{1,17},{... | collective-permute-start | bytes 196616 | tf_op jit(solution)/shard_map/ppermute | solution.py:29
  52.7 5.2 %collective-permute-start.13 = (bf16[128,256]{1,0:T(8,128)(2,1)S(1)}, bf16[128,256]{1,0:T(8,128)(2,1)S(1)}, u32[]{:S(2)}, u32[]{:S(2)}) collective-permute-start(bf16[128,256]{1,0:T(8,128)(2,1)S(1)} %get-tuple-element.51), channel_id=1, source_target_pairs={{0,24},{4,28},{8,16},{12,20},{16,8},{20,12},{24,0},{28,4},{1,25},{... | collective-permute-start | bytes 196616 | tf_op jit(solution)/shard_map/ppermute | solution.py:29
where the time goes:
time: 60.3 us; the launch traced here: 60.1 us
  Pallas kernels  21.9 us (36%)
  starting transfers between devices  19.5 us (32%)
  waiting for transfers between devices  15.2 us (25%)
  local copies, waits for them, and re-layouts  3.23 us (5%)
    pallas_call x3, Pallas kernels, plane_call(): pl.pallas_call(functools.partial(plane_kernel, plane, dirs, part is not N...  18.7 us
    ppermute x21, starting transfers between devices, across(): return lax.ppermute(value, axis, pairs)  16.6 us
    ppermute x21, waiting for transfers between devices, across(): return lax.ppermute(value, axis, pairs)  14.9 us
    ppermute x2, starting transfers between devices, from_behind(): return lax.ppermute(value, axis, pairs)  2.92 us
    pallas_call x1, Pallas kernels, shards(): pl.pallas_call(functools.partial(quark_kernel, masks, n_op, len(got), n_h...  2.26 us
    optimization_barrier x1, local copies, waits for them, and re-layouts, shards(): eigvecs, piece, both = lax.optimization_barrier((eigvecs, piece, both))  1.64 us
    unnamed x9, local copies, waits for them, and re-layouts  1.38 us
  transfers between devices with their start and end apart: 23, of which 8 were waited for; matrix products, arithmetic and copies ran while one was open for 5% of the time, Pallas kernels for 33%

commit v1 on v0

--- a/solution.py
+++ b/solution.py
@@ -176,32 +176,40 @@
     )(*args)
 
 
-def merge_kernel(keep_ref, got_ref, own_ref, *out_refs):
+def merge_kernel(n_early, keep_ref, got_ref, *refs):
+    early_refs = refs[:n_early]
+    pack_ref, own_ref = refs[n_early : n_early + 2]
     chip = lax.axis_index("space") >> 1
     shape = own_ref.shape
     own_ref[...] = (keep_ref[chip] + got_ref[chip].astype(jnp.float32)).reshape(shape)
-    for mask, out_ref in enumerate(out_refs, 1):
+    for mask, out_ref in enumerate(refs[n_early + 2 :], 1):
         total = keep_ref[chip ^ mask] + got_ref[chip ^ mask].astype(jnp.float32)
         out_ref[...] = total.reshape(shape).astype(jnp.bfloat16)
-
-
-def merge_call(keep, got):
+    for which, ref in enumerate(early_refs):
+        pack_ref[which] = ref[...]
+
+
+def merge_call(keep, got, early):
     chips, n_h, _, own, n_b = keep.shape
     shape = (n_h * 2 * own, n_b)
     vmem = pl.BlockSpec(memory_space=pltpu.VMEM)
-    return pl.pallas_call(
-        merge_kernel,
-        in_specs=[vmem, vmem],
-        out_specs=[vmem] * chips,
-        out_shape=[jax.ShapeDtypeStruct(shape, jnp.float32)]
+    out = pl.pallas_call(
+        functools.partial(merge_kernel, len(early)),
+        in_specs=[vmem] * (2 + len(early)),
+        out_specs=[vmem] * (1 + chips),
+        out_shape=[
+            jax.ShapeDtypeStruct((len(early),) + early[0].shape, jnp.bfloat16),
+            jax.ShapeDtypeStruct(shape, jnp.float32),
+        ]
         + [jax.ShapeDtypeStruct(shape, jnp.bfloat16)] * (chips - 1),
         compiler_params=pltpu.CompilerParams(vmem_limit_bytes=8 * 2**20),
+        cost_estimate=pl.CostEstimate(flops=2**16, bytes_accessed=2**12, transcendentals=0),
         name="merge_cores",
-    )(keep, got)
-
-
-def quark_kernel(masks, n_op, n_got, n_h, *refs):
-    n_tau = len(masks)
+    )(keep, got, *early)
+    return out[0], out[1:]
+
+
+def quark_kernel(masks, n_op, n_got, n_tau, n_h, *refs):
     got_refs = refs[:n_got]
     tau_refs = refs[n_got : n_got + n_tau]
     out_ref, left_ref = refs[n_got + n_tau :]
@@ -223,7 +231,10 @@
         jnp.concatenate(swap, 0).astype(jnp.bfloat16), odd, preferred_element_type=jnp.float32
     )
     left_ref[...] = left.astype(jnp.bfloat16)
-    depth = tau_refs[0].shape[0]
+    tau = []
+    for ref in tau_refs:
+        tau += [ref.at[which] for which in range(ref.shape[0])] if len(ref.shape) == 3 else [ref]
+    depth = tau[0].shape[0]
     whole = depth == 2 * n_b
     if not whole:
         out_ref[...] = jnp.zeros_like(out_ref)
@@ -234,7 +245,7 @@
             lhs = left_ref[...]
         else:
             lhs = left_ref[:, pl.ds(pl.multiple_of(first - pair * 2 * n_b, depth), depth)]
-        res = jnp.dot(lhs, tau_refs[which][...], preferred_element_type=jnp.float32)
+        res = jnp.dot(lhs, tau[which][...], preferred_element_type=jnp.float32)
         for hel in range(n_h):
             for part in range(2):
                 start = (hel * 2 + part) * own
@@ -315,10 +326,11 @@
     piece = lax.dynamic_slice(
         peram.reshape(n_b, SPINS, 2, n_b), (first % n_b, first // n_b, 0, 0), (depth, 1, 2, n_b)
     ).reshape(depth * 2, n_b)
-    eigvecs, piece, both = lax.optimization_barrier((eigvecs, piece, both))
+
+    moved = lax.optimization_barrier(jnp.transpose(eigvecs[0], (3, 0, 2, 1, 4)))
+    moved, piece, both = lax.optimization_barrier((moved, piece, both))
     own_piece = from_behind(piece, "tm", n_tm - 1)
-
-    vecs = [jnp.transpose(eigvecs[0, :, :, :, plane, :], (0, 2, 1, 3)) for plane in range(planes)]
+    vecs = [moved[plane] for plane in range(planes)]
     upper = from_behind(vecs[0], "space", -1)
 
     smem = pl.BlockSpec(memory_space=pltpu.SMEM)
@@ -355,26 +367,30 @@
     for plane in range(last):
         partial = plane_call(plane, (1, 2, 0), vecs[plane], vecs[plane + 1], link, phi, partial)
     held, partial = hold(held, partial)
-    ready = dict(held)
     stage(held, 2)
     keep, give = plane_call(last, (0,), vecs[last], upper, link, phi, partial, n_space)
     swapped = across(give, "space", 1)
     held, keep = hold(held, keep)
     for size in range(3, len(dims) + 1):
         stage(held, size)
-    merged = merge_call(keep, swapped)
+    early = [key for key in held if len(key) < 3]
+    late = [key for key in held if len(key) >= 3]
+    packed, merged = merge_call(keep, swapped, [held[key] for key in early])
     got = [merged[0]] + [across(arr, "space", 2 * mask) for mask, arr in enumerate(merged[1:], 1)]
-    tau, masks = [], []
+    last_held, got = hold({key: held[key] for key in late}, got)
+    held.update(last_held)
+    tau = [held[key] for key in early + late]
+    tau += [across(packed, "space", 1)] + [across(held[key], "space", 1) for key in late]
+    masks = []
     for flip in range(2):
-        for group_dims, arr in held.items():
+        for group_dims in early + late:
             mask = {"space": flip, "op": 0}
             for at in group_dims:
                 mask[dims[at][0]] ^= dims[at][1]
-            tau.append(across(ready.get(group_dims, arr), "space", 1) if flip else arr)
             masks.append((mask["space"], mask["op"]))
 
     lines = pl.pallas_call(
-        functools.partial(quark_kernel, masks, n_op, len(got), n_h),
+        functools.partial(quark_kernel, masks, n_op, len(got), len(tau), n_h),
         in_specs=[vmem] * (len(got) + len(tau)),
         out_specs=vmem,
         out_shape=jax.ShapeDtypeStruct((n_h, SPINS, 2, own, n_b), jnp.float32),

time: 60.3 us -> 55.7 us (0.924)
  starting transfers between devices: 19.5 us -> 17.1 us
  waiting for transfers between devices: 15.2 us -> 13.2 us
    ppermute x21 -> x15, waiting for transfers between devices: 14.9 us -> 9.18 us  [across(): return lax.ppermute(value, axis, pairs)]
    ppermute x2, waiting for transfers between devices: 0.34 us -> 4.03 us  [from_behind(): return lax.ppermute(value, axis, pairs)]
    ppermute x21 -> x15, starting transfers between devices: 16.6 us -> 13.5 us  [across(): return lax.ppermute(value, axis, pairs)]
    optimization_barrier x1 -> x0, local copies, waits for them, and re-layouts: 1.64 us -> none  [shards(): eigvecs, piece, both = lax.optimization_barrier((eigvecs, piece, both))]
    unnamed x9 -> x10, local copies, waits for them, and re-layouts: 1.38 us -> 2.8 us
    ppermute x2, starting transfers between devices: 2.92 us -> 3.57 us  [from_behind(): return lax.ppermute(value, axis, pairs)]
  transfers between devices with their start and end apart: 23 -> 17, of which waited for: 8 -> 7; matrix products, arithmetic and copies ran while one was open for 5% -> 5% of each run, Pallas kernels for 33% -> 35%
where the time goes in v1:
time: 55.7 us; the launch traced here: 55.5 us
  Pallas kernels  22.1 us (40%)
  starting transfers between devices  17.1 us (31%)
  waiting for transfers between devices  13.2 us (24%)
  local copies, waits for them, and re-layouts  3 us (5%)
    pallas_call x3, Pallas kernels, plane_call(): pl.pallas_call(functools.partial(plane_kernel, plane, dirs, part is not N...  18.7 us
    ppermute x15, starting transfers between devices, across(): return lax.ppermute(value, axis, pairs)  13.5 us
    ppermute x15, waiting for transfers between devices, across(): return lax.ppermute(value, axis, pairs)  9.18 us
    ppermute x2, waiting for transfers between devices, from_behind(): return lax.ppermute(value, axis, pairs)  4.03 us
    ppermute x2, starting transfers between devices, from_behind(): return lax.ppermute(value, axis, pairs)  3.57 us
    unnamed x10, local copies, waits for them, and re-layouts  2.8 us
    pallas_call x1, Pallas kernels, shards(): pl.pallas_call(functools.partial(quark_kernel, masks, n_op, len(got), len...  2.26 us
  transfers between devices with their start and end apart: 17, of which 7 were waited for; matrix products, arithmetic and copies ran while one was open for 5% of the time, Pallas kernels for 35%

profile of v1, /device:TPU:0, one launch (start us, length us, event | category | flops | bytes accessed | tf_op | source)
XLA Modules:
  0.0 55.5 jit_solution(2619021727977276002)
XLA Ops:
  0.0 3.0 %collective-permute-start = (s32[2,3]{1,0:T(2,128)}, s32[2,3]{1,0:T(2,128)S(1)}, u32[]{:S(2)}, u32[]{:S(2)}) collective-permute-start(s32[2,3]{1,0:T(2,128)} %refs_0_), channel_id=1, source_target_pairs={{0,1},{1,0},{2,3},{3,2},{4,5},{5,4},{6,7},{7,6},{8,9},{9,8},{10,11... | collective-permute-start | bytes 80 | tf_op jit(solution)/shard_map/ppermute | solution.py:29
  3.1 1.1 %dynamic-slice_bitcast_fusion = bf16[256,1,2,256]{3,2,0,1:T(2,128)(2,1)S(1)} fusion(bf16[256,16,2,256]{3,2,1,0:T(2,128)(2,1)} %bitcast.23, s32[]{:T(128)S(6)} %select_n.14), kind=kLoop, calls=%fused_computation.3 | loop fusion | bytes 524292
  4.2 0.1 reshape.10
  4.3 1.6 %copy.11 = bf16[1,2,256,3,2,256]{5,2,3,1,4,0:T(8,128)(2,1)S(1)} copy(bf16[1,2,256,3,2,256]{5,4,3,2,1,0:T(2,128)(2,1)} %param.6) | data formatting | bytes 3145728 | tf_op args[0]
  6.0 0.8 %collective-permute-done.1.refs_3_ = s32[3,2,4]{2,1,0:T(2,128)S(1)} collective-permute-done((s32[3,2,4]{2,1,0:T(2,128)}, s32[3,2,4]{2,1,0:T(2,128)S(1)}, u32[]{:S(2)}, u32[]{:S(2)}) %collective-permute-start.1) | collective-permute-done | bytes 128 | tf_op jit(solution)/shard_map/ppermute | solution.py:29
  6.8 0.1 slice_bitcast_fusion
  6.9 1.0 %collective-permute-start.9 = (bf16[2,3,256,256]{3,2,1,0:T(8,128)(2,1)S(1)}, bf16[2,3,256,256]{3,2,1,0:T(8,128)(2,1)S(1)}, u32[]{:S(2)}, u32[]{:S(2)}) collective-permute-start(bf16[2,3,256,256]{3,2,1,0:T(8,128)(2,1)S(1)} %get-tuple-element.71.refs_0_), channel_id=1, source_target_pairs={{0,28},{4,0},{8,4},{12,8},{16,12},{20,16},{24,20},{28,24},{1,29},{... | collective-permute-start | bytes 2359304 | tf_op jit(solution)/shard_map/ppermute | solution.py:24
  7.9 2.6 %collective-permute-start.2 = (bf16[512,256]{1,0:T(8,128)(2,1)S(1)}, bf16[512,256]{1,0:T(8,128)(2,1)S(1)}, u32[]{:S(2)}, u32[]{:S(2)}) collective-permute-start(bf16[512,256]{1,0:T(8,128)(2,1)S(1)} %reshape.10), channel_id=1, source_target_pairs={{0,2},{2,0},{1,3},{3,1},{4,6},{6,4},{5,7},{7,5},{8,10},{10,8},{9,1... | collective-permute-start | bytes 786440 | tf_op jit(solution)/shard_map/ppermute | solution.py:24
  10.5 0.9 %phases.1.refs_2_.refs_3_ = f32[2,2,3,2,2,256]{5,4,3,2,1,0:T(2,128)S(1)} custom-call(s32[2,3]{1,0:T(2,128)S(1)} %copy-done.1, s32[2,3]{1,0:T(2,128)S(1)} %collective-permute-done.refs_1_, s32[3,2,4]{2,1,0:T(2,128)S(1)} %bitcast.18, s32[3,2,4]{2,1,0:T(2,128)S(1)} %collective-permute-done.1.refs_3_, s32[4]{0:T(128)S(1)} %copy-done.2), custom_call_target="tpu_custom_call" | custom-call | tf_op jit(solution)/shard_map/phases/pallas_call | solution.py:338
  11.5 6.7 %plane1_12.1.refs_4_ = f32[2,2,256,256]{3,2,1,0:T(8,128)S(1)} custom-call(bf16[2,3,256,256]{3,2,1,0:T(8,128)(2,1)S(1)} %get-tuple-element.72.refs_0_.refs_1_, f32[3,3,3,2,2,256]{5,4,3,2,1,0:T(2,128)S(1)} %bitcast.19, f32[2,2,3,2,2,256]{5,4,3,2,1,0:T(2,128)S(1)} %phases.1.refs_2_.refs_3_), custom_call_target="tpu_custom_call" | custom-call | flops 3221225472 | bytes 4194304 | tf_op jit(solution)/shard_map/plane1_12/pallas_call | solution.py:163
  18.2 4.0 %collective-permute-done.2.refs_0_.refs_4_ = bf16[512,256]{1,0:T(8,128)(2,1)S(1)} collective-permute-done((bf16[512,256]{1,0:T(8,128)(2,1)S(1)}, bf16[512,256]{1,0:T(8,128)(2,1)S(1)}, u32[]{:S(2)}, u32[]{:S(2)}) %collective-permute-start.2) | collective-permute-done | bytes 262176 | tf_op jit(solution)/shard_map/ppermute | solution.py:24
  22.2 1.5 %collective-permute-start.5 = (bf16[512,256]{1,0:T(8,128)(2,1)S(1)}, bf16[512,256]{1,0:T(8,128)(2,1)S(1)}, u32[]{:S(2)}, u32[]{:S(2)}) collective-permute-start(bf16[512,256]{1,0:T(8,128)(2,1)S(1)} %collective-permute-done.2.refs_0_.refs_4_), channel_id=1, source_target_pairs={{0,16},{4,20},{8,24},{12,28},{16,0},{20,4},{24,8},{28,12},{1,17},{... | collective-permute-start | bytes 786440 | tf_op jit(solution)/shard_map/ppermute | solution.py:29
  23.8 1.5 %collective-permute-start.4 = (bf16[512,256]{1,0:T(8,128)(2,1)S(1)}, bf16[512,256]{1,0:T(8,128)(2,1)S(1)}, u32[]{:S(2)}, u32[]{:S(2)}) collective-permute-start(bf16[512,256]{1,0:T(8,128)(2,1)S(1)} %collective-permute-done.2.refs_0_.refs_4_), channel_id=1, source_target_pairs={{0,8},{4,12},{8,0},{12,4},{16,24},{20,28},{24,16},{28,20},{1,9},{5... | collective-permute-start | bytes 786440 | tf_op jit(solution)/shard_map/ppermute | solution.py:29
  25.3 0.4 collective-permute-start.3
  25.7 8.3 %plane0_120.1.refs_4_ = f32[2,2,256,256]{3,2,1,0:T(8,128)S(1)} custom-call(bf16[2,3,256,256]{3,2,1,0:T(8,128)(2,1)S(1)} %get-tuple-element.71.refs_0_, bf16[2,3,256,256]{3,2,1,0:T(8,128)(2,1)S(1)} %get-tuple-element.72.refs_0_.refs_1_, f32[3,3,3,2,2,256]{5,4,3,2,1,0:T(2,128)S(1)} %bitcast.20, f32[2,2,3,2,2,256]{5,4,3,2,1,0:T(2,128)S(1)} %phases.1.refs_2_.refs_3_, ...), custom_call_target="tpu_custom_call" | custom-call | flops 4026531840 | bytes 4194304 | tf_op jit(solution)/shard_map/plane0_120/pallas_call | solution.py:163
  34.0 0.6 %collective-permute-start.7 = (bf16[512,256]{1,0:T(8,128)(2,1)S(1)}, bf16[512,256]{1,0:T(8,128)(2,1)S(1)}, u32[]{:S(2)}, u32[]{:S(2)}) collective-permute-start(bf16[512,256]{1,0:T(8,128)(2,1)S(1)} %collective-permute-done.3.refs_1_.refs_5_), channel_id=1, source_target_pairs={{0,16},{4,20},{8,24},{12,28},{16,0},{20,4},{24,8},{28,12},{1,17},{... | collective-permute-start | bytes 786440 | tf_op jit(solution)/shard_map/ppermute | solution.py:29
  34.6 1.6 %collective-permute-start.6 = (bf16[512,256]{1,0:T(8,128)(2,1)S(1)}, bf16[512,256]{1,0:T(8,128)(2,1)S(1)}, u32[]{:S(2)}, u32[]{:S(2)}) collective-permute-start(bf16[512,256]{1,0:T(8,128)(2,1)S(1)} %collective-permute-done.4.refs_2_.refs_6_), channel_id=1, source_target_pairs={{0,1},{1,0},{2,3},{3,2},{4,5},{5,4},{6,7},{7,6},{8,9},{9,8},{10,11... | collective-permute-start | bytes 786440 | tf_op jit(solution)/shard_map/ppermute | solution.py:29
  36.2 0.5 collective-permute-start.8
  36.7 3.7 %plane1_0.1 = (f32[4,2,2,32,256]{4,3,2,1,0:T(8,128)S(1)}, bf16[4,2,2,32,256]{4,3,2,1,0:T(8,128)(2,1)S(1)}) custom-call(bf16[2,3,256,256]{3,2,1,0:T(8,128)(2,1)S(1)} %get-tuple-element.72.refs_0_.refs_1_, bf16[2,3,256,256]{3,2,1,0:T(8,128)(2,1)S(1)} %collective-permute-done.9.refs_1_, f32[3,3,3,2,2,256]{5,4,3,2,1,0:T(2,128)S(1)} %bitcast.21, ...), custom_call_target="tpu_custom_call" | custom-call | flops 2415919104 | bytes 4194304 | tf_op jit(solution)/shard_map/plane1_0/pallas_call | solution.py:163
  40.5 0.7 %collective-permute-done.7.refs_5_.refs_9_ = bf16[512,256]{1,0:T(8,128)(2,1)S(1)} collective-permute-done((bf16[512,256]{1,0:T(8,128)(2,1)S(1)}, bf16[512,256]{1,0:T(8,128)(2,1)S(1)}, u32[]{:S(2)}, u32[]{:S(2)}) %collective-permute-start.7) | collective-permute-done | bytes 262176 | tf_op jit(solution)/shard_map/ppermute | solution.py:29
  41.2 0.2 collective-permute-done.6.refs_4_.refs_8_
  41.5 1.2 %collective-permute-done.8.refs_6_.refs_10_ = bf16[512,256]{1,0:T(8,128)(2,1)S(1)} collective-permute-done((bf16[512,256]{1,0:T(8,128)(2,1)S(1)}, bf16[512,256]{1,0:T(8,128)(2,1)S(1)}, u32[]{:S(2)}, u32[]{:S(2)}) %collective-permute-start.8) | collective-permute-done | bytes 262176 | tf_op jit(solution)/shard_map/ppermute | solution.py:29
  42.7 0.2 merge_cores.1
  42.9 0.1 collective-permute-start.15
  42.9 0.6 %collective-permute-start.10 = (bf16[512,256]{1,0:T(8,128)(2,1)S(1)}, bf16[512,256]{1,0:T(8,128)(2,1)S(1)}, u32[]{:S(2)}, u32[]{:S(2)}) collective-permute-start(bf16[512,256]{1,0:T(8,128)(2,1)S(1)} %collective-permute-done.8.refs_6_.refs_10_), channel_id=1, source_target_pairs={{0,1},{1,0},{2,3},{3,2},{4,5},{5,4},{6,7},{7,6},{8,9},{9,8},{10,11... | collective-permute-start | bytes 786440 | tf_op jit(solution)/shard_map/ppermute | solution.py:29
  43.5 0.8 %collective-permute-start.12 = (bf16[128,256]{1,0:T(8,128)(2,1)S(1)}, bf16[128,256]{1,0:T(8,128)(2,1)S(1)}, u32[]{:S(2)}, u32[]{:S(2)}) collective-permute-start(bf16[128,256]{1,0:T(8,128)(2,1)S(1)} %get-tuple-element.62), channel_id=1, source_target_pairs={{0,8},{4,12},{8,0},{12,4},{16,24},{20,28},{24,16},{28,20},{1,9},{5... | collective-permute-start | bytes 196616 | tf_op jit(solution)/shard_map/ppermute | solution.py:29
  44.3 1.5 %collective-permute-start.13 = (bf16[128,256]{1,0:T(8,128)(2,1)S(1)}, bf16[128,256]{1,0:T(8,128)(2,1)S(1)}, u32[]{:S(2)}, u32[]{:S(2)}) collective-permute-start(bf16[128,256]{1,0:T(8,128)(2,1)S(1)} %get-tuple-element.63), channel_id=1, source_target_pairs={{0,16},{4,20},{8,24},{12,28},{16,0},{20,4},{24,8},{28,12},{1,17},{... | collective-permute-start | bytes 196616 | tf_op jit(solution)/shard_map/ppermute | solution.py:29
  45.8 1.2 %collective-permute-start.14 = (bf16[128,256]{1,0:T(8,128)(2,1)S(1)}, bf16[128,256]{1,0:T(8,128)(2,1)S(1)}, u32[]{:S(2)}, u32[]{:S(2)}) collective-permute-start(bf16[128,256]{1,0:T(8,128)(2,1)S(1)} %get-tuple-element.64), channel_id=1, source_target_pairs={{0,24},{4,28},{8,16},{12,20},{16,8},{20,12},{24,0},{28,4},{1,25},{... | collective-permute-start | bytes 196616 | tf_op jit(solution)/shard_map/ppermute | solution.py:29
  47.0 4.6 %collective-permute-done.10.refs_11_ = bf16[512,256]{1,0:T(8,128)(2,1)S(1)} collective-permute-done((bf16[512,256]{1,0:T(8,128)(2,1)S(1)}, bf16[512,256]{1,0:T(8,128)(2,1)S(1)}, u32[]{:S(2)}, u32[]{:S(2)}) %collective-permute-start.10) | collective-permute-done | bytes 262176 | tf_op jit(solution)/shard_map/ppermute | solution.py:29
  51.7 0.1 collective-permute-start.16
  51.8 1.5 %collective-permute-done.16.refs_13_ = bf16[512,256]{1,0:T(8,128)(2,1)S(1)} collective-permute-done((bf16[512,256]{1,0:T(8,128)(2,1)S(1)}, bf16[512,256]{1,0:T(8,128)(2,1)S(1)}, u32[]{:S(2)}, u32[]{:S(2)}) %collective-permute-start.16) | collective-permute-done | bytes 262176 | tf_op jit(solution)/shard_map/ppermute | solution.py:29
  53.3 2.3 %quark_products.1 = f32[2,16,2,32,256]{4,3,2,1,0:T(8,128)} custom-call(f32[128,256]{1,0:T(8,128)S(1)} %get-tuple-element.65.refs_0_, bf16[128,256]{1,0:T(8,128)(2,1)S(1)} %collective-permute-done.12.refs_1_, bf16[128,256]{1,0:T(8,128)(2,1)S(1)} %collective-permute-done.13.refs_2_, bf16[128,256]{1,0:T(8,128)(2,1)S(1)} %collective-permute-done.14.refs_3_, ...), custom_call_target="tpu_custom_call" | custom-call | flops 536870912 | bytes 7340032 | tf_op jit(solution)/shard_map/quark_products/pallas_call | solution.py:392
  (20 shorter events, 0.2 us)
Async XLA Ops:
  0.0 6.0 %collective-permute-start = (s32[2,3]{1,0:T(2,128)}, s32[2,3]{1,0:T(2,128)S(1)}, u32[]{:S(2)}, u32[]{:S(2)}) collective-permute-start(s32[2,3]{1,0:T(2,128)} %refs_0_), channel_id=1, source_target_pairs={{0,1},{1,0},{2,3},{3,2},{4,5},{5,4},{6,7},{7,6},{8,9},{9,8},{10,11... | collective-permute-start | bytes 80 | tf_op jit(solution)/shard_map/ppermute | solution.py:29
  3.0 3.8 %collective-permute-start.1 = (s32[3,2,4]{2,1,0:T(2,128)}, s32[3,2,4]{2,1,0:T(2,128)S(1)}, u32[]{:S(2)}, u32[]{:S(2)}) collective-permute-start(s32[3,2,4]{2,1,0:T(2,128)} %bitcast.17), channel_id=1, source_target_pairs={{0,1},{1,0},{2,3},{3,2},{4,5},{5,4},{6,7},{7,6},{8,9},{9,8},{10,11... | collective-permute-start | bytes 296 | tf_op jit(solution)/shard_map/ppermute | solution.py:29
  5.9 4.6 %copy-start = (s32[4,2,3]{0,1,2:T(2,128)S(1)}, s32[4,2,3]{0,1,2:T(2,128)}, u32[]{:S(2)}) copy-start(s32[4,2,3]{0,1,2:T(2,128)} %param.9) | copy-start | bytes 292
  6.0 4.6 %copy-start.1 = (s32[2,3]{1,0:T(2,128)S(1)}, s32[2,3]{1,0:T(2,128)}, u32[]{:S(2)}) copy-start(s32[2,3]{1,0:T(2,128)} %refs_0_) | copy-start | bytes 76
  6.0 4.6 %copy-start.2 = (s32[4]{0:T(128)S(1)}, s32[4]{0:T(128)}, u32[]{:S(2)}) copy-start(s32[4]{0:T(128)} %refs_4_.1) | copy-start | bytes 52
  6.0 5.5 %copy-start.3 = (f32[1,3,3,3,2,2,256]{6,5,4,3,2,1,0:T(2,128)S(1)}, f32[1,3,3,3,2,2,256]{6,5,4,3,2,1,0:T(2,128)}, u32[]{:S(2)}) copy-start(f32[1,3,3,3,2,2,256]{6,5,4,3,2,1,0:T(2,128)} %param.7) | copy-start | bytes 331780
  6.9 29.8 %collective-permute-start.9 = (bf16[2,3,256,256]{3,2,1,0:T(8,128)(2,1)S(1)}, bf16[2,3,256,256]{3,2,1,0:T(8,128)(2,1)S(1)}, u32[]{:S(2)}, u32[]{:S(2)}) collective-permute-start(bf16[2,3,256,256]{3,2,1,0:T(8,128)(2,1)S(1)} %get-tuple-element.71.refs_0_), channel_id=1, source_target_pairs={{0,28},{4,0},{8,4},{12,8},{16,12},{20,16},{24,20},{28,24},{1,29},{... | collective-permute-start | bytes 2359304 | tf_op jit(solution)/shard_map/ppermute | solution.py:24
  7.9 14.3 %collective-permute-start.2 = (bf16[512,256]{1,0:T(8,128)(2,1)S(1)}, bf16[512,256]{1,0:T(8,128)(2,1)S(1)}, u32[]{:S(2)}, u32[]{:S(2)}) collective-permute-start(bf16[512,256]{1,0:T(8,128)(2,1)S(1)} %reshape.10), channel_id=1, source_target_pairs={{0,2},{2,0},{1,3},{3,1},{4,6},{6,4},{5,7},{7,5},{8,10},{10,8},{9,1... | collective-permute-start | bytes 786440 | tf_op jit(solution)/shard_map/ppermute | solution.py:24
  22.2 11.7 %collective-permute-start.5 = (bf16[512,256]{1,0:T(8,128)(2,1)S(1)}, bf16[512,256]{1,0:T(8,128)(2,1)S(1)}, u32[]{:S(2)}, u32[]{:S(2)}) collective-permute-start(bf16[512,256]{1,0:T(8,128)(2,1)S(1)} %collective-permute-done.2.refs_0_.refs_4_), channel_id=1, source_target_pairs={{0,16},{4,20},{8,24},{12,28},{16,0},{20,4},{24,8},{28,12},{1,17},{... | collective-permute-start | bytes 786440 | tf_op jit(solution)/shard_map/ppermute | solution.py:29
  23.8 10.2 %collective-permute-start.4 = (bf16[512,256]{1,0:T(8,128)(2,1)S(1)}, bf16[512,256]{1,0:T(8,128)(2,1)S(1)}, u32[]{:S(2)}, u32[]{:S(2)}) collective-permute-start(bf16[512,256]{1,0:T(8,128)(2,1)S(1)} %collective-permute-done.2.refs_0_.refs_4_), channel_id=1, source_target_pairs={{0,8},{4,12},{8,0},{12,4},{16,24},{20,28},{24,16},{28,20},{1,9},{5... | collective-permute-start | bytes 786440 | tf_op jit(solution)/shard_map/ppermute | solution.py:29
  25.3 8.7 %collective-permute-start.3 = (bf16[512,256]{1,0:T(8,128)(2,1)S(1)}, bf16[512,256]{1,0:T(8,128)(2,1)S(1)}, u32[]{:S(2)}, u32[]{:S(2)}) collective-permute-start(bf16[512,256]{1,0:T(8,128)(2,1)S(1)} %collective-permute-done.2.refs_0_.refs_4_), channel_id=1, source_target_pairs={{0,1},{1,0},{2,3},{3,2},{4,5},{5,4},{6,7},{7,6},{8,9},{9,8},{10,11... | collective-permute-start | bytes 786440 | tf_op jit(solution)/shard_map/ppermute | solution.py:29
  34.0 7.2 %collective-permute-start.7 = (bf16[512,256]{1,0:T(8,128)(2,1)S(1)}, bf16[512,256]{1,0:T(8,128)(2,1)S(1)}, u32[]{:S(2)}, u32[]{:S(2)}) collective-permute-start(bf16[512,256]{1,0:T(8,128)(2,1)S(1)} %collective-permute-done.3.refs_1_.refs_5_), channel_id=1, source_target_pairs={{0,16},{4,20},{8,24},{12,28},{16,0},{20,4},{24,8},{28,12},{1,17},{... | collective-permute-start | bytes 786440 | tf_op jit(solution)/shard_map/ppermute | solution.py:29
  34.6 6.9 %collective-permute-start.6 = (bf16[512,256]{1,0:T(8,128)(2,1)S(1)}, bf16[512,256]{1,0:T(8,128)(2,1)S(1)}, u32[]{:S(2)}, u32[]{:S(2)}) collective-permute-start(bf16[512,256]{1,0:T(8,128)(2,1)S(1)} %collective-permute-done.4.refs_2_.refs_6_), channel_id=1, source_target_pairs={{0,1},{1,0},{2,3},{3,2},{4,5},{5,4},{6,7},{7,6},{8,9},{9,8},{10,11... | collective-permute-start | bytes 786440 | tf_op jit(solution)/shard_map/ppermute | solution.py:29
  36.2 6.5 %collective-permute-start.8 = (bf16[512,256]{1,0:T(8,128)(2,1)S(1)}, bf16[512,256]{1,0:T(8,128)(2,1)S(1)}, u32[]{:S(2)}, u32[]{:S(2)}) collective-permute-start(bf16[512,256]{1,0:T(8,128)(2,1)S(1)} %collective-permute-done.5.refs_3_.refs_7_), channel_id=1, source_target_pairs={{0,8},{4,12},{8,0},{12,4},{16,24},{20,28},{24,16},{28,20},{1,9},{5... | collective-permute-start | bytes 786440 | tf_op jit(solution)/shard_map/ppermute | solution.py:29
  40.4 2.2 %collective-permute-start.11 = (bf16[4,2,2,32,256]{4,3,2,1,0:T(8,128)(2,1)S(1)}, bf16[4,2,2,32,256]{4,3,2,1,0:T(8,128)(2,1)S(1)}, u32[]{:S(2)}, u32[]{:S(2)}) collective-permute-start(bf16[4,2,2,32,256]{4,3,2,1,0:T(8,128)(2,1)S(1)} %get-tuple-element.54), channel_id=1, source_target_pairs={{0,4},{4,0},{8,12},{12,8},{16,20},{20,16},{24,28},{28,24},{1,5},{5... | collective-permute-start | bytes 786440 | tf_op jit(solution)/shard_map/ppermute | solution.py:29
  42.9 10.4 %collective-permute-start.15 = (bf16[7,512,256]{2,1,0:T(8,128)(2,1)S(1)}, bf16[7,512,256]{2,1,0:T(8,128)(2,1)S(1)}, u32[]{:S(2)}, u32[]{:S(2)}) collective-permute-start(bf16[7,512,256]{2,1,0:T(8,128)(2,1)S(1)} %get-tuple-element.70), channel_id=1, source_target_pairs={{0,4},{4,0},{8,12},{12,8},{16,20},{20,16},{24,28},{28,24},{1,5},{5... | collective-permute-start | bytes 5505032 | tf_op jit(solution)/shard_map/ppermute | solution.py:29
  42.9 8.7 %collective-permute-start.10 = (bf16[512,256]{1,0:T(8,128)(2,1)S(1)}, bf16[512,256]{1,0:T(8,128)(2,1)S(1)}, u32[]{:S(2)}, u32[]{:S(2)}) collective-permute-start(bf16[512,256]{1,0:T(8,128)(2,1)S(1)} %collective-permute-done.8.refs_6_.refs_10_), channel_id=1, source_target_pairs={{0,1},{1,0},{2,3},{3,2},{4,5},{5,4},{6,7},{7,6},{8,9},{9,8},{10,11... | collective-permute-start | bytes 786440 | tf_op jit(solution)/shard_map/ppermute | solution.py:29
  43.5 8.1 %collective-permute-start.12 = (bf16[128,256]{1,0:T(8,128)(2,1)S(1)}, bf16[128,256]{1,0:T(8,128)(2,1)S(1)}, u32[]{:S(2)}, u32[]{:S(2)}) collective-permute-start(bf16[128,256]{1,0:T(8,128)(2,1)S(1)} %get-tuple-element.62), channel_id=1, source_target_pairs={{0,8},{4,12},{8,0},{12,4},{16,24},{20,28},{24,16},{28,20},{1,9},{5... | collective-permute-start | bytes 196616 | tf_op jit(solution)/shard_map/ppermute | solution.py:29
  44.3 7.3 %collective-permute-start.13 = (bf16[128,256]{1,0:T(8,128)(2,1)S(1)}, bf16[128,256]{1,0:T(8,128)(2,1)S(1)}, u32[]{:S(2)}, u32[]{:S(2)}) collective-permute-start(bf16[128,256]{1,0:T(8,128)(2,1)S(1)} %get-tuple-element.63), channel_id=1, source_target_pairs={{0,16},{4,20},{8,24},{12,28},{16,0},{20,4},{24,8},{28,12},{1,17},{... | collective-permute-start | bytes 196616 | tf_op jit(solution)/shard_map/ppermute | solution.py:29
  45.8 5.8 %collective-permute-start.14 = (bf16[128,256]{1,0:T(8,128)(2,1)S(1)}, bf16[128,256]{1,0:T(8,128)(2,1)S(1)}, u32[]{:S(2)}, u32[]{:S(2)}) collective-permute-start(bf16[128,256]{1,0:T(8,128)(2,1)S(1)} %get-tuple-element.64), channel_id=1, source_target_pairs={{0,24},{4,28},{8,16},{12,20},{16,8},{20,12},{24,0},{28,4},{1,25},{... | collective-permute-start | bytes 196616 | tf_op jit(solution)/shard_map/ppermute | solution.py:29
  51.7 1.6 %collective-permute-start.16 = (bf16[512,256]{1,0:T(8,128)(2,1)S(1)}, bf16[512,256]{1,0:T(8,128)(2,1)S(1)}, u32[]{:S(2)}, u32[]{:S(2)}) collective-permute-start(bf16[512,256]{1,0:T(8,128)(2,1)S(1)} %collective-permute-done.10.refs_11_), channel_id=1, source_target_pairs={{0,4},{4,0},{8,12},{12,8},{16,20},{20,16},{24,28},{28,24},{1,5},{5... | collective-permute-start | bytes 786440 | tf_op jit(solution)/shard_map/ppermute | solution.py:29

commit v2 on v1

--- a/solution.py
+++ b/solution.py
@@ -176,37 +176,47 @@
     )(*args)
 
 
-def merge_kernel(n_early, keep_ref, got_ref, *refs):
-    early_refs = refs[:n_early]
-    pack_ref, own_ref = refs[n_early : n_early + 2]
+def merge_kernel(keep_ref, got_ref, own_ref, *out_refs):
     chip = lax.axis_index("space") >> 1
     shape = own_ref.shape
     own_ref[...] = (keep_ref[chip] + got_ref[chip].astype(jnp.float32)).reshape(shape)
-    for mask, out_ref in enumerate(refs[n_early + 2 :], 1):
+    for mask, out_ref in enumerate(out_refs, 1):
         total = keep_ref[chip ^ mask] + got_ref[chip ^ mask].astype(jnp.float32)
         out_ref[...] = total.reshape(shape).astype(jnp.bfloat16)
-    for which, ref in enumerate(early_refs):
-        pack_ref[which] = ref[...]
-
-
-def merge_call(keep, got, early):
+
+
+def merge_call(keep, got):
     chips, n_h, _, own, n_b = keep.shape
     shape = (n_h * 2 * own, n_b)
     vmem = pl.BlockSpec(memory_space=pltpu.VMEM)
-    out = pl.pallas_call(
-        functools.partial(merge_kernel, len(early)),
-        in_specs=[vmem] * (2 + len(early)),
-        out_specs=[vmem] * (1 + chips),
-        out_shape=[
-            jax.ShapeDtypeStruct((len(early),) + early[0].shape, jnp.bfloat16),
-            jax.ShapeDtypeStruct(shape, jnp.float32),
-        ]
+    return pl.pallas_call(
+        merge_kernel,
+        in_specs=[vmem, vmem],
+        out_specs=[vmem] * chips,
+        out_shape=[jax.ShapeDtypeStruct(shape, jnp.float32)]
         + [jax.ShapeDtypeStruct(shape, jnp.bfloat16)] * (chips - 1),
         compiler_params=pltpu.CompilerParams(vmem_limit_bytes=8 * 2**20),
         cost_estimate=pl.CostEstimate(flops=2**16, bytes_accessed=2**12, transcendentals=0),
         name="merge_cores",
-    )(keep, got, *early)
-    return out[0], out[1:]
+    )(keep, got)
+
+
+def pack_kernel(*refs):
+    for which, ref in enumerate(refs[:-1]):
+        refs[-1][which] = ref[...]
+
+
+def pack_call(arrs):
+    vmem = pl.BlockSpec(memory_space=pltpu.VMEM)
+    return pl.pallas_call(
+        pack_kernel,
+        in_specs=[vmem] * len(arrs),
+        out_specs=vmem,
+        out_shape=jax.ShapeDtypeStruct((len(arrs),) + arrs[0].shape, arrs[0].dtype),
+        compiler_params=pltpu.CompilerParams(vmem_limit_bytes=8 * 2**20),
+        cost_estimate=pl.CostEstimate(flops=2**16, bytes_accessed=2**12, transcendentals=0),
+        name="pack_pieces",
+    )(*arrs)
 
 
 def quark_kernel(masks, n_op, n_got, n_tau, n_h, *refs):
@@ -361,11 +371,13 @@
 
     link = links[0]
     last = planes - 1
-    partial = plane_call(last, (1, 2), vecs[last], None, link, phi)
+    partial = None
+    for plane in range(planes):
+        partial = plane_call(plane, (1, 2), vecs[plane], None, link, phi, partial)
     held, partial = hold({(): own_piece}, partial)
     stage(held, 1)
     for plane in range(last):
-        partial = plane_call(plane, (1, 2, 0), vecs[plane], vecs[plane + 1], link, phi, partial)
+        partial = plane_call(plane, (0,), vecs[plane], vecs[plane + 1], link, phi, partial)
     held, partial = hold(held, partial)
     stage(held, 2)
     keep, give = plane_call(last, (0,), vecs[last], upper, link, phi, partial, n_space)
@@ -375,7 +387,8 @@
         stage(held, size)
     early = [key for key in held if len(key) < 3]
     late = [key for key in held if len(key) >= 3]
-    packed, merged = merge_call(keep, swapped, [held[key] for key in early])
+    packed = pack_call([held[key] for key in early])
+    merged = merge_call(keep, swapped)
     got = [merged[0]] + [across(arr, "space", 2 * mask) for mask, arr in enumerate(merged[1:], 1)]
     last_held, got = hold({key: held[key] for key in late}, got)
     held.update(last_held)

time: 55.7 us -> 59.4 us (1.066)
  Pallas kernels: 22.1 us -> 24.3 us
  waiting for transfers between devices: 13.2 us -> 14.6 us
    ppermute x15, waiting for transfers between devices: 9.18 us -> 14.6 us  [across(): return lax.ppermute(value, axis, pairs)]
    ppermute x2, waiting for transfers between devices: 4.03 us -> 0.01 us  [from_behind(): return lax.ppermute(value, axis, pairs)]
    pallas_call x3 -> x4, Pallas kernels: 18.7 us -> 20.9 us  [plane_call(): pl.pallas_call(functools.partial(plane_kernel, plane, dirs, part is not N...]
  transfers between devices with their start and end apart: 17 -> 17, of which waited for: 7 -> 12; matrix products, arithmetic and copies ran while one was open for 5% -> 5% of each run, Pallas kernels for 35% -> 37%
where the time goes in v2:
time: 59.4 us; the launch traced here: 59.3 us
  Pallas kernels  24.3 us (41%)
  starting transfers between devices  17.3 us (29%)
  waiting for transfers between devices  14.6 us (25%)
  local copies, waits for them, and re-layouts  3 us (5%)
    pallas_call x4, Pallas kernels, plane_call(): pl.pallas_call(functools.partial(plane_kernel, plane, dirs, part is not N...  20.9 us
    ppermute x15, waiting for transfers between devices, across(): return lax.ppermute(value, axis, pairs)  14.6 us
    ppermute x15, starting transfers between devices, across(): return lax.ppermute(value, axis, pairs)  13.9 us
    ppermute x2, starting transfers between devices, from_behind(): return lax.ppermute(value, axis, pairs)  3.35 us
    unnamed x10, local copies, waits for them, and re-layouts  2.8 us
    pallas_call x1, Pallas kernels, shards(): pl.pallas_call(functools.partial(quark_kernel, masks, n_op, len(got), len...  2.26 us
  transfers between devices with their start and end apart: 17, of which 12 were waited for; matrix products, arithmetic and copies ran while one was open for 5% of the time, Pallas kernels for 37%

profile of v2, /device:TPU:0, one launch (start us, length us, event | category | flops | bytes accessed | tf_op | source)
XLA Modules:
  0.0 59.3 jit_solution(12795543180862394635)
XLA Ops:
  0.0 3.0 %collective-permute-start = (s32[2,3]{1,0:T(2,128)}, s32[2,3]{1,0:T(2,128)S(1)}, u32[]{:S(2)}, u32[]{:S(2)}) collective-permute-start(s32[2,3]{1,0:T(2,128)} %refs_0_), channel_id=1, source_target_pairs={{0,1},{1,0},{2,3},{3,2},{4,5},{5,4},{6,7},{7,6},{8,9},{9,8},{10,11... | collective-permute-start | bytes 80 | tf_op jit(solution)/shard_map/ppermute | solution.py:29
  3.1 1.1 %dynamic-slice_bitcast_fusion = bf16[256,1,2,256]{3,2,0,1:T(2,128)(2,1)S(1)} fusion(bf16[256,16,2,256]{3,2,1,0:T(2,128)(2,1)} %bitcast.24, s32[]{:T(128)S(6)} %select_n.14), kind=kLoop, calls=%fused_computation.3 | loop fusion | bytes 524292
  4.3 1.6 %copy.11 = bf16[1,2,256,3,2,256]{5,2,3,1,4,0:T(8,128)(2,1)S(1)} copy(bf16[1,2,256,3,2,256]{5,4,3,2,1,0:T(2,128)(2,1)} %param.6) | data formatting | bytes 3145728 | tf_op args[0]
  6.0 0.8 %collective-permute-done.1.refs_3_ = s32[3,2,4]{2,1,0:T(2,128)S(1)} collective-permute-done((s32[3,2,4]{2,1,0:T(2,128)}, s32[3,2,4]{2,1,0:T(2,128)S(1)}, u32[]{:S(2)}, u32[]{:S(2)}) %collective-permute-start.1) | collective-permute-done | bytes 128 | tf_op jit(solution)/shard_map/ppermute | solution.py:29
  6.8 2.6 %collective-permute-start.2 = (bf16[512,256]{1,0:T(8,128)(2,1)S(1)}, bf16[512,256]{1,0:T(8,128)(2,1)S(1)}, u32[]{:S(2)}, u32[]{:S(2)}) collective-permute-start(bf16[512,256]{1,0:T(8,128)(2,1)S(1)} %reshape.10), channel_id=1, source_target_pairs={{0,2},{2,0},{1,3},{3,1},{4,6},{6,4},{5,7},{7,5},{8,10},{10,8},{9,1... | collective-permute-start | bytes 786440 | tf_op jit(solution)/shard_map/ppermute | solution.py:24
  9.5 0.8 %collective-permute-start.9 = (bf16[2,3,256,256]{3,2,1,0:T(8,128)(2,1)S(1)}, bf16[2,3,256,256]{3,2,1,0:T(8,128)(2,1)S(1)}, u32[]{:S(2)}, u32[]{:S(2)}) collective-permute-start(bf16[2,3,256,256]{3,2,1,0:T(8,128)(2,1)S(1)} %get-tuple-element.69.refs_0_), channel_id=1, source_target_pairs={{0,28},{4,0},{8,4},{12,8},{16,12},{20,16},{24,20},{28,24},{1,29},{... | collective-permute-start | bytes 2359304 | tf_op jit(solution)/shard_map/ppermute | solution.py:24
  10.3 0.9 %phases.1.refs_2_.refs_3_ = f32[2,2,3,2,2,256]{5,4,3,2,1,0:T(2,128)S(1)} custom-call(s32[2,3]{1,0:T(2,128)S(1)} %copy-done.1, s32[2,3]{1,0:T(2,128)S(1)} %collective-permute-done.refs_1_, s32[3,2,4]{2,1,0:T(2,128)S(1)} %bitcast.18, s32[3,2,4]{2,1,0:T(2,128)S(1)} %collective-permute-done.1.refs_3_, s32[4]{0:T(128)S(1)} %copy-done.2), custom_call_target="tpu_custom_call" | custom-call | tf_op jit(solution)/shard_map/phases/pallas_call | solution.py:348
  11.3 6.7 %plane0_12.1.refs_3_ = f32[2,2,256,256]{3,2,1,0:T(8,128)S(1)} custom-call(bf16[2,3,256,256]{3,2,1,0:T(8,128)(2,1)S(1)} %get-tuple-element.69.refs_0_, f32[3,3,3,2,2,256]{5,4,3,2,1,0:T(2,128)S(1)} %bitcast.19, f32[2,2,3,2,2,256]{5,4,3,2,1,0:T(2,128)S(1)} %phases.1.refs_2_.refs_3_), custom_call_target="tpu_custom_call" | custom-call | flops 3221225472 | bytes 4194304 | tf_op jit(solution)/shard_map/plane0_12/pallas_call | solution.py:163
  18.0 6.7 %plane1_12.1.refs_4_ = f32[2,2,256,256]{3,2,1,0:T(8,128)S(1)} custom-call(bf16[2,3,256,256]{3,2,1,0:T(8,128)(2,1)S(1)} %get-tuple-element.70.refs_0_.refs_1_, f32[3,3,3,2,2,256]{5,4,3,2,1,0:T(2,128)S(1)} %bitcast.20, f32[2,2,3,2,2,256]{5,4,3,2,1,0:T(2,128)S(1)} %phases.1.refs_2_.refs_3_, f32[2,2,256,256]{3,2,1,0:T(8,128)S(1)} %plane0_12.1.refs_3_), custom_call_target="tpu_custom_call" | custom-call | flops 3221225472 | bytes 4194304 | tf_op jit(solution)/shard_map/plane1_12/pallas_call | solution.py:163
  24.7 0.9 %collective-permute-start.5 = (bf16[512,256]{1,0:T(8,128)(2,1)S(1)}, bf16[512,256]{1,0:T(8,128)(2,1)S(1)}, u32[]{:S(2)}, u32[]{:S(2)}) collective-permute-start(bf16[512,256]{1,0:T(8,128)(2,1)S(1)} %collective-permute-done.2.refs_0_.refs_4_), channel_id=1, source_target_pairs={{0,16},{4,20},{8,24},{12,28},{16,0},{20,4},{24,8},{28,12},{1,17},{... | collective-permute-start | bytes 786440 | tf_op jit(solution)/shard_map/ppermute | solution.py:29
  25.7 1.5 %collective-permute-start.4 = (bf16[512,256]{1,0:T(8,128)(2,1)S(1)}, bf16[512,256]{1,0:T(8,128)(2,1)S(1)}, u32[]{:S(2)}, u32[]{:S(2)}) collective-permute-start(bf16[512,256]{1,0:T(8,128)(2,1)S(1)} %collective-permute-done.2.refs_0_.refs_4_), channel_id=1, source_target_pairs={{0,8},{4,12},{8,0},{12,4},{16,24},{20,28},{24,16},{28,20},{1,9},{5... | collective-permute-start | bytes 786440 | tf_op jit(solution)/shard_map/ppermute | solution.py:29
  27.1 1.3 %collective-permute-start.3 = (bf16[512,256]{1,0:T(8,128)(2,1)S(1)}, bf16[512,256]{1,0:T(8,128)(2,1)S(1)}, u32[]{:S(2)}, u32[]{:S(2)}) collective-permute-start(bf16[512,256]{1,0:T(8,128)(2,1)S(1)} %collective-permute-done.2.refs_0_.refs_4_), channel_id=1, source_target_pairs={{0,1},{1,0},{2,3},{3,2},{4,5},{5,4},{6,7},{7,6},{8,9},{9,8},{10,11... | collective-permute-start | bytes 786440 | tf_op jit(solution)/shard_map/ppermute | solution.py:29
  28.4 3.7 %plane0_0.1.refs_4_ = f32[2,2,256,256]{3,2,1,0:T(8,128)S(1)} custom-call(bf16[2,3,256,256]{3,2,1,0:T(8,128)(2,1)S(1)} %get-tuple-element.69.refs_0_, bf16[2,3,256,256]{3,2,1,0:T(8,128)(2,1)S(1)} %get-tuple-element.70.refs_0_.refs_1_, f32[3,3,3,2,2,256]{5,4,3,2,1,0:T(2,128)S(1)} %bitcast.21, f32[2,2,3,2,2,256]{5,4,3,2,1,0:T(2,128)S(1)} %phases.1.refs_2_.refs_3_, ...), custom_call_target="tpu_custom_call" | custom-call | flops 2415919104 | bytes 4194304 | tf_op jit(solution)/shard_map/plane0_0/pallas_call | solution.py:163
  32.1 0.7 %collective-permute-done.5.refs_3_.refs_7_ = bf16[512,256]{1,0:T(8,128)(2,1)S(1)} collective-permute-done((bf16[512,256]{1,0:T(8,128)(2,1)S(1)}, bf16[512,256]{1,0:T(8,128)(2,1)S(1)}, u32[]{:S(2)}, u32[]{:S(2)}) %collective-permute-start.5) | collective-permute-done | bytes 262176 | tf_op jit(solution)/shard_map/ppermute | solution.py:29
  32.8 1.2 %collective-permute-done.4.refs_2_.refs_6_ = bf16[512,256]{1,0:T(8,128)(2,1)S(1)} collective-permute-done((bf16[512,256]{1,0:T(8,128)(2,1)S(1)}, bf16[512,256]{1,0:T(8,128)(2,1)S(1)}, u32[]{:S(2)}, u32[]{:S(2)}) %collective-permute-start.4) | collective-permute-done | bytes 262176 | tf_op jit(solution)/shard_map/ppermute | solution.py:29
  34.1 1.2 %collective-permute-done.3.refs_1_.refs_5_ = bf16[512,256]{1,0:T(8,128)(2,1)S(1)} collective-permute-done((bf16[512,256]{1,0:T(8,128)(2,1)S(1)}, bf16[512,256]{1,0:T(8,128)(2,1)S(1)}, u32[]{:S(2)}, u32[]{:S(2)}) %collective-permute-start.3) | collective-permute-done | bytes 262176 | tf_op jit(solution)/shard_map/ppermute | solution.py:29
  35.3 0.5 collective-permute-start.7
  35.8 1.2 %collective-permute-start.6 = (bf16[512,256]{1,0:T(8,128)(2,1)S(1)}, bf16[512,256]{1,0:T(8,128)(2,1)S(1)}, u32[]{:S(2)}, u32[]{:S(2)}) collective-permute-start(bf16[512,256]{1,0:T(8,128)(2,1)S(1)} %collective-permute-done.4.refs_2_.refs_6_), channel_id=1, source_target_pairs={{0,1},{1,0},{2,3},{3,2},{4,5},{5,4},{6,7},{7,6},{8,9},{9,8},{10,11... | collective-permute-start | bytes 786440 | tf_op jit(solution)/shard_map/ppermute | solution.py:29
  37.0 0.5 collective-permute-start.8
  37.6 3.7 %plane1_0.1 = (f32[4,2,2,32,256]{4,3,2,1,0:T(8,128)S(1)}, bf16[4,2,2,32,256]{4,3,2,1,0:T(8,128)(2,1)S(1)}) custom-call(bf16[2,3,256,256]{3,2,1,0:T(8,128)(2,1)S(1)} %get-tuple-element.70.refs_0_.refs_1_, bf16[2,3,256,256]{3,2,1,0:T(8,128)(2,1)S(1)} %collective-permute-done.9.refs_1_, f32[3,3,3,2,2,256]{5,4,3,2,1,0:T(2,128)S(1)} %bitcast.22, ...), custom_call_target="tpu_custom_call" | custom-call | flops 2415919104 | bytes 4194304 | tf_op jit(solution)/shard_map/plane1_0/pallas_call | solution.py:163
  41.3 1.3 %collective-permute-done.7.refs_5_.refs_9_ = bf16[512,256]{1,0:T(8,128)(2,1)S(1)} collective-permute-done((bf16[512,256]{1,0:T(8,128)(2,1)S(1)}, bf16[512,256]{1,0:T(8,128)(2,1)S(1)}, u32[]{:S(2)}, u32[]{:S(2)}) %collective-permute-start.7) | collective-permute-done | bytes 262176 | tf_op jit(solution)/shard_map/ppermute | solution.py:29
  42.8 1.0 %collective-permute-done.8.refs_6_.refs_10_ = bf16[512,256]{1,0:T(8,128)(2,1)S(1)} collective-permute-done((bf16[512,256]{1,0:T(8,128)(2,1)S(1)}, bf16[512,256]{1,0:T(8,128)(2,1)S(1)}, u32[]{:S(2)}, u32[]{:S(2)}) %collective-permute-start.8) | collective-permute-done | bytes 262176 | tf_op jit(solution)/shard_map/ppermute | solution.py:29
  43.9 0.5 collective-permute-start.11
  44.4 0.8 %collective-permute-start.10 = (bf16[512,256]{1,0:T(8,128)(2,1)S(1)}, bf16[512,256]{1,0:T(8,128)(2,1)S(1)}, u32[]{:S(2)}, u32[]{:S(2)}) collective-permute-start(bf16[512,256]{1,0:T(8,128)(2,1)S(1)} %collective-permute-done.8.refs_6_.refs_10_), channel_id=1, source_target_pairs={{0,1},{1,0},{2,3},{3,2},{4,5},{5,4},{6,7},{7,6},{8,9},{9,8},{10,11... | collective-permute-start | bytes 786440 | tf_op jit(solution)/shard_map/ppermute | solution.py:29
  45.2 2.9 %collective-permute-done.11.got_ref = bf16[4,2,2,32,256]{4,3,2,1,0:T(8,128)(2,1)S(1)} collective-permute-done((bf16[4,2,2,32,256]{4,3,2,1,0:T(8,128)(2,1)S(1)}, bf16[4,2,2,32,256]{4,3,2,1,0:T(8,128)(2,1)S(1)}, u32[]{:S(2)}, u32[]{:S(2)}) %collective-permute-start.11) | collective-permute-done | bytes 262176 | tf_op jit(solution)/shard_map/ppermute | solution.py:29
  48.1 0.8 %collective-permute-start.12 = (bf16[128,256]{1,0:T(8,128)(2,1)S(1)}, bf16[128,256]{1,0:T(8,128)(2,1)S(1)}, u32[]{:S(2)}, u32[]{:S(2)}) collective-permute-start(bf16[128,256]{1,0:T(8,128)(2,1)S(1)} %get-tuple-element.55), channel_id=1, source_target_pairs={{0,8},{4,12},{8,0},{12,4},{16,24},{20,28},{24,16},{28,20},{1,9},{5... | collective-permute-start | bytes 196616 | tf_op jit(solution)/shard_map/ppermute | solution.py:29
  48.9 1.4 %collective-permute-start.13 = (bf16[128,256]{1,0:T(8,128)(2,1)S(1)}, bf16[128,256]{1,0:T(8,128)(2,1)S(1)}, u32[]{:S(2)}, u32[]{:S(2)}) collective-permute-start(bf16[128,256]{1,0:T(8,128)(2,1)S(1)} %get-tuple-element.56), channel_id=1, source_target_pairs={{0,16},{4,20},{8,24},{12,28},{16,0},{20,4},{24,8},{28,12},{1,17},{... | collective-permute-start | bytes 196616 | tf_op jit(solution)/shard_map/ppermute | solution.py:29
  50.3 1.4 %collective-permute-start.14 = (bf16[128,256]{1,0:T(8,128)(2,1)S(1)}, bf16[128,256]{1,0:T(8,128)(2,1)S(1)}, u32[]{:S(2)}, u32[]{:S(2)}) collective-permute-start(bf16[128,256]{1,0:T(8,128)(2,1)S(1)} %get-tuple-element.57), channel_id=1, source_target_pairs={{0,24},{4,28},{8,16},{12,20},{16,8},{20,12},{24,0},{28,4},{1,25},{... | collective-permute-start | bytes 196616 | tf_op jit(solution)/shard_map/ppermute | solution.py:29
  51.7 1.0 %collective-permute-done.10.refs_11_ = bf16[512,256]{1,0:T(8,128)(2,1)S(1)} collective-permute-done((bf16[512,256]{1,0:T(8,128)(2,1)S(1)}, bf16[512,256]{1,0:T(8,128)(2,1)S(1)}, u32[]{:S(2)}, u32[]{:S(2)}) %collective-permute-start.10) | collective-permute-done | bytes 262176 | tf_op jit(solution)/shard_map/ppermute | solution.py:29
  53.1 2.3 %collective-permute-done.14.refs_3_ = bf16[128,256]{1,0:T(8,128)(2,1)S(1)} collective-permute-done((bf16[128,256]{1,0:T(8,128)(2,1)S(1)}, bf16[128,256]{1,0:T(8,128)(2,1)S(1)}, u32[]{:S(2)}, u32[]{:S(2)}) %collective-permute-start.14) | collective-permute-done | bytes 65568 | tf_op jit(solution)/shard_map/ppermute | solution.py:29
  55.5 1.5 %collective-permute-done.16.refs_13_ = bf16[512,256]{1,0:T(8,128)(2,1)S(1)} collective-permute-done((bf16[512,256]{1,0:T(8,128)(2,1)S(1)}, bf16[512,256]{1,0:T(8,128)(2,1)S(1)}, u32[]{:S(2)}, u32[]{:S(2)}) %collective-permute-start.16) | collective-permute-done | bytes 262176 | tf_op jit(solution)/shard_map/ppermute | solution.py:29
  57.0 2.3 %quark_products.1 = f32[2,16,2,32,256]{4,3,2,1,0:T(8,128)} custom-call(f32[128,256]{1,0:T(8,128)S(1)} %get-tuple-element.58.refs_0_, bf16[128,256]{1,0:T(8,128)(2,1)S(1)} %collective-permute-done.12.refs_1_, bf16[128,256]{1,0:T(8,128)(2,1)S(1)} %collective-permute-done.13.refs_2_, bf16[128,256]{1,0:T(8,128)(2,1)S(1)} %collective-permute-done.14.refs_3_, ...), custom_call_target="tpu_custom_call" | custom-call | flops 536870912 | bytes 7340032 | tf_op jit(solution)/shard_map/quark_products/pallas_call | solution.py:405
  (22 shorter events, 1.2 us)
Async XLA Ops:
  0.0 6.0 %collective-permute-start = (s32[2,3]{1,0:T(2,128)}, s32[2,3]{1,0:T(2,128)S(1)}, u32[]{:S(2)}, u32[]{:S(2)}) collective-permute-start(s32[2,3]{1,0:T(2,128)} %refs_0_), channel_id=1, source_target_pairs={{0,1},{1,0},{2,3},{3,2},{4,5},{5,4},{6,7},{7,6},{8,9},{9,8},{10,11... | collective-permute-start | bytes 80 | tf_op jit(solution)/shard_map/ppermute | solution.py:29
  3.0 3.8 %collective-permute-start.1 = (s32[3,2,4]{2,1,0:T(2,128)}, s32[3,2,4]{2,1,0:T(2,128)S(1)}, u32[]{:S(2)}, u32[]{:S(2)}) collective-permute-start(s32[3,2,4]{2,1,0:T(2,128)} %bitcast.17), channel_id=1, source_target_pairs={{0,1},{1,0},{2,3},{3,2},{4,5},{5,4},{6,7},{7,6},{8,9},{9,8},{10,11... | collective-permute-start | bytes 296 | tf_op jit(solution)/shard_map/ppermute | solution.py:29
  5.9 4.4 %copy-start = (s32[4,2,3]{0,1,2:T(2,128)S(1)}, s32[4,2,3]{0,1,2:T(2,128)}, u32[]{:S(2)}) copy-start(s32[4,2,3]{0,1,2:T(2,128)} %param.9) | copy-start | bytes 292
  6.0 4.3 %copy-start.1 = (s32[2,3]{1,0:T(2,128)S(1)}, s32[2,3]{1,0:T(2,128)}, u32[]{:S(2)}) copy-start(s32[2,3]{1,0:T(2,128)} %refs_0_) | copy-start | bytes 76
  6.0 4.3 %copy-start.2 = (s32[4]{0:T(128)S(1)}, s32[4]{0:T(128)}, u32[]{:S(2)}) copy-start(s32[4]{0:T(128)} %refs_4_.1) | copy-start | bytes 52
  6.0 5.3 %copy-start.3 = (f32[1,3,3,3,2,2,256]{6,5,4,3,2,1,0:T(2,128)S(1)}, f32[1,3,3,3,2,2,256]{6,5,4,3,2,1,0:T(2,128)}, u32[]{:S(2)}) copy-start(f32[1,3,3,3,2,2,256]{6,5,4,3,2,1,0:T(2,128)} %param.7) | copy-start | bytes 331780
  6.8 17.9 %collective-permute-start.2 = (bf16[512,256]{1,0:T(8,128)(2,1)S(1)}, bf16[512,256]{1,0:T(8,128)(2,1)S(1)}, u32[]{:S(2)}, u32[]{:S(2)}) collective-permute-start(bf16[512,256]{1,0:T(8,128)(2,1)S(1)} %reshape.10), channel_id=1, source_target_pairs={{0,2},{2,0},{1,3},{3,1},{4,6},{6,4},{5,7},{7,5},{8,10},{10,8},{9,1... | collective-permute-start | bytes 786440 | tf_op jit(solution)/shard_map/ppermute | solution.py:24
  9.5 28.0 %collective-permute-start.9 = (bf16[2,3,256,256]{3,2,1,0:T(8,128)(2,1)S(1)}, bf16[2,3,256,256]{3,2,1,0:T(8,128)(2,1)S(1)}, u32[]{:S(2)}, u32[]{:S(2)}) collective-permute-start(bf16[2,3,256,256]{3,2,1,0:T(8,128)(2,1)S(1)} %get-tuple-element.69.refs_0_), channel_id=1, source_target_pairs={{0,28},{4,0},{8,4},{12,8},{16,12},{20,16},{24,20},{28,24},{1,29},{... | collective-permute-start | bytes 2359304 | tf_op jit(solution)/shard_map/ppermute | solution.py:24
  24.7 8.1 %collective-permute-start.5 = (bf16[512,256]{1,0:T(8,128)(2,1)S(1)}, bf16[512,256]{1,0:T(8,128)(2,1)S(1)}, u32[]{:S(2)}, u32[]{:S(2)}) collective-permute-start(bf16[512,256]{1,0:T(8,128)(2,1)S(1)} %collective-permute-done.2.refs_0_.refs_4_), channel_id=1, source_target_pairs={{0,16},{4,20},{8,24},{12,28},{16,0},{20,4},{24,8},{28,12},{1,17},{... | collective-permute-start | bytes 786440 | tf_op jit(solution)/shard_map/ppermute | solution.py:29
  25.7 8.4 %collective-permute-start.4 = (bf16[512,256]{1,0:T(8,128)(2,1)S(1)}, bf16[512,256]{1,0:T(8,128)(2,1)S(1)}, u32[]{:S(2)}, u32[]{:S(2)}) collective-permute-start(bf16[512,256]{1,0:T(8,128)(2,1)S(1)} %collective-permute-done.2.refs_0_.refs_4_), channel_id=1, source_target_pairs={{0,8},{4,12},{8,0},{12,4},{16,24},{20,28},{24,16},{28,20},{1,9},{5... | collective-permute-start | bytes 786440 | tf_op jit(solution)/shard_map/ppermute | solution.py:29
  27.1 8.1 %collective-permute-start.3 = (bf16[512,256]{1,0:T(8,128)(2,1)S(1)}, bf16[512,256]{1,0:T(8,128)(2,1)S(1)}, u32[]{:S(2)}, u32[]{:S(2)}) collective-permute-start(bf16[512,256]{1,0:T(8,128)(2,1)S(1)} %collective-permute-done.2.refs_0_.refs_4_), channel_id=1, source_target_pairs={{0,1},{1,0},{2,3},{3,2},{4,5},{5,4},{6,7},{7,6},{8,9},{9,8},{10,11... | collective-permute-start | bytes 786440 | tf_op jit(solution)/shard_map/ppermute | solution.py:29
  35.3 7.3 %collective-permute-start.7 = (bf16[512,256]{1,0:T(8,128)(2,1)S(1)}, bf16[512,256]{1,0:T(8,128)(2,1)S(1)}, u32[]{:S(2)}, u32[]{:S(2)}) collective-permute-start(bf16[512,256]{1,0:T(8,128)(2,1)S(1)} %collective-permute-done.3.refs_1_.refs_5_), channel_id=1, source_target_pairs={{0,16},{4,20},{8,24},{12,28},{16,0},{20,4},{24,8},{28,12},{1,17},{... | collective-permute-start | bytes 786440 | tf_op jit(solution)/shard_map/ppermute | solution.py:29
  35.8 7.0 %collective-permute-start.6 = (bf16[512,256]{1,0:T(8,128)(2,1)S(1)}, bf16[512,256]{1,0:T(8,128)(2,1)S(1)}, u32[]{:S(2)}, u32[]{:S(2)}) collective-permute-start(bf16[512,256]{1,0:T(8,128)(2,1)S(1)} %collective-permute-done.4.refs_2_.refs_6_), channel_id=1, source_target_pairs={{0,1},{1,0},{2,3},{3,2},{4,5},{5,4},{6,7},{7,6},{8,9},{9,8},{10,11... | collective-permute-start | bytes 786440 | tf_op jit(solution)/shard_map/ppermute | solution.py:29
  37.0 6.7 %collective-permute-start.8 = (bf16[512,256]{1,0:T(8,128)(2,1)S(1)}, bf16[512,256]{1,0:T(8,128)(2,1)S(1)}, u32[]{:S(2)}, u32[]{:S(2)}) collective-permute-start(bf16[512,256]{1,0:T(8,128)(2,1)S(1)} %collective-permute-done.5.refs_3_.refs_7_), channel_id=1, source_target_pairs={{0,8},{4,12},{8,0},{12,4},{16,24},{20,28},{24,16},{28,20},{1,9},{5... | collective-permute-start | bytes 786440 | tf_op jit(solution)/shard_map/ppermute | solution.py:29
  43.8 13.2 %collective-permute-start.15 = (bf16[7,512,256]{2,1,0:T(8,128)(2,1)S(1)}, bf16[7,512,256]{2,1,0:T(8,128)(2,1)S(1)}, u32[]{:S(2)}, u32[]{:S(2)}) collective-permute-start(bf16[7,512,256]{2,1,0:T(8,128)(2,1)S(1)} %pack_pieces.1), channel_id=1, source_target_pairs={{0,4},{4,0},{8,12},{12,8},{16,20},{20,16},{24,28},{28,24},{1,5},{5... | collective-permute-start | bytes 5505032 | tf_op jit(solution)/shard_map/ppermute | solution.py:29
  43.9 4.1 %collective-permute-start.11 = (bf16[4,2,2,32,256]{4,3,2,1,0:T(8,128)(2,1)S(1)}, bf16[4,2,2,32,256]{4,3,2,1,0:T(8,128)(2,1)S(1)}, u32[]{:S(2)}, u32[]{:S(2)}) collective-permute-start(bf16[4,2,2,32,256]{4,3,2,1,0:T(8,128)(2,1)S(1)} %get-tuple-element.53), channel_id=1, source_target_pairs={{0,4},{4,0},{8,12},{12,8},{16,20},{20,16},{24,28},{28,24},{1,5},{5... | collective-permute-start | bytes 786440 | tf_op jit(solution)/shard_map/ppermute | solution.py:29
  44.4 8.3 %collective-permute-start.10 = (bf16[512,256]{1,0:T(8,128)(2,1)S(1)}, bf16[512,256]{1,0:T(8,128)(2,1)S(1)}, u32[]{:S(2)}, u32[]{:S(2)}) collective-permute-start(bf16[512,256]{1,0:T(8,128)(2,1)S(1)} %collective-permute-done.8.refs_6_.refs_10_), channel_id=1, source_target_pairs={{0,1},{1,0},{2,3},{3,2},{4,5},{5,4},{6,7},{7,6},{8,9},{9,8},{10,11... | collective-permute-start | bytes 786440 | tf_op jit(solution)/shard_map/ppermute | solution.py:29
  48.1 4.6 %collective-permute-start.12 = (bf16[128,256]{1,0:T(8,128)(2,1)S(1)}, bf16[128,256]{1,0:T(8,128)(2,1)S(1)}, u32[]{:S(2)}, u32[]{:S(2)}) collective-permute-start(bf16[128,256]{1,0:T(8,128)(2,1)S(1)} %get-tuple-element.55), channel_id=1, source_target_pairs={{0,8},{4,12},{8,0},{12,4},{16,24},{20,28},{24,16},{28,20},{1,9},{5... | collective-permute-start | bytes 196616 | tf_op jit(solution)/shard_map/ppermute | solution.py:29
  48.9 4.3 %collective-permute-start.13 = (bf16[128,256]{1,0:T(8,128)(2,1)S(1)}, bf16[128,256]{1,0:T(8,128)(2,1)S(1)}, u32[]{:S(2)}, u32[]{:S(2)}) collective-permute-start(bf16[128,256]{1,0:T(8,128)(2,1)S(1)} %get-tuple-element.56), channel_id=1, source_target_pairs={{0,16},{4,20},{8,24},{12,28},{16,0},{20,4},{24,8},{28,12},{1,17},{... | collective-permute-start | bytes 196616 | tf_op jit(solution)/shard_map/ppermute | solution.py:29
  50.3 5.2 %collective-permute-start.14 = (bf16[128,256]{1,0:T(8,128)(2,1)S(1)}, bf16[128,256]{1,0:T(8,128)(2,1)S(1)}, u32[]{:S(2)}, u32[]{:S(2)}) collective-permute-start(bf16[128,256]{1,0:T(8,128)(2,1)S(1)} %get-tuple-element.57), channel_id=1, source_target_pairs={{0,24},{4,28},{8,16},{12,20},{16,8},{20,12},{24,0},{28,4},{1,25},{... | collective-permute-start | bytes 196616 | tf_op jit(solution)/shard_map/ppermute | solution.py:29
  55.5 1.5 %collective-permute-start.16 = (bf16[512,256]{1,0:T(8,128)(2,1)S(1)}, bf16[512,256]{1,0:T(8,128)(2,1)S(1)}, u32[]{:S(2)}, u32[]{:S(2)}) collective-permute-start(bf16[512,256]{1,0:T(8,128)(2,1)S(1)} %collective-permute-done.10.refs_11_), channel_id=1, source_target_pairs={{0,4},{4,0},{8,12},{12,8},{16,20},{20,16},{24,28},{28,24},{1,5},{5... | collective-permute-start | bytes 786440 | tf_op jit(solution)/shard_map/ppermute | solution.py:29

commit v3 on v2

--- a/solution.py
+++ b/solution.py
@@ -15,6 +15,7 @@
 SPINS = 16
 ROWS = 16
 HALF = 128
+BLOCK = 32
 VMEM_BYTES = 20 * 2**20
 
 
@@ -75,8 +76,8 @@
                             old_r, old_i = acc[kind, hel]
                             g_r, g_i = old_r + g_r, old_i + g_i
                         acc[kind, hel] = (g_r, g_i)
-            for (kind, hel), (g_r, g_i) in acc.items():
-                store(kind, hel, col, half, (g_r, g_i))
+            for (kind, hel), both in acc.items():
+                store(kind, hel, col, half, both)
 
 
 def plane_kernel(plane, dirs, has_part, n_out, *refs):
@@ -85,57 +86,80 @@
     next_ref = refs.pop(0) if 0 in dirs else None
     u_ref, phi_ref = refs.pop(0), refs.pop(0)
     part_ref = refs.pop(0) if has_part else None
-    out_ref = refs.pop(0)
+    keep_ref = refs.pop(0) if n_out else None
     give_ref = refs.pop(0) if n_out else None
-    g_ref, h_ref, sh_ref = refs
+    sum_ref, mat_ref, one_ref, two_ref, sh_ref = refs
     n_h = phi_ref.shape[1]
     _, _, n_b, width = v_ref.shape
-    kinds = (g_ref, h_ref)
-
-    def block(step, carry):
-        row = pl.multiple_of(step * ROWS, ROWS)
-        rows = pl.ds(row, ROWS)
-        for slot, direc in enumerate(dirs):
+    bufs = (one_ref, two_ref)
+    last = n_b // BLOCK - 1
+
+    for col in range(3):
+        mat_ref[:, pl.ds(col * width, width)] = v_ref[:, col].reshape(2 * n_b, width)
+
+    def fill(which, buf):
+        for sub in range(BLOCK // ROWS):
+            rows = pl.ds(pl.multiple_of(which * BLOCK + sub * ROWS, ROWS), ROWS)
+            shifted = sh_ref.at[buf, sub]
+            for slot, direc in enumerate(dirs):
+                for part in range(2):
+                    for col in range(3):
+                        source = next_ref if direc == 0 else v_ref
+                        field = source[part, col, rows, :].astype(jnp.float32)
+                        if direc == 1:
+                            field = shift_y(field)
+                        elif direc == 2:
+                            field = shift_z(field)
+                        shifted[slot, part, col] = field
+
+            def store(kind, hel, col, half, both, sub=sub):
+                for part in range(2):
+                    row = ((kind * n_h + hel) * 2 + part) * BLOCK + sub * ROWS
+                    lanes = pl.ds(col * width + half * HALF, HALF)
+                    bufs[buf][pl.ds(row, ROWS), lanes] = both[part].astype(jnp.bfloat16)
+
+            weighted_links(u_ref, phi_ref, shifted, dirs, plane, n_h, store)
+
+    def contract(which, buf):
+        rows = pl.ds(pl.multiple_of(which * BLOCK, BLOCK), BLOCK)
+        prod = dot_nt(bufs[buf][...], mat_ref[...])
+        for kind in range(2):
+            for hel in range(n_h):
+                row = (kind * n_h + hel) * 2 * BLOCK
+                re_row, im_row = prod[row : row + BLOCK], prod[row + BLOCK : row + 2 * BLOCK]
+                real = re_row[:, :n_b] + im_row[:, n_b:]
+                if kind:
+                    imag = re_row[:, n_b:] - im_row[:, :n_b]
+                else:
+                    imag = im_row[:, :n_b] - re_row[:, n_b:]
+                for part, total in enumerate((real, imag)):
+                    if has_part:
+                        total = total + part_ref[kind, hel, part, rows, :]
+                    sum_ref[kind, hel, part, rows, :] = total
+
+    fill(0, 0)
+
+    def pair(step, carry):
+        fill(2 * step + 1, 1)
+        contract(2 * step, 0)
+        fill(2 * step + 2, 0)
+        contract(2 * step + 1, 1)
+        return carry
+
+    lax.fori_loop(0, last // 2, pair, 0)
+    fill(last, 1)
+    contract(last - 1, 0)
+    contract(last, 1)
+
+    if n_out:
+        core = lax.axis_index("space") & 1
+        for hel in range(n_h):
             for part in range(2):
-                for col in range(3):
-                    source = next_ref if direc == 0 else v_ref
-                    field = source[part, col, rows, :].astype(jnp.float32)
-                    if direc == 1:
-                        field = shift_y(field)
-                    elif direc == 2:
-                        field = shift_z(field)
-                    sh_ref[slot, part, col] = field
-
-        def store(kind, hel, col, half, both):
-            for part in range(2):
-                there = pl.ds(pl.multiple_of(part * n_b + row, ROWS), ROWS)
-                lanes = pl.ds(col * width + half * HALF, HALF)
-                kinds[kind][hel, there, lanes] = both[part].astype(jnp.bfloat16)
-
-        weighted_links(u_ref, phi_ref, sh_ref, dirs, plane, n_h, store)
-        return carry
-
-    lax.fori_loop(0, n_b // ROWS, block, 0)
-
-    def multiply(hel, carry):
-        mat = jnp.concatenate([v_ref[:, col].reshape(2 * n_b, width) for col in range(3)], 1)
-        one = dot_nt(mat, g_ref[hel])
-        two = dot_nt(h_ref[hel], mat)
-        real = one[:n_b, :n_b] + one[n_b:, n_b:] + two[:n_b, :n_b] + two[n_b:, n_b:]
-        imag = one[:n_b, n_b:] - one[n_b:, :n_b] + two[:n_b, n_b:] - two[n_b:, :n_b]
-        for part, total in enumerate((real, imag)):
-            if has_part:
-                total = total + part_ref[hel, part]
-            if n_out:
-                core = lax.axis_index("space") & 1
+                total = jnp.transpose(sum_ref[0, hel, part]) + sum_ref[1, hel, part]
                 halves = total.reshape(n_out // 2, 2, n_b // n_out, n_b)
-                out_ref[:, hel, part] = jnp.where(core == 0, halves[:, 0], halves[:, 1])
-                give_ref[:, hel, part] = jnp.where(core == 0, halves[:, 1], halves[:, 0]).astype(jnp.bfloat16)
-            else:
-                out_ref[hel, part] = total
-        return carry
-
-    lax.fori_loop(0, n_h, multiply, 0)
+                keep_ref[:, hel, part] = jnp.where(core == 0, halves[:, 0], halves[:, 1])
+                give = jnp.where(core == 0, halves[:, 1], halves[:, 0])
+                give_ref[:, hel, part] = give.astype(jnp.bfloat16)
 
 
 def plane_call(plane, dirs, vec, ahead, link, phi, part=None, n_out=0):
@@ -145,12 +169,15 @@
     args = [vec] + ([ahead] if 0 in dirs else []) + [link, phi]
     args += [part] if part is not None else []
     specs = [vmem] * len(args)
+    sums = (2, n_h, 2, n_b, n_b)
     scratch = [
-        pltpu.VMEM((n_h, 2 * n_b, 3 * width), jnp.bfloat16),
-        pltpu.VMEM((n_h, 2 * n_b, 3 * width), jnp.bfloat16),
-        pltpu.VMEM((len(dirs), 2, 3, ROWS, width), jnp.float32),
+        pltpu.VMEM((2 * n_b, 3 * width), jnp.bfloat16),
+        pltpu.VMEM((4 * n_h * BLOCK, 3 * width), jnp.bfloat16),
+        pltpu.VMEM((4 * n_h * BLOCK, 3 * width), jnp.bfloat16),
+        pltpu.VMEM((2, BLOCK // ROWS, len(dirs), 2, 3, ROWS, width), jnp.float32),
     ]
     if n_out:
+        scratch.insert(0, pltpu.VMEM(sums, jnp.float32))
         blocks = (n_out // 2, n_h, 2, n_b // n_out, n_b)
         out_shape = [
             jax.ShapeDtypeStruct(blocks, jnp.float32),
@@ -158,7 +185,7 @@
         ]
         out_specs = [vmem, vmem]
     else:
-        out_shape = jax.ShapeDtypeStruct((n_h, 2, n_b, n_b), jnp.float32)
+        out_shape = jax.ShapeDtypeStruct(sums, jnp.float32)
         out_specs = vmem
     return pl.pallas_call(
         functools.partial(plane_kernel, plane, dirs, part is not None, n_out),
@@ -338,7 +365,6 @@
     ).reshape(depth * 2, n_b)
 
     moved = lax.optimization_barrier(jnp.transpose(eigvecs[0], (3, 0, 2, 1, 4)))
-    moved, piece, both = lax.optimization_barrier((moved, piece, both))
     own_piece = from_behind(piece, "tm", n_tm - 1)
     vecs = [moved[plane] for plane in range(planes)]
     upper = from_behind(vecs[0], "space", -1)
@@ -387,7 +413,8 @@
         stage(held, size)
     early = [key for key in held if len(key) < 3]
     late = [key for key in held if len(key) >= 3]
-    packed = pack_call([held[key] for key in early])
+    early_held, swapped = hold({key: held[key] for key in early}, swapped)
+    packed = pack_call([early_held[key] for key in early])
     merged = merge_call(keep, swapped)
     got = [merged[0]] + [across(arr, "space", 2 * mask) for mask, arr in enumerate(merged[1:], 1)]
     last_held, got = hold({key: held[key] for key in late}, got)

time: 59.4 us -> 54.2 us (0.912)
  waiting for transfers between devices: 14.6 us -> 9.6 us
  Pallas kernels: 24.3 us -> 20.5 us
  starting transfers between devices: 17.3 us -> 20.7 us
    ppermute x15, waiting for transfers between devices: 14.6 us -> 9.59 us  [across(): return lax.ppermute(value, axis, pairs)]
    pallas_call x4, Pallas kernels: 20.9 us -> 17.2 us  [plane_call(): pl.pallas_call(functools.partial(plane_kernel, plane, dirs, part is not N...]
    ppermute x2, starting transfers between devices: 3.35 us -> 5.2 us  [from_behind(): return lax.ppermute(value, axis, pairs)]
    ppermute x15, starting transfers between devices: 13.9 us -> 15.5 us  [across(): return lax.ppermute(value, axis, pairs)]
  transfers between devices with their start and end apart: 17 -> 17, of which waited for: 12 -> 8; matrix products, arithmetic and copies ran while one was open for 5% -> 3% of each run, Pallas kernels for 37% -> 34%
where the time goes in v3:
time: 54.2 us; the launch traced here: 54 us
  starting transfers between devices  20.7 us (38%)
  Pallas kernels  20.5 us (38%)
  waiting for transfers between devices  9.6 us (18%)
  local copies, waits for them, and re-layouts  3 us (6%)
    pallas_call x4, Pallas kernels, plane_call(): pl.pallas_call(functools.partial(plane_kernel, plane, dirs, part is not N...  17.2 us
    ppermute x15, starting transfers between devices, across(): return lax.ppermute(value, axis, pairs)  15.5 us
    ppermute x15, waiting for transfers between devices, across(): return lax.ppermute(value, axis, pairs)  9.59 us
    ppermute x2, starting transfers between devices, from_behind(): return lax.ppermute(value, axis, pairs)  5.2 us
    unnamed x10, local copies, waits for them, and re-layouts  2.79 us
    pallas_call x1, Pallas kernels, shards(): pl.pallas_call(functools.partial(quark_kernel, masks, n_op, len(got), len...  2.26 us
  transfers between devices with their start and end apart: 17, of which 8 were waited for; matrix products, arithmetic and copies ran while one was open for 3% of the time, Pallas kernels for 34%

profile of v3, /device:TPU:0, one launch (start us, length us, event | category | flops | bytes accessed | tf_op | source)
XLA Modules:
  0.0 54.0 jit_solution(2068544329094396273)
XLA Ops:
  0.0 1.1 %dynamic-slice_bitcast_fusion = bf16[256,1,2,256]{3,2,0,1:T(2,128)(2,1)S(1)} fusion(bf16[256,16,2,256]{3,2,1,0:T(2,128)(2,1)} %bitcast.24, s32[]{:T(128)S(6)} %select_n.14), kind=kLoop, calls=%fused_computation.3 | loop fusion | bytes 524292
  1.2 4.1 %collective-permute-start = (bf16[512,256]{1,0:T(8,128)(2,1)S(1)}, bf16[512,256]{1,0:T(8,128)(2,1)S(1)}, u32[]{:S(2)}, u32[]{:S(2)}) collective-permute-start(bf16[512,256]{1,0:T(8,128)(2,1)S(1)} %reshape.10), channel_id=1, source_target_pairs={{0,2},{2,0},{1,3},{3,1},{4,6},{6,4},{5,7},{7,5},{8,10},{10,8},{9,1... | collective-permute-start | bytes 786440 | tf_op jit(solution)/shard_map/ppermute | solution.py:25
  5.3 1.6 %collective-permute-start.2 = (s32[3,2,4]{2,1,0:T(2,128)}, s32[3,2,4]{2,1,0:T(2,128)S(1)}, u32[]{:S(2)}, u32[]{:S(2)}) collective-permute-start(s32[3,2,4]{2,1,0:T(2,128)} %bitcast.17), channel_id=1, source_target_pairs={{0,1},{1,0},{2,3},{3,2},{4,5},{5,4},{6,7},{7,6},{8,9},{9,8},{10,11... | collective-permute-start | bytes 296 | tf_op jit(solution)/shard_map/ppermute | solution.py:30
  6.9 0.4 collective-permute-start.1
  7.4 1.6 %copy.11 = bf16[1,2,256,3,2,256]{5,2,3,1,4,0:T(8,128)(2,1)S(1)} copy(bf16[1,2,256,3,2,256]{5,4,3,2,1,0:T(2,128)(2,1)} %param.6) | data formatting | bytes 3145728 | tf_op args[0]
  9.1 0.1 slice_bitcast_fusion
  9.2 1.1 %collective-permute-start.9 = (bf16[2,3,256,256]{3,2,1,0:T(8,128)(2,1)S(1)}, bf16[2,3,256,256]{3,2,1,0:T(8,128)(2,1)S(1)}, u32[]{:S(2)}, u32[]{:S(2)}) collective-permute-start(bf16[2,3,256,256]{3,2,1,0:T(8,128)(2,1)S(1)} %get-tuple-element.73.refs_0_), channel_id=1, source_target_pairs={{0,28},{4,0},{8,4},{12,8},{16,12},{20,16},{24,20},{28,24},{1,29},{... | collective-permute-start | bytes 2359304 | tf_op jit(solution)/shard_map/ppermute | solution.py:25
  10.3 0.8 %collective-permute-done.1.refs_1_ = s32[2,3]{1,0:T(2,128)S(1)} collective-permute-done((s32[2,3]{1,0:T(2,128)}, s32[2,3]{1,0:T(2,128)S(1)}, u32[]{:S(2)}, u32[]{:S(2)}) %collective-permute-start.1) | collective-permute-done | bytes 56 | tf_op jit(solution)/shard_map/ppermute | solution.py:30
  11.1 0.9 %phases.1.refs_2_.refs_3_ = f32[2,2,3,2,2,256]{5,4,3,2,1,0:T(2,128)S(1)} custom-call(s32[2,3]{1,0:T(2,128)S(1)} %copy-done.1, s32[2,3]{1,0:T(2,128)S(1)} %collective-permute-done.1.refs_1_, s32[3,2,4]{2,1,0:T(2,128)S(1)} %bitcast.18, s32[3,2,4]{2,1,0:T(2,128)S(1)} %collective-permute-done.2.refs_3_, s32[4]{0:T(128)S(1)} %copy-done.2), custom_call_target="tpu_custom_call" | custom-call | tf_op jit(solution)/shard_map/phases/pallas_call | solution.py:374
  12.0 5.1 %plane0_12.1.refs_3_ = f32[2,2,2,256,256]{4,3,2,1,0:T(8,128)S(1)} custom-call(bf16[2,3,256,256]{3,2,1,0:T(8,128)(2,1)S(1)} %get-tuple-element.73.refs_0_, f32[3,3,3,2,2,256]{5,4,3,2,1,0:T(2,128)S(1)} %bitcast.19, f32[2,2,3,2,2,256]{5,4,3,2,1,0:T(2,128)S(1)} %phases.1.refs_2_.refs_3_), custom_call_target="tpu_custom_call" | custom-call | flops 3221225472 | bytes 4194304 | tf_op jit(solution)/shard_map/plane0_12/pallas_call | solution.py:190
  17.1 5.2 %plane1_12.1.refs_4_ = f32[2,2,2,256,256]{4,3,2,1,0:T(8,128)S(1)} custom-call(bf16[2,3,256,256]{3,2,1,0:T(8,128)(2,1)S(1)} %get-tuple-element.74.refs_0_.refs_1_, f32[3,3,3,2,2,256]{5,4,3,2,1,0:T(2,128)S(1)} %bitcast.20, f32[2,2,3,2,2,256]{5,4,3,2,1,0:T(2,128)S(1)} %phases.1.refs_2_.refs_3_, f32[2,2,2,256,256]{4,3,2,1,0:T(8,128)S(1)} %plane0_12.1.refs_3_), custom_call_target="tpu_custom_call" | custom-call | flops 3221225472 | bytes 4194304 | tf_op jit(solution)/shard_map/plane1_12/pallas_call | solution.py:190
  22.3 2.6 %collective-permute-start.3 = (bf16[512,256]{1,0:T(8,128)(2,1)S(1)}, bf16[512,256]{1,0:T(8,128)(2,1)S(1)}, u32[]{:S(2)}, u32[]{:S(2)}) collective-permute-start(bf16[512,256]{1,0:T(8,128)(2,1)S(1)} %collective-permute-done.refs_0_.refs_4_), channel_id=1, source_target_pairs={{0,1},{1,0},{2,3},{3,2},{4,5},{5,4},{6,7},{7,6},{8,9},{9,8},{10,11... | collective-permute-start | bytes 786440 | tf_op jit(solution)/shard_map/ppermute | solution.py:30
  24.9 1.5 %collective-permute-start.4 = (bf16[512,256]{1,0:T(8,128)(2,1)S(1)}, bf16[512,256]{1,0:T(8,128)(2,1)S(1)}, u32[]{:S(2)}, u32[]{:S(2)}) collective-permute-start(bf16[512,256]{1,0:T(8,128)(2,1)S(1)} %collective-permute-done.refs_0_.refs_4_), channel_id=1, source_target_pairs={{0,8},{4,12},{8,0},{12,4},{16,24},{20,28},{24,16},{28,20},{1,9},{5... | collective-permute-start | bytes 786440 | tf_op jit(solution)/shard_map/ppermute | solution.py:30
  26.4 1.5 %collective-permute-start.5 = (bf16[512,256]{1,0:T(8,128)(2,1)S(1)}, bf16[512,256]{1,0:T(8,128)(2,1)S(1)}, u32[]{:S(2)}, u32[]{:S(2)}) collective-permute-start(bf16[512,256]{1,0:T(8,128)(2,1)S(1)} %collective-permute-done.refs_0_.refs_4_), channel_id=1, source_target_pairs={{0,16},{4,20},{8,24},{12,28},{16,0},{20,4},{24,8},{28,12},{1,17},{... | collective-permute-start | bytes 786440 | tf_op jit(solution)/shard_map/ppermute | solution.py:30
  27.9 3.4 %plane0_0.1.refs_4_ = f32[2,2,2,256,256]{4,3,2,1,0:T(8,128)S(1)} custom-call(bf16[2,3,256,256]{3,2,1,0:T(8,128)(2,1)S(1)} %get-tuple-element.73.refs_0_, bf16[2,3,256,256]{3,2,1,0:T(8,128)(2,1)S(1)} %get-tuple-element.74.refs_0_.refs_1_, f32[3,3,3,2,2,256]{5,4,3,2,1,0:T(2,128)S(1)} %bitcast.21, f32[2,2,3,2,2,256]{5,4,3,2,1,0:T(2,128)S(1)} %phases.1.refs_2_.refs_3_, ...), custom_call_target="tpu_custom_call" | custom-call | flops 2415919104 | bytes 4194304 | tf_op jit(solution)/shard_map/plane0_0/pallas_call | solution.py:190
  31.3 0.5 collective-permute-done.4.refs_2_.refs_6_
  31.8 1.2 %collective-permute-done.5.refs_3_.refs_7_ = bf16[512,256]{1,0:T(8,128)(2,1)S(1)} collective-permute-done((bf16[512,256]{1,0:T(8,128)(2,1)S(1)}, bf16[512,256]{1,0:T(8,128)(2,1)S(1)}, u32[]{:S(2)}, u32[]{:S(2)}) %collective-permute-start.5) | collective-permute-done | bytes 262176 | tf_op jit(solution)/shard_map/ppermute | solution.py:30
  33.0 0.4 collective-permute-start.6
  33.3 1.5 %collective-permute-start.7 = (bf16[512,256]{1,0:T(8,128)(2,1)S(1)}, bf16[512,256]{1,0:T(8,128)(2,1)S(1)}, u32[]{:S(2)}, u32[]{:S(2)}) collective-permute-start(bf16[512,256]{1,0:T(8,128)(2,1)S(1)} %collective-permute-done.3.refs_1_.refs_5_), channel_id=1, source_target_pairs={{0,16},{4,20},{8,24},{12,28},{16,0},{20,4},{24,8},{28,12},{1,17},{... | collective-permute-start | bytes 786440 | tf_op jit(solution)/shard_map/ppermute | solution.py:30
  34.9 0.5 collective-permute-start.8
  35.4 3.5 %plane1_0.1 = (f32[4,2,2,32,256]{4,3,2,1,0:T(8,128)S(1)}, bf16[4,2,2,32,256]{4,3,2,1,0:T(8,128)(2,1)S(1)}) custom-call(bf16[2,3,256,256]{3,2,1,0:T(8,128)(2,1)S(1)} %get-tuple-element.74.refs_0_.refs_1_, bf16[2,3,256,256]{3,2,1,0:T(8,128)(2,1)S(1)} %collective-permute-done.9.refs_1_, f32[3,3,3,2,2,256]{5,4,3,2,1,0:T(2,128)S(1)} %bitcast.22, ...), custom_call_target="tpu_custom_call" | custom-call | flops 2415919104 | bytes 4194304 | tf_op jit(solution)/shard_map/plane1_0/pallas_call | solution.py:190
  39.0 0.4 collective-permute-done.6.refs_4_.refs_8_
  39.3 0.4 collective-permute-done.7.refs_5_.refs_9_
  39.7 1.5 %collective-permute-done.8.refs_6_.refs_10_ = bf16[512,256]{1,0:T(8,128)(2,1)S(1)} collective-permute-done((bf16[512,256]{1,0:T(8,128)(2,1)S(1)}, bf16[512,256]{1,0:T(8,128)(2,1)S(1)}, u32[]{:S(2)}, u32[]{:S(2)}) %collective-permute-start.8) | collective-permute-done | bytes 262176 | tf_op jit(solution)/shard_map/ppermute | solution.py:30
  41.2 0.1 pack_pieces.1
  41.4 1.7 %collective-permute-start.10 = (bf16[512,256]{1,0:T(8,128)(2,1)S(1)}, bf16[512,256]{1,0:T(8,128)(2,1)S(1)}, u32[]{:S(2)}, u32[]{:S(2)}) collective-permute-start(bf16[512,256]{1,0:T(8,128)(2,1)S(1)} %collective-permute-done.8.refs_6_.refs_10_), channel_id=1, source_target_pairs={{0,1},{1,0},{2,3},{3,2},{4,5},{5,4},{6,7},{7,6},{8,9},{9,8},{10,11... | collective-permute-start | bytes 786440 | tf_op jit(solution)/shard_map/ppermute | solution.py:30
  43.2 0.9 %collective-permute-start.12 = (bf16[128,256]{1,0:T(8,128)(2,1)S(1)}, bf16[128,256]{1,0:T(8,128)(2,1)S(1)}, u32[]{:S(2)}, u32[]{:S(2)}) collective-permute-start(bf16[128,256]{1,0:T(8,128)(2,1)S(1)} %get-tuple-element.58), channel_id=1, source_target_pairs={{0,8},{4,12},{8,0},{12,4},{16,24},{20,28},{24,16},{28,20},{1,9},{5... | collective-permute-start | bytes 196616 | tf_op jit(solution)/shard_map/ppermute | solution.py:30
  44.2 0.5 collective-permute-start.13
  44.7 2.1 %collective-permute-start.14 = (bf16[128,256]{1,0:T(8,128)(2,1)S(1)}, bf16[128,256]{1,0:T(8,128)(2,1)S(1)}, u32[]{:S(2)}, u32[]{:S(2)}) collective-permute-start(bf16[128,256]{1,0:T(8,128)(2,1)S(1)} %get-tuple-element.60), channel_id=1, source_target_pairs={{0,24},{4,28},{8,16},{12,20},{16,8},{20,12},{24,0},{28,4},{1,25},{... | collective-permute-start | bytes 196616 | tf_op jit(solution)/shard_map/ppermute | solution.py:30
  46.8 3.4 %collective-permute-done.10.refs_11_ = bf16[512,256]{1,0:T(8,128)(2,1)S(1)} collective-permute-done((bf16[512,256]{1,0:T(8,128)(2,1)S(1)}, bf16[512,256]{1,0:T(8,128)(2,1)S(1)}, u32[]{:S(2)}, u32[]{:S(2)}) %collective-permute-start.10) | collective-permute-done | bytes 262176 | tf_op jit(solution)/shard_map/ppermute | solution.py:30
  50.2 1.5 %collective-permute-done.16.refs_13_ = bf16[512,256]{1,0:T(8,128)(2,1)S(1)} collective-permute-done((bf16[512,256]{1,0:T(8,128)(2,1)S(1)}, bf16[512,256]{1,0:T(8,128)(2,1)S(1)}, u32[]{:S(2)}, u32[]{:S(2)}) %collective-permute-start.16) | collective-permute-done | bytes 262176 | tf_op jit(solution)/shard_map/ppermute | solution.py:30
  51.8 2.3 %quark_products.1 = f32[2,16,2,32,256]{4,3,2,1,0:T(8,128)} custom-call(f32[128,256]{1,0:T(8,128)S(1)} %get-tuple-element.61.refs_0_, bf16[128,256]{1,0:T(8,128)(2,1)S(1)} %collective-permute-done.12.refs_1_, bf16[128,256]{1,0:T(8,128)(2,1)S(1)} %collective-permute-done.13.refs_2_, bf16[128,256]{1,0:T(8,128)(2,1)S(1)} %collective-permute-done.14.refs_3_, ...), custom_call_target="tpu_custom_call" | custom-call | flops 536870912 | bytes 7340032 | tf_op jit(solution)/shard_map/quark_products/pallas_call | solution.py:432
  (22 shorter events, 0.4 us)
Async XLA Ops:
  1.2 21.1 %collective-permute-start = (bf16[512,256]{1,0:T(8,128)(2,1)S(1)}, bf16[512,256]{1,0:T(8,128)(2,1)S(1)}, u32[]{:S(2)}, u32[]{:S(2)}) collective-permute-start(bf16[512,256]{1,0:T(8,128)(2,1)S(1)} %reshape.10), channel_id=1, source_target_pairs={{0,2},{2,0},{1,3},{3,1},{4,6},{6,4},{5,7},{7,5},{8,10},{10,8},{9,1... | collective-permute-start | bytes 786440 | tf_op jit(solution)/shard_map/ppermute | solution.py:25
  5.3 5.7 %collective-permute-start.2 = (s32[3,2,4]{2,1,0:T(2,128)}, s32[3,2,4]{2,1,0:T(2,128)S(1)}, u32[]{:S(2)}, u32[]{:S(2)}) collective-permute-start(s32[3,2,4]{2,1,0:T(2,128)} %bitcast.17), channel_id=1, source_target_pairs={{0,1},{1,0},{2,3},{3,2},{4,5},{5,4},{6,7},{7,6},{8,9},{9,8},{10,11... | collective-permute-start | bytes 296 | tf_op jit(solution)/shard_map/ppermute | solution.py:30
  6.9 4.1 %collective-permute-start.1 = (s32[2,3]{1,0:T(2,128)}, s32[2,3]{1,0:T(2,128)S(1)}, u32[]{:S(2)}, u32[]{:S(2)}) collective-permute-start(s32[2,3]{1,0:T(2,128)} %refs_0_.1), channel_id=1, source_target_pairs={{0,1},{1,0},{2,3},{3,2},{4,5},{5,4},{6,7},{7,6},{8,9},{9,8},{10,11... | collective-permute-start | bytes 80 | tf_op jit(solution)/shard_map/ppermute | solution.py:30
  9.0 2.0 %copy-start = (s32[4,2,3]{0,1,2:T(2,128)S(1)}, s32[4,2,3]{0,1,2:T(2,128)}, u32[]{:S(2)}) copy-start(s32[4,2,3]{0,1,2:T(2,128)} %param.9) | copy-start | bytes 292
  9.0 2.0 %copy-start.1 = (s32[2,3]{1,0:T(2,128)S(1)}, s32[2,3]{1,0:T(2,128)}, u32[]{:S(2)}) copy-start(s32[2,3]{1,0:T(2,128)} %refs_0_.1) | copy-start | bytes 76
  9.0 2.0 %copy-start.2 = (s32[4]{0:T(128)S(1)}, s32[4]{0:T(128)}, u32[]{:S(2)}) copy-start(s32[4]{0:T(128)} %refs_4_.1) | copy-start | bytes 52
  9.1 3.0 %copy-start.3 = (f32[1,3,3,3,2,2,256]{6,5,4,3,2,1,0:T(2,128)S(1)}, f32[1,3,3,3,2,2,256]{6,5,4,3,2,1,0:T(2,128)}, u32[]{:S(2)}) copy-start(f32[1,3,3,3,2,2,256]{6,5,4,3,2,1,0:T(2,128)} %param.7) | copy-start | bytes 331780
  9.2 26.2 %collective-permute-start.9 = (bf16[2,3,256,256]{3,2,1,0:T(8,128)(2,1)S(1)}, bf16[2,3,256,256]{3,2,1,0:T(8,128)(2,1)S(1)}, u32[]{:S(2)}, u32[]{:S(2)}) collective-permute-start(bf16[2,3,256,256]{3,2,1,0:T(8,128)(2,1)S(1)} %get-tuple-element.73.refs_0_), channel_id=1, source_target_pairs={{0,28},{4,0},{8,4},{12,8},{16,12},{20,16},{24,20},{28,24},{1,29},{... | collective-permute-start | bytes 2359304 | tf_op jit(solution)/shard_map/ppermute | solution.py:25
  22.3 9.0 %collective-permute-start.3 = (bf16[512,256]{1,0:T(8,128)(2,1)S(1)}, bf16[512,256]{1,0:T(8,128)(2,1)S(1)}, u32[]{:S(2)}, u32[]{:S(2)}) collective-permute-start(bf16[512,256]{1,0:T(8,128)(2,1)S(1)} %collective-permute-done.refs_0_.refs_4_), channel_id=1, source_target_pairs={{0,1},{1,0},{2,3},{3,2},{4,5},{5,4},{6,7},{7,6},{8,9},{9,8},{10,11... | collective-permute-start | bytes 786440 | tf_op jit(solution)/shard_map/ppermute | solution.py:30
  24.9 6.9 %collective-permute-start.4 = (bf16[512,256]{1,0:T(8,128)(2,1)S(1)}, bf16[512,256]{1,0:T(8,128)(2,1)S(1)}, u32[]{:S(2)}, u32[]{:S(2)}) collective-permute-start(bf16[512,256]{1,0:T(8,128)(2,1)S(1)} %collective-permute-done.refs_0_.refs_4_), channel_id=1, source_target_pairs={{0,8},{4,12},{8,0},{12,4},{16,24},{20,28},{24,16},{28,20},{1,9},{5... | collective-permute-start | bytes 786440 | tf_op jit(solution)/shard_map/ppermute | solution.py:30
  26.4 6.6 %collective-permute-start.5 = (bf16[512,256]{1,0:T(8,128)(2,1)S(1)}, bf16[512,256]{1,0:T(8,128)(2,1)S(1)}, u32[]{:S(2)}, u32[]{:S(2)}) collective-permute-start(bf16[512,256]{1,0:T(8,128)(2,1)S(1)} %collective-permute-done.refs_0_.refs_4_), channel_id=1, source_target_pairs={{0,16},{4,20},{8,24},{12,28},{16,0},{20,4},{24,8},{28,12},{1,17},{... | collective-permute-start | bytes 786440 | tf_op jit(solution)/shard_map/ppermute | solution.py:30
  33.0 6.4 %collective-permute-start.6 = (bf16[512,256]{1,0:T(8,128)(2,1)S(1)}, bf16[512,256]{1,0:T(8,128)(2,1)S(1)}, u32[]{:S(2)}, u32[]{:S(2)}) collective-permute-start(bf16[512,256]{1,0:T(8,128)(2,1)S(1)} %collective-permute-done.4.refs_2_.refs_6_), channel_id=1, source_target_pairs={{0,1},{1,0},{2,3},{3,2},{4,5},{5,4},{6,7},{7,6},{8,9},{9,8},{10,11... | collective-permute-start | bytes 786440 | tf_op jit(solution)/shard_map/ppermute | solution.py:30
  33.3 6.4 %collective-permute-start.7 = (bf16[512,256]{1,0:T(8,128)(2,1)S(1)}, bf16[512,256]{1,0:T(8,128)(2,1)S(1)}, u32[]{:S(2)}, u32[]{:S(2)}) collective-permute-start(bf16[512,256]{1,0:T(8,128)(2,1)S(1)} %collective-permute-done.3.refs_1_.refs_5_), channel_id=1, source_target_pairs={{0,16},{4,20},{8,24},{12,28},{16,0},{20,4},{24,8},{28,12},{1,17},{... | collective-permute-start | bytes 786440 | tf_op jit(solution)/shard_map/ppermute | solution.py:30
  34.9 6.4 %collective-permute-start.8 = (bf16[512,256]{1,0:T(8,128)(2,1)S(1)}, bf16[512,256]{1,0:T(8,128)(2,1)S(1)}, u32[]{:S(2)}, u32[]{:S(2)}) collective-permute-start(bf16[512,256]{1,0:T(8,128)(2,1)S(1)} %collective-permute-done.5.refs_3_.refs_7_), channel_id=1, source_target_pairs={{0,8},{4,12},{8,0},{12,4},{16,24},{20,28},{24,16},{28,20},{1,9},{5... | collective-permute-start | bytes 786440 | tf_op jit(solution)/shard_map/ppermute | solution.py:30
  38.9 2.3 %collective-permute-start.11 = (bf16[4,2,2,32,256]{4,3,2,1,0:T(8,128)(2,1)S(1)}, bf16[4,2,2,32,256]{4,3,2,1,0:T(8,128)(2,1)S(1)}, u32[]{:S(2)}, u32[]{:S(2)}) collective-permute-start(bf16[4,2,2,32,256]{4,3,2,1,0:T(8,128)(2,1)S(1)} %get-tuple-element.55), channel_id=1, source_target_pairs={{0,4},{4,0},{8,12},{12,8},{16,20},{20,16},{24,28},{28,24},{1,5},{5... | collective-permute-start | bytes 786440 | tf_op jit(solution)/shard_map/ppermute | solution.py:30
  41.4 10.4 %collective-permute-start.15 = (bf16[7,512,256]{2,1,0:T(8,128)(2,1)S(1)}, bf16[7,512,256]{2,1,0:T(8,128)(2,1)S(1)}, u32[]{:S(2)}, u32[]{:S(2)}) collective-permute-start(bf16[7,512,256]{2,1,0:T(8,128)(2,1)S(1)} %pack_pieces.1), channel_id=1, source_target_pairs={{0,4},{4,0},{8,12},{12,8},{16,20},{20,16},{24,28},{28,24},{1,5},{5... | collective-permute-start | bytes 5505032 | tf_op jit(solution)/shard_map/ppermute | solution.py:30
  41.4 8.7 %collective-permute-start.10 = (bf16[512,256]{1,0:T(8,128)(2,1)S(1)}, bf16[512,256]{1,0:T(8,128)(2,1)S(1)}, u32[]{:S(2)}, u32[]{:S(2)}) collective-permute-start(bf16[512,256]{1,0:T(8,128)(2,1)S(1)} %collective-permute-done.8.refs_6_.refs_10_), channel_id=1, source_target_pairs={{0,1},{1,0},{2,3},{3,2},{4,5},{5,4},{6,7},{7,6},{8,9},{9,8},{10,11... | collective-permute-start | bytes 786440 | tf_op jit(solution)/shard_map/ppermute | solution.py:30
  43.2 6.9 %collective-permute-start.12 = (bf16[128,256]{1,0:T(8,128)(2,1)S(1)}, bf16[128,256]{1,0:T(8,128)(2,1)S(1)}, u32[]{:S(2)}, u32[]{:S(2)}) collective-permute-start(bf16[128,256]{1,0:T(8,128)(2,1)S(1)} %get-tuple-element.58), channel_id=1, source_target_pairs={{0,8},{4,12},{8,0},{12,4},{16,24},{20,28},{24,16},{28,20},{1,9},{5... | collective-permute-start | bytes 196616 | tf_op jit(solution)/shard_map/ppermute | solution.py:30
  44.2 6.0 %collective-permute-start.13 = (bf16[128,256]{1,0:T(8,128)(2,1)S(1)}, bf16[128,256]{1,0:T(8,128)(2,1)S(1)}, u32[]{:S(2)}, u32[]{:S(2)}) collective-permute-start(bf16[128,256]{1,0:T(8,128)(2,1)S(1)} %get-tuple-element.59), channel_id=1, source_target_pairs={{0,16},{4,20},{8,24},{12,28},{16,0},{20,4},{24,8},{28,12},{1,17},{... | collective-permute-start | bytes 196616 | tf_op jit(solution)/shard_map/ppermute | solution.py:30
  44.7 5.5 %collective-permute-start.14 = (bf16[128,256]{1,0:T(8,128)(2,1)S(1)}, bf16[128,256]{1,0:T(8,128)(2,1)S(1)}, u32[]{:S(2)}, u32[]{:S(2)}) collective-permute-start(bf16[128,256]{1,0:T(8,128)(2,1)S(1)} %get-tuple-element.60), channel_id=1, source_target_pairs={{0,24},{4,28},{8,16},{12,20},{16,8},{20,12},{24,0},{28,4},{1,25},{... | collective-permute-start | bytes 196616 | tf_op jit(solution)/shard_map/ppermute | solution.py:30
  50.2 1.6 %collective-permute-start.16 = (bf16[512,256]{1,0:T(8,128)(2,1)S(1)}, bf16[512,256]{1,0:T(8,128)(2,1)S(1)}, u32[]{:S(2)}, u32[]{:S(2)}) collective-permute-start(bf16[512,256]{1,0:T(8,128)(2,1)S(1)} %collective-permute-done.10.refs_11_), channel_id=1, source_target_pairs={{0,4},{4,0},{8,12},{12,8},{16,20},{20,16},{24,28},{28,24},{1,5},{5... | collective-permute-start | bytes 786440 | tf_op jit(solution)/shard_map/ppermute | solution.py:30

commit v4 on v3

--- a/solution.py
+++ b/solution.py
@@ -28,6 +28,15 @@
 def across(value, axis, mask):
     pairs = [(source, source ^ mask) for source in range(lax.axis_size(axis))]
     return lax.ppermute(value, axis, pairs)
+
+
+def diagonal(value, n_space, n_op):
+    pairs = []
+    for space in range(n_space):
+        for oper in range(n_op):
+            target = (space ^ (n_space - 2)) * n_op + (oper ^ (n_op - 1))
+            pairs.append((space * n_op + oper, target))
+    return lax.ppermute(value, ("space", "op"), pairs)
 
 
 def dot_nt(left, right):
@@ -195,8 +204,8 @@
         scratch_shapes=scratch,
         compiler_params=pltpu.CompilerParams(vmem_limit_bytes=VMEM_BYTES),
         cost_estimate=pl.CostEstimate(
-            flops=(16 + 8 * len(dirs)) * n_h * n_b * n_b * 3 * width,
-            bytes_accessed=2**22,
+            flops=2**34,
+            bytes_accessed=2**28,
             transcendentals=0,
         ),
         name="plane%d_%s" % (plane, "".join(str(direc) for direc in dirs)),
@@ -397,30 +406,30 @@
 
     link = links[0]
     last = planes - 1
-    partial = None
-    for plane in range(planes):
-        partial = plane_call(plane, (1, 2), vecs[plane], None, link, phi, partial)
+    corner = tuple(range(len(dims)))
+    partial = plane_call(last, (1, 2), vecs[last], None, link, phi)
     held, partial = hold({(): own_piece}, partial)
     stage(held, 1)
+    if len(dims) > 2:
+        far = diagonal(held[()], n_space, n_op)
     for plane in range(last):
-        partial = plane_call(plane, (0,), vecs[plane], vecs[plane + 1], link, phi, partial)
+        partial = plane_call(plane, (1, 2, 0), vecs[plane], vecs[plane + 1], link, phi, partial)
     held, partial = hold(held, partial)
-    stage(held, 2)
+    early = list(held)
+    flipped = [across(pack_call([held[key] for key in early]), "space", 1)]
+    for size in range(2, max(3, len(dims))):
+        stage(held, size)
+    if len(dims) > 2:
+        held[corner] = far
+    late = [key for key in held if key not in early]
     keep, give = plane_call(last, (0,), vecs[last], upper, link, phi, partial, n_space)
     swapped = across(give, "space", 1)
-    held, keep = hold(held, keep)
-    for size in range(3, len(dims) + 1):
-        stage(held, size)
-    early = [key for key in held if len(key) < 3]
-    late = [key for key in held if len(key) >= 3]
-    early_held, swapped = hold({key: held[key] for key in early}, swapped)
-    packed = pack_call([early_held[key] for key in early])
     merged = merge_call(keep, swapped)
+    after, swapped = hold({key: held[key] for key in late}, swapped)
+    held.update(after)
+    flipped.append(across(pack_call([held[key] for key in late]), "space", 1))
     got = [merged[0]] + [across(arr, "space", 2 * mask) for mask, arr in enumerate(merged[1:], 1)]
-    last_held, got = hold({key: held[key] for key in late}, got)
-    held.update(last_held)
-    tau = [held[key] for key in early + late]
-    tau += [across(packed, "space", 1)] + [across(held[key], "space", 1) for key in late]
+    tau = [held[key] for key in early + late] + flipped
     masks = []
     for flip in range(2):
         for group_dims in early + late:

time: 54.2 us -> 52.4 us (0.967)
  Pallas kernels: 20.5 us -> 18.8 us
    pallas_call x4 -> x3, Pallas kernels: 17.2 us -> 15.4 us  [plane_call(): pl.pallas_call(functools.partial(plane_kernel, plane, dirs, part is not N...]
    ppermute x15 -> x14, waiting for transfers between devices: 9.59 us -> 9.27 us  [across(): return lax.ppermute(value, axis, pairs)]
    ppermute x15 -> x14, starting transfers between devices: 15.5 us -> 15.6 us  [across(): return lax.ppermute(value, axis, pairs)]
  transfers between devices with their start and end apart: 17 -> 17, of which waited for: 8 -> 8; matrix products, arithmetic and copies ran while one was open for 3% -> 3% of each run, Pallas kernels for 34% -> 32%
where the time goes in v4:
time: 52.4 us; the launch traced here: 52.2 us
  starting transfers between devices  20.8 us (40%)
  Pallas kernels  18.8 us (36%)
  waiting for transfers between devices  9.42 us (18%)
  local copies, waits for them, and re-layouts  3 us (6%)
    ppermute x14, starting transfers between devices, across(): return lax.ppermute(value, axis, pairs)  15.6 us
    pallas_call x3, Pallas kernels, plane_call(): pl.pallas_call(functools.partial(plane_kernel, plane, dirs, part is not N...  15.4 us
    ppermute x14, waiting for transfers between devices, across(): return lax.ppermute(value, axis, pairs)  9.27 us
    ppermute x2, starting transfers between devices, from_behind(): return lax.ppermute(value, axis, pairs)  5.2 us
    unnamed x10, local copies, waits for them, and re-layouts  2.79 us
    pallas_call x1, Pallas kernels, shards(): pl.pallas_call(functools.partial(quark_kernel, masks, n_op, len(got), len...  2.26 us
  transfers between devices with their start and end apart: 17, of which 8 were waited for; matrix products, arithmetic and copies ran while one was open for 3% of the time, Pallas kernels for 32%

profile of v4, /device:TPU:0, one launch (start us, length us, event | category | flops | bytes accessed | tf_op | source)
XLA Modules:
  0.0 52.2 jit_solution(5020824667024674566)
XLA Ops:
  0.0 1.1 %dynamic-slice_bitcast_fusion = bf16[256,1,2,256]{3,2,0,1:T(2,128)(2,1)S(1)} fusion(bf16[256,16,2,256]{3,2,1,0:T(2,128)(2,1)} %bitcast.23, s32[]{:T(128)S(6)} %select_n.14), kind=kLoop, calls=%fused_computation.3 | loop fusion | bytes 524292
  1.1 0.1 reshape.10
  1.2 4.1 %collective-permute-start.3 = (bf16[512,256]{1,0:T(8,128)(2,1)S(1)}, bf16[512,256]{1,0:T(8,128)(2,1)S(1)}, u32[]{:S(2)}, u32[]{:S(2)}) collective-permute-start(bf16[512,256]{1,0:T(8,128)(2,1)S(1)} %reshape.10), channel_id=1, source_target_pairs={{0,2},{2,0},{1,3},{3,1},{4,6},{6,4},{5,7},{7,5},{8,10},{10,8},{9,1... | collective-permute-start | bytes 786440 | tf_op jit(solution)/shard_map/ppermute | solution.py:25
  5.3 1.6 %collective-permute-start.2 = (s32[3,2,4]{2,1,0:T(2,128)}, s32[3,2,4]{2,1,0:T(2,128)S(1)}, u32[]{:S(2)}, u32[]{:S(2)}) collective-permute-start(s32[3,2,4]{2,1,0:T(2,128)} %bitcast.17), channel_id=1, source_target_pairs={{0,1},{1,0},{2,3},{3,2},{4,5},{5,4},{6,7},{7,6},{8,9},{9,8},{10,11... | collective-permute-start | bytes 296 | tf_op jit(solution)/shard_map/ppermute | solution.py:30
  6.9 0.4 collective-permute-start.1
  7.4 1.6 %copy.11 = bf16[1,2,256,3,2,256]{5,2,3,1,4,0:T(8,128)(2,1)S(1)} copy(bf16[1,2,256,3,2,256]{5,4,3,2,1,0:T(2,128)(2,1)} %param.6) | data formatting | bytes 3145728 | tf_op args[0]
  9.1 0.1 slice_bitcast_fusion
  9.2 1.1 %collective-permute-start = (bf16[2,3,256,256]{3,2,1,0:T(8,128)(2,1)S(1)}, bf16[2,3,256,256]{3,2,1,0:T(8,128)(2,1)S(1)}, u32[]{:S(2)}, u32[]{:S(2)}) collective-permute-start(bf16[2,3,256,256]{3,2,1,0:T(8,128)(2,1)S(1)} %get-tuple-element.39.refs_0_), channel_id=1, source_target_pairs={{0,28},{4,0},{8,4},{12,8},{16,12},{20,16},{24,20},{28,24},{1,29},{... | collective-permute-start | bytes 2359304 | tf_op jit(solution)/shard_map/ppermute | solution.py:25
  10.3 0.8 %collective-permute-done.1.refs_1_ = s32[2,3]{1,0:T(2,128)S(1)} collective-permute-done((s32[2,3]{1,0:T(2,128)}, s32[2,3]{1,0:T(2,128)S(1)}, u32[]{:S(2)}, u32[]{:S(2)}) %collective-permute-start.1) | collective-permute-done | bytes 56 | tf_op jit(solution)/shard_map/ppermute | solution.py:30
  11.1 0.9 %phases.1.refs_2_.refs_3_ = f32[2,2,3,2,2,256]{5,4,3,2,1,0:T(2,128)S(1)} custom-call(s32[2,3]{1,0:T(2,128)S(1)} %copy-done.1, s32[2,3]{1,0:T(2,128)S(1)} %collective-permute-done.1.refs_1_, s32[3,2,4]{2,1,0:T(2,128)S(1)} %bitcast.18, s32[3,2,4]{2,1,0:T(2,128)S(1)} %collective-permute-done.2.refs_3_, s32[4]{0:T(128)S(1)} %copy-done.2), custom_call_target="tpu_custom_call" | custom-call | tf_op jit(solution)/shard_map/phases/pallas_call | solution.py:383
  12.0 5.1 %plane1_12.1.refs_4_ = f32[2,2,2,256,256]{4,3,2,1,0:T(8,128)S(1)} custom-call(bf16[2,3,256,256]{3,2,1,0:T(8,128)(2,1)S(1)} %get-tuple-element.40.refs_0_.refs_1_, f32[3,3,3,2,2,256]{5,4,3,2,1,0:T(2,128)S(1)} %bitcast.19, f32[2,2,3,2,2,256]{5,4,3,2,1,0:T(2,128)S(1)} %phases.1.refs_2_.refs_3_), custom_call_target="tpu_custom_call" | custom-call | flops 17179869184 | bytes 268435456 | tf_op jit(solution)/shard_map/plane1_12/pallas_call | solution.py:199
  17.1 0.1 collective-permute-done.3.refs_0_.refs_4_
  17.3 2.4 %collective-permute-start.4 = (bf16[512,256]{1,0:T(8,128)(2,1)S(1)}, bf16[512,256]{1,0:T(8,128)(2,1)S(1)}, u32[]{:S(2)}, u32[]{:S(2)}) collective-permute-start(bf16[512,256]{1,0:T(8,128)(2,1)S(1)} %collective-permute-done.3.refs_0_.refs_4_), channel_id=1, source_target_pairs={{0,1},{1,0},{2,3},{3,2},{4,5},{5,4},{6,7},{7,6},{8,9},{9,8},{10,11... | collective-permute-start | bytes 786440 | tf_op jit(solution)/shard_map/ppermute | solution.py:30
  19.7 1.5 %collective-permute-start.5 = (bf16[512,256]{1,0:T(8,128)(2,1)S(1)}, bf16[512,256]{1,0:T(8,128)(2,1)S(1)}, u32[]{:S(2)}, u32[]{:S(2)}) collective-permute-start(bf16[512,256]{1,0:T(8,128)(2,1)S(1)} %collective-permute-done.3.refs_0_.refs_4_), channel_id=1, source_target_pairs={{0,8},{4,12},{8,0},{12,4},{16,24},{20,28},{24,16},{28,20},{1,9},{5... | collective-permute-start | bytes 786440 | tf_op jit(solution)/shard_map/ppermute | solution.py:30
  21.2 1.5 %collective-permute-start.6 = (bf16[512,256]{1,0:T(8,128)(2,1)S(1)}, bf16[512,256]{1,0:T(8,128)(2,1)S(1)}, u32[]{:S(2)}, u32[]{:S(2)}) collective-permute-start(bf16[512,256]{1,0:T(8,128)(2,1)S(1)} %collective-permute-done.3.refs_0_.refs_4_), channel_id=1, source_target_pairs={{0,16},{4,20},{8,24},{12,28},{16,0},{20,4},{24,8},{28,12},{1,17},{... | collective-permute-start | bytes 786440 | tf_op jit(solution)/shard_map/ppermute | solution.py:30
  22.7 6.8 %plane0_120.1.refs_4_ = f32[2,2,2,256,256]{4,3,2,1,0:T(8,128)S(1)} custom-call(bf16[2,3,256,256]{3,2,1,0:T(8,128)(2,1)S(1)} %get-tuple-element.39.refs_0_, bf16[2,3,256,256]{3,2,1,0:T(8,128)(2,1)S(1)} %get-tuple-element.40.refs_0_.refs_1_, f32[3,3,3,2,2,256]{5,4,3,2,1,0:T(2,128)S(1)} %bitcast.20, f32[2,2,3,2,2,256]{5,4,3,2,1,0:T(2,128)S(1)} %phases.1.refs_2_.refs_3_, ...), custom_call_target="tpu_custom_call" | custom-call | flops 17179869184 | bytes 268435456 | tf_op jit(solution)/shard_map/plane0_120/pallas_call | solution.py:199
  29.5 2.7 %collective-permute-done.5.refs_2_.refs_6_ = bf16[512,256]{1,0:T(8,128)(2,1)S(1)} collective-permute-done((bf16[512,256]{1,0:T(8,128)(2,1)S(1)}, bf16[512,256]{1,0:T(8,128)(2,1)S(1)}, u32[]{:S(2)}, u32[]{:S(2)}) %collective-permute-start.5) | collective-permute-done | bytes 262176 | tf_op jit(solution)/shard_map/ppermute | solution.py:30
  32.2 1.8 %collective-permute-done.6.refs_3_.refs_7_ = bf16[512,256]{1,0:T(8,128)(2,1)S(1)} collective-permute-done((bf16[512,256]{1,0:T(8,128)(2,1)S(1)}, bf16[512,256]{1,0:T(8,128)(2,1)S(1)}, u32[]{:S(2)}, u32[]{:S(2)}) %collective-permute-start.6) | collective-permute-done | bytes 262176 | tf_op jit(solution)/shard_map/ppermute | solution.py:30
  34.0 2.4 %collective-permute-start.12 = (bf16[512,256]{1,0:T(8,128)(2,1)S(1)}, bf16[512,256]{1,0:T(8,128)(2,1)S(1)}, u32[]{:S(2)}, u32[]{:S(2)}) collective-permute-start(bf16[512,256]{1,0:T(8,128)(2,1)S(1)} %collective-permute-done.4.refs_1_.refs_5_), channel_id=1, source_target_pairs={{0,16},{4,20},{8,24},{12,28},{16,0},{20,4},{24,8},{28,12},{1,17},{... | collective-permute-start | bytes 786440 | tf_op jit(solution)/shard_map/ppermute | solution.py:30
  36.4 1.3 %collective-permute-start.13 = (bf16[512,256]{1,0:T(8,128)(2,1)S(1)}, bf16[512,256]{1,0:T(8,128)(2,1)S(1)}, u32[]{:S(2)}, u32[]{:S(2)}) collective-permute-start(bf16[512,256]{1,0:T(8,128)(2,1)S(1)} %collective-permute-done.6.refs_3_.refs_7_), channel_id=1, source_target_pairs={{0,8},{4,12},{8,0},{12,4},{16,24},{20,28},{24,16},{28,20},{1,9},{5... | collective-permute-start | bytes 786440 | tf_op jit(solution)/shard_map/ppermute | solution.py:30
  37.7 3.5 %plane1_0.1 = (f32[4,2,2,32,256]{4,3,2,1,0:T(8,128)S(1)}, bf16[4,2,2,32,256]{4,3,2,1,0:T(8,128)(2,1)S(1)}) custom-call(bf16[2,3,256,256]{3,2,1,0:T(8,128)(2,1)S(1)} %get-tuple-element.40.refs_0_.refs_1_, bf16[2,3,256,256]{3,2,1,0:T(8,128)(2,1)S(1)} %collective-permute-done.refs_1_, f32[3,3,3,2,2,256]{5,4,3,2,1,0:T(2,128)S(1)} %bitcast.21, ...), custom_call_target="tpu_custom_call" | custom-call | flops 17179869184 | bytes 268435456 | tf_op jit(solution)/shard_map/plane1_0/pallas_call | solution.py:199
  41.3 0.1 collective-permute-start.7
  41.4 0.6 %collective-permute-start.15 = (bf16[4,512,256]{2,1,0:T(8,128)(2,1)S(1)}, bf16[4,512,256]{2,1,0:T(8,128)(2,1)S(1)}, u32[]{:S(2)}, u32[]{:S(2)}) collective-permute-start(bf16[4,512,256]{2,1,0:T(8,128)(2,1)S(1)} %pack_pieces.2), channel_id=1, source_target_pairs={{0,4},{4,0},{8,12},{12,8},{16,20},{20,16},{24,28},{28,24},{1,5},{5... | collective-permute-start | bytes 3145736 | tf_op jit(solution)/shard_map/ppermute | solution.py:30
  42.0 0.8 %collective-permute-done.13.refs_2_.refs_10_ = bf16[512,256]{1,0:T(8,128)(2,1)S(1)} collective-permute-done((bf16[512,256]{1,0:T(8,128)(2,1)S(1)}, bf16[512,256]{1,0:T(8,128)(2,1)S(1)}, u32[]{:S(2)}, u32[]{:S(2)}) %collective-permute-start.13) | collective-permute-done | bytes 262176 | tf_op jit(solution)/shard_map/ppermute | solution.py:30
  42.8 0.1 collective-permute-done.7.got_ref
  42.9 0.2 collective-permute-start.16
  43.2 0.6 %collective-permute-start.10 = (bf16[128,256]{1,0:T(8,128)(2,1)S(1)}, bf16[128,256]{1,0:T(8,128)(2,1)S(1)}, u32[]{:S(2)}, u32[]{:S(2)}) collective-permute-start(bf16[128,256]{1,0:T(8,128)(2,1)S(1)} %get-tuple-element.30), channel_id=1, source_target_pairs={{0,24},{4,28},{8,16},{12,20},{16,8},{20,12},{24,0},{28,4},{1,25},{... | collective-permute-start | bytes 196616 | tf_op jit(solution)/shard_map/ppermute | solution.py:30
  43.8 0.9 %collective-permute-start.8 = (bf16[128,256]{1,0:T(8,128)(2,1)S(1)}, bf16[128,256]{1,0:T(8,128)(2,1)S(1)}, u32[]{:S(2)}, u32[]{:S(2)}) collective-permute-start(bf16[128,256]{1,0:T(8,128)(2,1)S(1)} %get-tuple-element.28), channel_id=1, source_target_pairs={{0,8},{4,12},{8,0},{12,4},{16,24},{20,28},{24,16},{28,20},{1,9},{5... | collective-permute-start | bytes 196616 | tf_op jit(solution)/shard_map/ppermute | solution.py:30
  44.8 2.0 %collective-permute-start.9 = (bf16[128,256]{1,0:T(8,128)(2,1)S(1)}, bf16[128,256]{1,0:T(8,128)(2,1)S(1)}, u32[]{:S(2)}, u32[]{:S(2)}) collective-permute-start(bf16[128,256]{1,0:T(8,128)(2,1)S(1)} %get-tuple-element.29), channel_id=1, source_target_pairs={{0,16},{4,20},{8,24},{12,28},{16,0},{20,4},{24,8},{28,12},{1,17},{... | collective-permute-start | bytes 196616 | tf_op jit(solution)/shard_map/ppermute | solution.py:30
  46.8 2.2 %collective-permute-done.10.refs_3_ = bf16[128,256]{1,0:T(8,128)(2,1)S(1)} collective-permute-done((bf16[128,256]{1,0:T(8,128)(2,1)S(1)}, bf16[128,256]{1,0:T(8,128)(2,1)S(1)}, u32[]{:S(2)}, u32[]{:S(2)}) %collective-permute-start.10) | collective-permute-done | bytes 65568 | tf_op jit(solution)/shard_map/ppermute | solution.py:30
  49.0 1.0 %collective-permute-done.9.refs_2_ = bf16[128,256]{1,0:T(8,128)(2,1)S(1)} collective-permute-done((bf16[128,256]{1,0:T(8,128)(2,1)S(1)}, bf16[128,256]{1,0:T(8,128)(2,1)S(1)}, u32[]{:S(2)}, u32[]{:S(2)}) %collective-permute-start.9) | collective-permute-done | bytes 65568 | tf_op jit(solution)/shard_map/ppermute | solution.py:30
  50.0 2.3 %quark_products.1 = f32[2,16,2,32,256]{4,3,2,1,0:T(8,128)} custom-call(f32[128,256]{1,0:T(8,128)S(1)} %get-tuple-element.27.refs_0_, bf16[128,256]{1,0:T(8,128)(2,1)S(1)} %collective-permute-done.8.refs_1_, bf16[128,256]{1,0:T(8,128)(2,1)S(1)} %collective-permute-done.9.refs_2_, bf16[128,256]{1,0:T(8,128)(2,1)S(1)} %collective-permute-done.10.refs_3_, ...), custom_call_target="tpu_custom_call" | custom-call | flops 536870912 | bytes 7340032 | tf_op jit(solution)/shard_map/quark_products/pallas_call | solution.py:441
  (22 shorter events, 0.3 us)
Async XLA Ops:
  1.2 16.0 %collective-permute-start.3 = (bf16[512,256]{1,0:T(8,128)(2,1)S(1)}, bf16[512,256]{1,0:T(8,128)(2,1)S(1)}, u32[]{:S(2)}, u32[]{:S(2)}) collective-permute-start(bf16[512,256]{1,0:T(8,128)(2,1)S(1)} %reshape.10), channel_id=1, source_target_pairs={{0,2},{2,0},{1,3},{3,1},{4,6},{6,4},{5,7},{7,5},{8,10},{10,8},{9,1... | collective-permute-start | bytes 786440 | tf_op jit(solution)/shard_map/ppermute | solution.py:25
  5.3 5.7 %collective-permute-start.2 = (s32[3,2,4]{2,1,0:T(2,128)}, s32[3,2,4]{2,1,0:T(2,128)S(1)}, u32[]{:S(2)}, u32[]{:S(2)}) collective-permute-start(s32[3,2,4]{2,1,0:T(2,128)} %bitcast.17), channel_id=1, source_target_pairs={{0,1},{1,0},{2,3},{3,2},{4,5},{5,4},{6,7},{7,6},{8,9},{9,8},{10,11... | collective-permute-start | bytes 296 | tf_op jit(solution)/shard_map/ppermute | solution.py:30
  6.9 4.1 %collective-permute-start.1 = (s32[2,3]{1,0:T(2,128)}, s32[2,3]{1,0:T(2,128)S(1)}, u32[]{:S(2)}, u32[]{:S(2)}) collective-permute-start(s32[2,3]{1,0:T(2,128)} %refs_0_.1), channel_id=1, source_target_pairs={{0,1},{1,0},{2,3},{3,2},{4,5},{5,4},{6,7},{7,6},{8,9},{9,8},{10,11... | collective-permute-start | bytes 80 | tf_op jit(solution)/shard_map/ppermute | solution.py:30
  9.0 2.0 %copy-start = (s32[4,2,3]{0,1,2:T(2,128)S(1)}, s32[4,2,3]{0,1,2:T(2,128)}, u32[]{:S(2)}) copy-start(s32[4,2,3]{0,1,2:T(2,128)} %param.9) | copy-start | bytes 292
  9.0 2.0 %copy-start.1 = (s32[2,3]{1,0:T(2,128)S(1)}, s32[2,3]{1,0:T(2,128)}, u32[]{:S(2)}) copy-start(s32[2,3]{1,0:T(2,128)} %refs_0_.1) | copy-start | bytes 76
  9.0 2.0 %copy-start.2 = (s32[4]{0:T(128)S(1)}, s32[4]{0:T(128)}, u32[]{:S(2)}) copy-start(s32[4]{0:T(128)} %refs_4_.1) | copy-start | bytes 52
  9.1 3.0 %copy-start.3 = (f32[1,3,3,3,2,2,256]{6,5,4,3,2,1,0:T(2,128)S(1)}, f32[1,3,3,3,2,2,256]{6,5,4,3,2,1,0:T(2,128)}, u32[]{:S(2)}) copy-start(f32[1,3,3,3,2,2,256]{6,5,4,3,2,1,0:T(2,128)} %param.7) | copy-start | bytes 331780
  9.2 28.5 %collective-permute-start = (bf16[2,3,256,256]{3,2,1,0:T(8,128)(2,1)S(1)}, bf16[2,3,256,256]{3,2,1,0:T(8,128)(2,1)S(1)}, u32[]{:S(2)}, u32[]{:S(2)}) collective-permute-start(bf16[2,3,256,256]{3,2,1,0:T(8,128)(2,1)S(1)} %get-tuple-element.39.refs_0_), channel_id=1, source_target_pairs={{0,28},{4,0},{8,4},{12,8},{16,12},{20,16},{24,20},{28,24},{1,29},{... | collective-permute-start | bytes 2359304 | tf_op jit(solution)/shard_map/ppermute | solution.py:25
  17.3 12.2 %collective-permute-start.4 = (bf16[512,256]{1,0:T(8,128)(2,1)S(1)}, bf16[512,256]{1,0:T(8,128)(2,1)S(1)}, u32[]{:S(2)}, u32[]{:S(2)}) collective-permute-start(bf16[512,256]{1,0:T(8,128)(2,1)S(1)} %collective-permute-done.3.refs_0_.refs_4_), channel_id=1, source_target_pairs={{0,1},{1,0},{2,3},{3,2},{4,5},{5,4},{6,7},{7,6},{8,9},{9,8},{10,11... | collective-permute-start | bytes 786440 | tf_op jit(solution)/shard_map/ppermute | solution.py:30
  19.7 12.5 %collective-permute-start.5 = (bf16[512,256]{1,0:T(8,128)(2,1)S(1)}, bf16[512,256]{1,0:T(8,128)(2,1)S(1)}, u32[]{:S(2)}, u32[]{:S(2)}) collective-permute-start(bf16[512,256]{1,0:T(8,128)(2,1)S(1)} %collective-permute-done.3.refs_0_.refs_4_), channel_id=1, source_target_pairs={{0,8},{4,12},{8,0},{12,4},{16,24},{20,28},{24,16},{28,20},{1,9},{5... | collective-permute-start | bytes 786440 | tf_op jit(solution)/shard_map/ppermute | solution.py:30
  21.2 12.8 %collective-permute-start.6 = (bf16[512,256]{1,0:T(8,128)(2,1)S(1)}, bf16[512,256]{1,0:T(8,128)(2,1)S(1)}, u32[]{:S(2)}, u32[]{:S(2)}) collective-permute-start(bf16[512,256]{1,0:T(8,128)(2,1)S(1)} %collective-permute-done.3.refs_0_.refs_4_), channel_id=1, source_target_pairs={{0,16},{4,20},{8,24},{12,28},{16,0},{20,4},{24,8},{28,12},{1,17},{... | collective-permute-start | bytes 786440 | tf_op jit(solution)/shard_map/ppermute | solution.py:30
  22.7 18.7 %collective-permute-start.14 = (bf16[512,256]{1,0:T(8,128)(2,1)S(1)}, bf16[512,256]{1,0:T(8,128)(2,1)S(1)}, u32[]{:S(2)}, u32[]{:S(2)}) collective-permute-start(bf16[512,256]{1,0:T(8,128)(2,1)S(1)} %collective-permute-done.3.refs_0_.refs_4_), channel_id=1, source_target_pairs={{0,25},{1,24},{4,29},{5,28},{8,17},{9,16},{12,21},{13,20},{16,9},{... | collective-permute-start | bytes 786440 | tf_op jit(solution)/shard_map/ppermute | solution.py:39
  34.0 8.0 %collective-permute-start.11 = (bf16[512,256]{1,0:T(8,128)(2,1)S(1)}, bf16[512,256]{1,0:T(8,128)(2,1)S(1)}, u32[]{:S(2)}, u32[]{:S(2)}) collective-permute-start(bf16[512,256]{1,0:T(8,128)(2,1)S(1)} %collective-permute-done.5.refs_2_.refs_6_), channel_id=1, source_target_pairs={{0,1},{1,0},{2,3},{3,2},{4,5},{5,4},{6,7},{7,6},{8,9},{9,8},{10,11... | collective-permute-start | bytes 786440 | tf_op jit(solution)/shard_map/ppermute | solution.py:30
  34.0 8.0 %collective-permute-start.12 = (bf16[512,256]{1,0:T(8,128)(2,1)S(1)}, bf16[512,256]{1,0:T(8,128)(2,1)S(1)}, u32[]{:S(2)}, u32[]{:S(2)}) collective-permute-start(bf16[512,256]{1,0:T(8,128)(2,1)S(1)} %collective-permute-done.4.refs_1_.refs_5_), channel_id=1, source_target_pairs={{0,16},{4,20},{8,24},{12,28},{16,0},{20,4},{24,8},{28,12},{1,17},{... | collective-permute-start | bytes 786440 | tf_op jit(solution)/shard_map/ppermute | solution.py:30
  36.4 6.4 %collective-permute-start.13 = (bf16[512,256]{1,0:T(8,128)(2,1)S(1)}, bf16[512,256]{1,0:T(8,128)(2,1)S(1)}, u32[]{:S(2)}, u32[]{:S(2)}) collective-permute-start(bf16[512,256]{1,0:T(8,128)(2,1)S(1)} %collective-permute-done.6.refs_3_.refs_7_), channel_id=1, source_target_pairs={{0,8},{4,12},{8,0},{12,4},{16,24},{20,28},{24,16},{28,20},{1,9},{5... | collective-permute-start | bytes 786440 | tf_op jit(solution)/shard_map/ppermute | solution.py:30
  41.3 1.6 %collective-permute-start.7 = (bf16[4,2,2,32,256]{4,3,2,1,0:T(8,128)(2,1)S(1)}, bf16[4,2,2,32,256]{4,3,2,1,0:T(8,128)(2,1)S(1)}, u32[]{:S(2)}, u32[]{:S(2)}) collective-permute-start(bf16[4,2,2,32,256]{4,3,2,1,0:T(8,128)(2,1)S(1)} %get-tuple-element.26), channel_id=1, source_target_pairs={{0,4},{4,0},{8,12},{12,8},{16,20},{20,16},{24,28},{28,24},{1,5},{5... | collective-permute-start | bytes 786440 | tf_op jit(solution)/shard_map/ppermute | solution.py:30
  41.4 8.5 %collective-permute-start.15 = (bf16[4,512,256]{2,1,0:T(8,128)(2,1)S(1)}, bf16[4,512,256]{2,1,0:T(8,128)(2,1)S(1)}, u32[]{:S(2)}, u32[]{:S(2)}) collective-permute-start(bf16[4,512,256]{2,1,0:T(8,128)(2,1)S(1)} %pack_pieces.2), channel_id=1, source_target_pairs={{0,4},{4,0},{8,12},{12,8},{16,20},{20,16},{24,28},{28,24},{1,5},{5... | collective-permute-start | bytes 3145736 | tf_op jit(solution)/shard_map/ppermute | solution.py:30
  42.9 7.0 %collective-permute-start.16 = (bf16[4,512,256]{2,1,0:T(8,128)(2,1)S(1)}, bf16[4,512,256]{2,1,0:T(8,128)(2,1)S(1)}, u32[]{:S(2)}, u32[]{:S(2)}) collective-permute-start(bf16[4,512,256]{2,1,0:T(8,128)(2,1)S(1)} %pack_pieces.3), channel_id=1, source_target_pairs={{0,4},{4,0},{8,12},{12,8},{16,20},{20,16},{24,28},{28,24},{1,5},{5... | collective-permute-start | bytes 3145736 | tf_op jit(solution)/shard_map/ppermute | solution.py:30
  43.2 5.8 %collective-permute-start.10 = (bf16[128,256]{1,0:T(8,128)(2,1)S(1)}, bf16[128,256]{1,0:T(8,128)(2,1)S(1)}, u32[]{:S(2)}, u32[]{:S(2)}) collective-permute-start(bf16[128,256]{1,0:T(8,128)(2,1)S(1)} %get-tuple-element.30), channel_id=1, source_target_pairs={{0,24},{4,28},{8,16},{12,20},{16,8},{20,12},{24,0},{28,4},{1,25},{... | collective-permute-start | bytes 196616 | tf_op jit(solution)/shard_map/ppermute | solution.py:30
  43.8 5.2 %collective-permute-start.8 = (bf16[128,256]{1,0:T(8,128)(2,1)S(1)}, bf16[128,256]{1,0:T(8,128)(2,1)S(1)}, u32[]{:S(2)}, u32[]{:S(2)}) collective-permute-start(bf16[128,256]{1,0:T(8,128)(2,1)S(1)} %get-tuple-element.28), channel_id=1, source_target_pairs={{0,8},{4,12},{8,0},{12,4},{16,24},{20,28},{24,16},{28,20},{1,9},{5... | collective-permute-start | bytes 196616 | tf_op jit(solution)/shard_map/ppermute | solution.py:30
  44.8 5.2 %collective-permute-start.9 = (bf16[128,256]{1,0:T(8,128)(2,1)S(1)}, bf16[128,256]{1,0:T(8,128)(2,1)S(1)}, u32[]{:S(2)}, u32[]{:S(2)}) collective-permute-start(bf16[128,256]{1,0:T(8,128)(2,1)S(1)} %get-tuple-element.29), channel_id=1, source_target_pairs={{0,16},{4,20},{8,24},{12,28},{16,0},{20,4},{24,8},{28,12},{1,17},{... | collective-permute-start | bytes 196616 | tf_op jit(solution)/shard_map/ppermute | solution.py:30

commit v5 on v4

--- a/solution.py
+++ b/solution.py
@@ -414,21 +414,21 @@
         far = diagonal(held[()], n_space, n_op)
     for plane in range(last):
         partial = plane_call(plane, (1, 2, 0), vecs[plane], vecs[plane + 1], link, phi, partial)
-    held, partial = hold(held, partial)
+    keep, give = plane_call(last, (0,), vecs[last], upper, link, phi, partial, n_space)
+    swapped = across(give, "space", 1)
     early = list(held)
-    flipped = [across(pack_call([held[key] for key in early]), "space", 1)]
-    for size in range(2, max(3, len(dims))):
-        stage(held, size)
     if len(dims) > 2:
         held[corner] = far
+    held, keep = hold(held, keep)
+    flipped = [across(pack_call([held[key] for key in early]), "space", 1)]
+    for size in range(2, len(dims) if len(dims) > 2 else 3):
+        stage(held, size)
     late = [key for key in held if key not in early]
-    keep, give = plane_call(last, (0,), vecs[last], upper, link, phi, partial, n_space)
-    swapped = across(give, "space", 1)
     merged = merge_call(keep, swapped)
-    after, swapped = hold({key: held[key] for key in late}, swapped)
+    got = [merged[0]] + [across(arr, "space", 2 * mask) for mask, arr in enumerate(merged[1:], 1)]
+    after, got = hold({key: held[key] for key in late}, got)
     held.update(after)
     flipped.append(across(pack_call([held[key] for key in late]), "space", 1))
-    got = [merged[0]] + [across(arr, "space", 2 * mask) for mask, arr in enumerate(merged[1:], 1)]
     tau = [held[key] for key in early + late] + flipped
     masks = []
     for flip in range(2):

time: 52.4 us -> 52.9 us (level)
  transfers between devices with their start and end apart: 17 -> 17, of which waited for: 8 -> 8; matrix products, arithmetic and copies ran while one was open for 3% -> 3% of each run, Pallas kernels for 32% -> 31%
where the time goes in v5:
time: 52.9 us; the launch traced here: 52.7 us
  starting transfers between devices  21.1 us (40%)
  Pallas kernels  18.8 us (36%)
  waiting for transfers between devices  9.69 us (18%)
  local copies, waits for them, and re-layouts  3 us (6%)
    ppermute x14, starting transfers between devices, across(): return lax.ppermute(value, axis, pairs)  15.9 us
    pallas_call x3, Pallas kernels, plane_call(): pl.pallas_call(functools.partial(plane_kernel, plane, dirs, part is not N...  15.4 us
    ppermute x14, waiting for transfers between devices, across(): return lax.ppermute(value, axis, pairs)  9.53 us
    ppermute x2, starting transfers between devices, from_behind(): return lax.ppermute(value, axis, pairs)  5.2 us
    unnamed x10, local copies, waits for them, and re-layouts  2.79 us
    pallas_call x1, Pallas kernels, shards(): pl.pallas_call(functools.partial(quark_kernel, masks, n_op, len(got), len...  2.26 us
  transfers between devices with their start and end apart: 17, of which 8 were waited for; matrix products, arithmetic and copies ran while one was open for 3% of the time, Pallas kernels for 31%

profile of v5, /device:TPU:0, one launch (start us, length us, event | category | flops | bytes accessed | tf_op | source)
XLA Modules:
  0.0 52.7 jit_solution(5053136703103792171)
XLA Ops:
  0.0 1.1 %dynamic-slice_bitcast_fusion = bf16[256,1,2,256]{3,2,0,1:T(2,128)(2,1)S(1)} fusion(bf16[256,16,2,256]{3,2,1,0:T(2,128)(2,1)} %bitcast.23, s32[]{:T(128)S(6)} %select_n.14), kind=kLoop, calls=%fused_computation.3 | loop fusion | bytes 524292
  1.1 0.1 reshape.10
  1.2 4.1 %collective-permute-start = (bf16[512,256]{1,0:T(8,128)(2,1)S(1)}, bf16[512,256]{1,0:T(8,128)(2,1)S(1)}, u32[]{:S(2)}, u32[]{:S(2)}) collective-permute-start(bf16[512,256]{1,0:T(8,128)(2,1)S(1)} %reshape.10), channel_id=1, source_target_pairs={{0,2},{2,0},{1,3},{3,1},{4,6},{6,4},{5,7},{7,5},{8,10},{10,8},{9,1... | collective-permute-start | bytes 786440 | tf_op jit(solution)/shard_map/ppermute | solution.py:25
  5.3 1.6 %collective-permute-start.2 = (s32[3,2,4]{2,1,0:T(2,128)}, s32[3,2,4]{2,1,0:T(2,128)S(1)}, u32[]{:S(2)}, u32[]{:S(2)}) collective-permute-start(s32[3,2,4]{2,1,0:T(2,128)} %bitcast.17), channel_id=1, source_target_pairs={{0,1},{1,0},{2,3},{3,2},{4,5},{5,4},{6,7},{7,6},{8,9},{9,8},{10,11... | collective-permute-start | bytes 296 | tf_op jit(solution)/shard_map/ppermute | solution.py:30
  6.9 0.4 collective-permute-start.1
  7.4 1.6 %copy.11 = bf16[1,2,256,3,2,256]{5,2,3,1,4,0:T(8,128)(2,1)S(1)} copy(bf16[1,2,256,3,2,256]{5,4,3,2,1,0:T(2,128)(2,1)} %param.6) | data formatting | bytes 3145728 | tf_op args[0]
  9.1 0.1 slice_bitcast_fusion
  9.2 1.1 %collective-permute-start.7 = (bf16[2,3,256,256]{3,2,1,0:T(8,128)(2,1)S(1)}, bf16[2,3,256,256]{3,2,1,0:T(8,128)(2,1)S(1)}, u32[]{:S(2)}, u32[]{:S(2)}) collective-permute-start(bf16[2,3,256,256]{3,2,1,0:T(8,128)(2,1)S(1)} %get-tuple-element.49.refs_0_), channel_id=1, source_target_pairs={{0,28},{4,0},{8,4},{12,8},{16,12},{20,16},{24,20},{28,24},{1,29},{... | collective-permute-start | bytes 2359304 | tf_op jit(solution)/shard_map/ppermute | solution.py:25
  10.3 0.8 %collective-permute-done.1.refs_1_ = s32[2,3]{1,0:T(2,128)S(1)} collective-permute-done((s32[2,3]{1,0:T(2,128)}, s32[2,3]{1,0:T(2,128)S(1)}, u32[]{:S(2)}, u32[]{:S(2)}) %collective-permute-start.1) | collective-permute-done | bytes 56 | tf_op jit(solution)/shard_map/ppermute | solution.py:30
  11.1 0.9 %phases.1.refs_2_.refs_3_ = f32[2,2,3,2,2,256]{5,4,3,2,1,0:T(2,128)S(1)} custom-call(s32[2,3]{1,0:T(2,128)S(1)} %copy-done.1, s32[2,3]{1,0:T(2,128)S(1)} %collective-permute-done.1.refs_1_, s32[3,2,4]{2,1,0:T(2,128)S(1)} %bitcast.18, s32[3,2,4]{2,1,0:T(2,128)S(1)} %collective-permute-done.2.refs_3_, s32[4]{0:T(128)S(1)} %copy-done.2), custom_call_target="tpu_custom_call" | custom-call | tf_op jit(solution)/shard_map/phases/pallas_call | solution.py:383
  12.0 5.1 %plane1_12.1.refs_4_ = f32[2,2,2,256,256]{4,3,2,1,0:T(8,128)S(1)} custom-call(bf16[2,3,256,256]{3,2,1,0:T(8,128)(2,1)S(1)} %get-tuple-element.50.refs_0_.refs_1_, f32[3,3,3,2,2,256]{5,4,3,2,1,0:T(2,128)S(1)} %bitcast.19, f32[2,2,3,2,2,256]{5,4,3,2,1,0:T(2,128)S(1)} %phases.1.refs_2_.refs_3_), custom_call_target="tpu_custom_call" | custom-call | flops 17179869184 | bytes 268435456 | tf_op jit(solution)/shard_map/plane1_12/pallas_call | solution.py:199
  17.1 0.1 collective-permute-done.refs_0_.refs_4_
  17.3 2.4 %collective-permute-start.3 = (bf16[512,256]{1,0:T(8,128)(2,1)S(1)}, bf16[512,256]{1,0:T(8,128)(2,1)S(1)}, u32[]{:S(2)}, u32[]{:S(2)}) collective-permute-start(bf16[512,256]{1,0:T(8,128)(2,1)S(1)} %collective-permute-done.refs_0_.refs_4_), channel_id=1, source_target_pairs={{0,1},{1,0},{2,3},{3,2},{4,5},{5,4},{6,7},{7,6},{8,9},{9,8},{10,11... | collective-permute-start | bytes 786440 | tf_op jit(solution)/shard_map/ppermute | solution.py:30
  19.7 1.5 %collective-permute-start.4 = (bf16[512,256]{1,0:T(8,128)(2,1)S(1)}, bf16[512,256]{1,0:T(8,128)(2,1)S(1)}, u32[]{:S(2)}, u32[]{:S(2)}) collective-permute-start(bf16[512,256]{1,0:T(8,128)(2,1)S(1)} %collective-permute-done.refs_0_.refs_4_), channel_id=1, source_target_pairs={{0,8},{4,12},{8,0},{12,4},{16,24},{20,28},{24,16},{28,20},{1,9},{5... | collective-permute-start | bytes 786440 | tf_op jit(solution)/shard_map/ppermute | solution.py:30
  21.2 1.5 %collective-permute-start.5 = (bf16[512,256]{1,0:T(8,128)(2,1)S(1)}, bf16[512,256]{1,0:T(8,128)(2,1)S(1)}, u32[]{:S(2)}, u32[]{:S(2)}) collective-permute-start(bf16[512,256]{1,0:T(8,128)(2,1)S(1)} %collective-permute-done.refs_0_.refs_4_), channel_id=1, source_target_pairs={{0,16},{4,20},{8,24},{12,28},{16,0},{20,4},{24,8},{28,12},{1,17},{... | collective-permute-start | bytes 786440 | tf_op jit(solution)/shard_map/ppermute | solution.py:30
  22.7 6.8 %plane0_120.1.refs_4_ = f32[2,2,2,256,256]{4,3,2,1,0:T(8,128)S(1)} custom-call(bf16[2,3,256,256]{3,2,1,0:T(8,128)(2,1)S(1)} %get-tuple-element.49.refs_0_, bf16[2,3,256,256]{3,2,1,0:T(8,128)(2,1)S(1)} %get-tuple-element.50.refs_0_.refs_1_, f32[3,3,3,2,2,256]{5,4,3,2,1,0:T(2,128)S(1)} %bitcast.20, f32[2,2,3,2,2,256]{5,4,3,2,1,0:T(2,128)S(1)} %phases.1.refs_2_.refs_3_, ...), custom_call_target="tpu_custom_call" | custom-call | flops 17179869184 | bytes 268435456 | tf_op jit(solution)/shard_map/plane0_120/pallas_call | solution.py:199
  29.5 3.5 %plane1_0.1 = (f32[4,2,2,32,256]{4,3,2,1,0:T(8,128)S(1)}, bf16[4,2,2,32,256]{4,3,2,1,0:T(8,128)(2,1)S(1)}) custom-call(bf16[2,3,256,256]{3,2,1,0:T(8,128)(2,1)S(1)} %get-tuple-element.50.refs_0_.refs_1_, bf16[2,3,256,256]{3,2,1,0:T(8,128)(2,1)S(1)} %collective-permute-done.7.refs_1_, f32[3,3,3,2,2,256]{5,4,3,2,1,0:T(2,128)S(1)} %bitcast.21, ...), custom_call_target="tpu_custom_call" | custom-call | flops 17179869184 | bytes 268435456 | tf_op jit(solution)/shard_map/plane1_0/pallas_call | solution.py:199
  33.1 0.1 collective-permute-start.11
  33.2 0.2 collective-permute-done.5.refs_3_.refs_7_
  33.4 1.3 %collective-permute-start.10 = (bf16[512,256]{1,0:T(8,128)(2,1)S(1)}, bf16[512,256]{1,0:T(8,128)(2,1)S(1)}, u32[]{:S(2)}, u32[]{:S(2)}) collective-permute-start(bf16[512,256]{1,0:T(8,128)(2,1)S(1)} %collective-permute-done.5.refs_3_.refs_7_), channel_id=1, source_target_pairs={{0,8},{4,12},{8,0},{12,4},{16,24},{20,28},{24,16},{28,20},{1,9},{5... | collective-permute-start | bytes 786440 | tf_op jit(solution)/shard_map/ppermute | solution.py:30
  34.7 1.9 %collective-permute-start.8 = (bf16[512,256]{1,0:T(8,128)(2,1)S(1)}, bf16[512,256]{1,0:T(8,128)(2,1)S(1)}, u32[]{:S(2)}, u32[]{:S(2)}) collective-permute-start(bf16[512,256]{1,0:T(8,128)(2,1)S(1)} %collective-permute-done.4.refs_2_.refs_6_), channel_id=1, source_target_pairs={{0,1},{1,0},{2,3},{3,2},{4,5},{5,4},{6,7},{7,6},{8,9},{9,8},{10,11... | collective-permute-start | bytes 786440 | tf_op jit(solution)/shard_map/ppermute | solution.py:30
  36.7 1.5 %collective-permute-start.9 = (bf16[512,256]{1,0:T(8,128)(2,1)S(1)}, bf16[512,256]{1,0:T(8,128)(2,1)S(1)}, u32[]{:S(2)}, u32[]{:S(2)}) collective-permute-start(bf16[512,256]{1,0:T(8,128)(2,1)S(1)} %collective-permute-done.3.refs_1_.refs_5_), channel_id=1, source_target_pairs={{0,16},{4,20},{8,24},{12,28},{16,0},{20,4},{24,8},{28,12},{1,17},{... | collective-permute-start | bytes 786440 | tf_op jit(solution)/shard_map/ppermute | solution.py:30
  38.3 0.6 %collective-permute-start.12 = (bf16[128,256]{1,0:T(8,128)(2,1)S(1)}, bf16[128,256]{1,0:T(8,128)(2,1)S(1)}, u32[]{:S(2)}, u32[]{:S(2)}) collective-permute-start(bf16[128,256]{1,0:T(8,128)(2,1)S(1)} %get-tuple-element.37), channel_id=1, source_target_pairs={{0,8},{4,12},{8,0},{12,4},{16,24},{20,28},{24,16},{28,20},{1,9},{5... | collective-permute-start | bytes 196616 | tf_op jit(solution)/shard_map/ppermute | solution.py:30
  38.9 0.5 collective-permute-start.13
  39.4 3.2 %collective-permute-done.10.refs_3_.refs_11_ = bf16[512,256]{1,0:T(8,128)(2,1)S(1)} collective-permute-done((bf16[512,256]{1,0:T(8,128)(2,1)S(1)}, bf16[512,256]{1,0:T(8,128)(2,1)S(1)}, u32[]{:S(2)}, u32[]{:S(2)}) %collective-permute-start.10) | collective-permute-done | bytes 262176 | tf_op jit(solution)/shard_map/ppermute | solution.py:30
  42.5 2.3 %collective-permute-start.14 = (bf16[128,256]{1,0:T(8,128)(2,1)S(1)}, bf16[128,256]{1,0:T(8,128)(2,1)S(1)}, u32[]{:S(2)}, u32[]{:S(2)}) collective-permute-start(bf16[128,256]{1,0:T(8,128)(2,1)S(1)} %get-tuple-element.39), channel_id=1, source_target_pairs={{0,24},{4,28},{8,16},{12,20},{16,8},{20,12},{24,0},{28,4},{1,25},{... | collective-permute-start | bytes 196616 | tf_op jit(solution)/shard_map/ppermute | solution.py:30
  44.9 0.1 collective-permute-start.15
  45.0 1.3 %collective-permute-done.9.refs_2_.refs_10_ = bf16[512,256]{1,0:T(8,128)(2,1)S(1)} collective-permute-done((bf16[512,256]{1,0:T(8,128)(2,1)S(1)}, bf16[512,256]{1,0:T(8,128)(2,1)S(1)}, u32[]{:S(2)}, u32[]{:S(2)}) %collective-permute-start.9) | collective-permute-done | bytes 262176 | tf_op jit(solution)/shard_map/ppermute | solution.py:30
  46.2 0.7 %collective-permute-done.13.refs_2_ = bf16[128,256]{1,0:T(8,128)(2,1)S(1)} collective-permute-done((bf16[128,256]{1,0:T(8,128)(2,1)S(1)}, bf16[128,256]{1,0:T(8,128)(2,1)S(1)}, u32[]{:S(2)}, u32[]{:S(2)}) %collective-permute-start.13) | collective-permute-done | bytes 65568 | tf_op jit(solution)/shard_map/ppermute | solution.py:30
  46.9 0.8 %collective-permute-done.14.refs_3_ = bf16[128,256]{1,0:T(8,128)(2,1)S(1)} collective-permute-done((bf16[128,256]{1,0:T(8,128)(2,1)S(1)}, bf16[128,256]{1,0:T(8,128)(2,1)S(1)}, u32[]{:S(2)}, u32[]{:S(2)}) %collective-permute-start.14) | collective-permute-done | bytes 65568 | tf_op jit(solution)/shard_map/ppermute | solution.py:30
  47.8 2.6 %collective-permute-done.16.refs_13_ = bf16[4,512,256]{2,1,0:T(8,128)(2,1)S(1)} collective-permute-done((bf16[4,512,256]{2,1,0:T(8,128)(2,1)S(1)}, bf16[4,512,256]{2,1,0:T(8,128)(2,1)S(1)}, u32[]{:S(2)}, u32[]{:S(2)}) %collective-permute-start.16) | collective-permute-done | bytes 1048608 | tf_op jit(solution)/shard_map/ppermute | solution.py:30
  50.5 2.3 %quark_products.1 = f32[2,16,2,32,256]{4,3,2,1,0:T(8,128)} custom-call(f32[128,256]{1,0:T(8,128)S(1)} %get-tuple-element.40.refs_0_, bf16[128,256]{1,0:T(8,128)(2,1)S(1)} %collective-permute-done.12.refs_1_, bf16[128,256]{1,0:T(8,128)(2,1)S(1)} %collective-permute-done.13.refs_2_, bf16[128,256]{1,0:T(8,128)(2,1)S(1)} %collective-permute-done.14.refs_3_, ...), custom_call_target="tpu_custom_call" | custom-call | flops 536870912 | bytes 7340032 | tf_op jit(solution)/shard_map/quark_products/pallas_call | solution.py:441
  (22 shorter events, 0.3 us)
Async XLA Ops:
  1.2 16.0 %collective-permute-start = (bf16[512,256]{1,0:T(8,128)(2,1)S(1)}, bf16[512,256]{1,0:T(8,128)(2,1)S(1)}, u32[]{:S(2)}, u32[]{:S(2)}) collective-permute-start(bf16[512,256]{1,0:T(8,128)(2,1)S(1)} %reshape.10), channel_id=1, source_target_pairs={{0,2},{2,0},{1,3},{3,1},{4,6},{6,4},{5,7},{7,5},{8,10},{10,8},{9,1... | collective-permute-start | bytes 786440 | tf_op jit(solution)/shard_map/ppermute | solution.py:25
  5.3 5.7 %collective-permute-start.2 = (s32[3,2,4]{2,1,0:T(2,128)}, s32[3,2,4]{2,1,0:T(2,128)S(1)}, u32[]{:S(2)}, u32[]{:S(2)}) collective-permute-start(s32[3,2,4]{2,1,0:T(2,128)} %bitcast.17), channel_id=1, source_target_pairs={{0,1},{1,0},{2,3},{3,2},{4,5},{5,4},{6,7},{7,6},{8,9},{9,8},{10,11... | collective-permute-start | bytes 296 | tf_op jit(solution)/shard_map/ppermute | solution.py:30
  6.9 4.1 %collective-permute-start.1 = (s32[2,3]{1,0:T(2,128)}, s32[2,3]{1,0:T(2,128)S(1)}, u32[]{:S(2)}, u32[]{:S(2)}) collective-permute-start(s32[2,3]{1,0:T(2,128)} %refs_0_.1), channel_id=1, source_target_pairs={{0,1},{1,0},{2,3},{3,2},{4,5},{5,4},{6,7},{7,6},{8,9},{9,8},{10,11... | collective-permute-start | bytes 80 | tf_op jit(solution)/shard_map/ppermute | solution.py:30
  9.0 2.0 %copy-start = (s32[4,2,3]{0,1,2:T(2,128)S(1)}, s32[4,2,3]{0,1,2:T(2,128)}, u32[]{:S(2)}) copy-start(s32[4,2,3]{0,1,2:T(2,128)} %param.9) | copy-start | bytes 292
  9.0 2.0 %copy-start.1 = (s32[2,3]{1,0:T(2,128)S(1)}, s32[2,3]{1,0:T(2,128)}, u32[]{:S(2)}) copy-start(s32[2,3]{1,0:T(2,128)} %refs_0_.1) | copy-start | bytes 76
  9.0 2.0 %copy-start.2 = (s32[4]{0:T(128)S(1)}, s32[4]{0:T(128)}, u32[]{:S(2)}) copy-start(s32[4]{0:T(128)} %refs_4_.1) | copy-start | bytes 52
  9.1 3.0 %copy-start.3 = (f32[1,3,3,3,2,2,256]{6,5,4,3,2,1,0:T(2,128)S(1)}, f32[1,3,3,3,2,2,256]{6,5,4,3,2,1,0:T(2,128)}, u32[]{:S(2)}) copy-start(f32[1,3,3,3,2,2,256]{6,5,4,3,2,1,0:T(2,128)} %param.7) | copy-start | bytes 331780
  9.2 20.3 %collective-permute-start.7 = (bf16[2,3,256,256]{3,2,1,0:T(8,128)(2,1)S(1)}, bf16[2,3,256,256]{3,2,1,0:T(8,128)(2,1)S(1)}, u32[]{:S(2)}, u32[]{:S(2)}) collective-permute-start(bf16[2,3,256,256]{3,2,1,0:T(8,128)(2,1)S(1)} %get-tuple-element.49.refs_0_), channel_id=1, source_target_pairs={{0,28},{4,0},{8,4},{12,8},{16,12},{20,16},{24,20},{28,24},{1,29},{... | collective-permute-start | bytes 2359304 | tf_op jit(solution)/shard_map/ppermute | solution.py:25
  17.3 15.9 %collective-permute-start.3 = (bf16[512,256]{1,0:T(8,128)(2,1)S(1)}, bf16[512,256]{1,0:T(8,128)(2,1)S(1)}, u32[]{:S(2)}, u32[]{:S(2)}) collective-permute-start(bf16[512,256]{1,0:T(8,128)(2,1)S(1)} %collective-permute-done.refs_0_.refs_4_), channel_id=1, source_target_pairs={{0,1},{1,0},{2,3},{3,2},{4,5},{5,4},{6,7},{7,6},{8,9},{9,8},{10,11... | collective-permute-start | bytes 786440 | tf_op jit(solution)/shard_map/ppermute | solution.py:30
  19.7 13.4 %collective-permute-start.4 = (bf16[512,256]{1,0:T(8,128)(2,1)S(1)}, bf16[512,256]{1,0:T(8,128)(2,1)S(1)}, u32[]{:S(2)}, u32[]{:S(2)}) collective-permute-start(bf16[512,256]{1,0:T(8,128)(2,1)S(1)} %collective-permute-done.refs_0_.refs_4_), channel_id=1, source_target_pairs={{0,8},{4,12},{8,0},{12,4},{16,24},{20,28},{24,16},{28,20},{1,9},{5... | collective-permute-start | bytes 786440 | tf_op jit(solution)/shard_map/ppermute | solution.py:30
  21.2 12.2 %collective-permute-start.5 = (bf16[512,256]{1,0:T(8,128)(2,1)S(1)}, bf16[512,256]{1,0:T(8,128)(2,1)S(1)}, u32[]{:S(2)}, u32[]{:S(2)}) collective-permute-start(bf16[512,256]{1,0:T(8,128)(2,1)S(1)} %collective-permute-done.refs_0_.refs_4_), channel_id=1, source_target_pairs={{0,16},{4,20},{8,24},{12,28},{16,0},{20,4},{24,8},{28,12},{1,17},{... | collective-permute-start | bytes 786440 | tf_op jit(solution)/shard_map/ppermute | solution.py:30
  22.7 10.7 %collective-permute-start.6 = (bf16[512,256]{1,0:T(8,128)(2,1)S(1)}, bf16[512,256]{1,0:T(8,128)(2,1)S(1)}, u32[]{:S(2)}, u32[]{:S(2)}) collective-permute-start(bf16[512,256]{1,0:T(8,128)(2,1)S(1)} %collective-permute-done.refs_0_.refs_4_), channel_id=1, source_target_pairs={{0,25},{1,24},{4,29},{5,28},{8,17},{9,16},{12,21},{13,20},{16,9},{... | collective-permute-start | bytes 786440 | tf_op jit(solution)/shard_map/ppermute | solution.py:39
  33.1 5.1 %collective-permute-start.11 = (bf16[4,2,2,32,256]{4,3,2,1,0:T(8,128)(2,1)S(1)}, bf16[4,2,2,32,256]{4,3,2,1,0:T(8,128)(2,1)S(1)}, u32[]{:S(2)}, u32[]{:S(2)}) collective-permute-start(bf16[4,2,2,32,256]{4,3,2,1,0:T(8,128)(2,1)S(1)} %get-tuple-element.35), channel_id=1, source_target_pairs={{0,4},{4,0},{8,12},{12,8},{16,20},{20,16},{24,28},{28,24},{1,5},{5... | collective-permute-start | bytes 786440 | tf_op jit(solution)/shard_map/ppermute | solution.py:30
  33.4 9.1 %collective-permute-start.10 = (bf16[512,256]{1,0:T(8,128)(2,1)S(1)}, bf16[512,256]{1,0:T(8,128)(2,1)S(1)}, u32[]{:S(2)}, u32[]{:S(2)}) collective-permute-start(bf16[512,256]{1,0:T(8,128)(2,1)S(1)} %collective-permute-done.5.refs_3_.refs_7_), channel_id=1, source_target_pairs={{0,8},{4,12},{8,0},{12,4},{16,24},{20,28},{24,16},{28,20},{1,9},{5... | collective-permute-start | bytes 786440 | tf_op jit(solution)/shard_map/ppermute | solution.py:30
  34.7 10.1 %collective-permute-start.8 = (bf16[512,256]{1,0:T(8,128)(2,1)S(1)}, bf16[512,256]{1,0:T(8,128)(2,1)S(1)}, u32[]{:S(2)}, u32[]{:S(2)}) collective-permute-start(bf16[512,256]{1,0:T(8,128)(2,1)S(1)} %collective-permute-done.4.refs_2_.refs_6_), channel_id=1, source_target_pairs={{0,1},{1,0},{2,3},{3,2},{4,5},{5,4},{6,7},{7,6},{8,9},{9,8},{10,11... | collective-permute-start | bytes 786440 | tf_op jit(solution)/shard_map/ppermute | solution.py:30
  36.7 9.5 %collective-permute-start.9 = (bf16[512,256]{1,0:T(8,128)(2,1)S(1)}, bf16[512,256]{1,0:T(8,128)(2,1)S(1)}, u32[]{:S(2)}, u32[]{:S(2)}) collective-permute-start(bf16[512,256]{1,0:T(8,128)(2,1)S(1)} %collective-permute-done.3.refs_1_.refs_5_), channel_id=1, source_target_pairs={{0,16},{4,20},{8,24},{12,28},{16,0},{20,4},{24,8},{28,12},{1,17},{... | collective-permute-start | bytes 786440 | tf_op jit(solution)/shard_map/ppermute | solution.py:30
  38.3 8.0 %collective-permute-start.12 = (bf16[128,256]{1,0:T(8,128)(2,1)S(1)}, bf16[128,256]{1,0:T(8,128)(2,1)S(1)}, u32[]{:S(2)}, u32[]{:S(2)}) collective-permute-start(bf16[128,256]{1,0:T(8,128)(2,1)S(1)} %get-tuple-element.37), channel_id=1, source_target_pairs={{0,8},{4,12},{8,0},{12,4},{16,24},{20,28},{24,16},{28,20},{1,9},{5... | collective-permute-start | bytes 196616 | tf_op jit(solution)/shard_map/ppermute | solution.py:30
  38.9 8.1 %collective-permute-start.13 = (bf16[128,256]{1,0:T(8,128)(2,1)S(1)}, bf16[128,256]{1,0:T(8,128)(2,1)S(1)}, u32[]{:S(2)}, u32[]{:S(2)}) collective-permute-start(bf16[128,256]{1,0:T(8,128)(2,1)S(1)} %get-tuple-element.38), channel_id=1, source_target_pairs={{0,16},{4,20},{8,24},{12,28},{16,0},{20,4},{24,8},{28,12},{1,17},{... | collective-permute-start | bytes 196616 | tf_op jit(solution)/shard_map/ppermute | solution.py:30
  42.5 5.2 %collective-permute-start.14 = (bf16[128,256]{1,0:T(8,128)(2,1)S(1)}, bf16[128,256]{1,0:T(8,128)(2,1)S(1)}, u32[]{:S(2)}, u32[]{:S(2)}) collective-permute-start(bf16[128,256]{1,0:T(8,128)(2,1)S(1)} %get-tuple-element.39), channel_id=1, source_target_pairs={{0,24},{4,28},{8,16},{12,20},{16,8},{20,12},{24,0},{28,4},{1,25},{... | collective-permute-start | bytes 196616 | tf_op jit(solution)/shard_map/ppermute | solution.py:30
  44.9 3.0 %collective-permute-start.15 = (bf16[4,512,256]{2,1,0:T(8,128)(2,1)S(1)}, bf16[4,512,256]{2,1,0:T(8,128)(2,1)S(1)}, u32[]{:S(2)}, u32[]{:S(2)}) collective-permute-start(bf16[4,512,256]{2,1,0:T(8,128)(2,1)S(1)} %pack_pieces.2), channel_id=1, source_target_pairs={{0,4},{4,0},{8,12},{12,8},{16,20},{20,16},{24,28},{28,24},{1,5},{5... | collective-permute-start | bytes 3145736 | tf_op jit(solution)/shard_map/ppermute | solution.py:30
  47.8 2.7 %collective-permute-start.16 = (bf16[4,512,256]{2,1,0:T(8,128)(2,1)S(1)}, bf16[4,512,256]{2,1,0:T(8,128)(2,1)S(1)}, u32[]{:S(2)}, u32[]{:S(2)}) collective-permute-start(bf16[4,512,256]{2,1,0:T(8,128)(2,1)S(1)} %pack_pieces.3), channel_id=1, source_target_pairs={{0,4},{4,0},{8,12},{12,8},{16,20},{20,16},{24,28},{28,24},{1,5},{5... | collective-permute-start | bytes 3145736 | tf_op jit(solution)/shard_map/ppermute | solution.py:30

commit v6 on v5

--- a/solution.py
+++ b/solution.py
@@ -212,28 +212,25 @@
     )(*args)
 
 
-def merge_kernel(keep_ref, got_ref, own_ref, *out_refs):
-    chip = lax.axis_index("space") >> 1
-    shape = own_ref.shape
-    own_ref[...] = (keep_ref[chip] + got_ref[chip].astype(jnp.float32)).reshape(shape)
-    for mask, out_ref in enumerate(out_refs, 1):
-        total = keep_ref[chip ^ mask] + got_ref[chip ^ mask].astype(jnp.float32)
-        out_ref[...] = total.reshape(shape).astype(jnp.bfloat16)
-
-
-def merge_call(keep, got):
-    chips, n_h, _, own, n_b = keep.shape
-    shape = (n_h * 2 * own, n_b)
+def merge_kernel(bit, keep_ref, got_ref, next_ref, give_ref):
+    mine = (lax.axis_index("space") >> bit) & 1
+    total = keep_ref[...] + got_ref[...].astype(jnp.float32)
+    halves = total.reshape((total.shape[0] // 2, 2) + total.shape[1:])
+    next_ref[...] = jnp.where(mine == 0, halves[:, 0], halves[:, 1])
+    give_ref[...] = jnp.where(mine == 0, halves[:, 1], halves[:, 0]).astype(jnp.bfloat16)
+
+
+def merge_call(keep, got, bit):
+    shape = (keep.shape[0] // 2,) + keep.shape[1:]
     vmem = pl.BlockSpec(memory_space=pltpu.VMEM)
     return pl.pallas_call(
-        merge_kernel,
+        functools.partial(merge_kernel, bit),
         in_specs=[vmem, vmem],
-        out_specs=[vmem] * chips,
-        out_shape=[jax.ShapeDtypeStruct(shape, jnp.float32)]
-        + [jax.ShapeDtypeStruct(shape, jnp.bfloat16)] * (chips - 1),
+        out_specs=[vmem, vmem],
+        out_shape=[jax.ShapeDtypeStruct(shape, jnp.float32), jax.ShapeDtypeStruct(shape, jnp.bfloat16)],
         compiler_params=pltpu.CompilerParams(vmem_limit_bytes=8 * 2**20),
         cost_estimate=pl.CostEstimate(flops=2**16, bytes_accessed=2**12, transcendentals=0),
-        name="merge_cores",
+        name="merge_bit%d" % bit,
     )(keep, got)
 
 
@@ -265,9 +262,8 @@
     col = lax.broadcasted_iota(jnp.int32, (n_b, 2 * n_b), 1)
     even = (col == 2 * row).astype(jnp.bfloat16)
     odd = (col == 2 * row + 1).astype(jnp.bfloat16)
-    total = got_refs[0][...]
-    for ref in got_refs[1:]:
-        total = total + ref[...].astype(jnp.float32)
+    total = got_refs[0][0] + got_refs[1][0].astype(jnp.float32)
+    total = total.reshape(n_h * 2 * own, n_b)
     swap = []
     for hel in range(n_h):
         start = hel * 2 * own
@@ -424,10 +420,13 @@
     for size in range(2, len(dims) if len(dims) > 2 else 3):
         stage(held, size)
     late = [key for key in held if key not in early]
-    merged = merge_call(keep, swapped)
-    got = [merged[0]] + [across(arr, "space", 2 * mask) for mask, arr in enumerate(merged[1:], 1)]
-    after, got = hold({key: held[key] for key in late}, got)
-    held.update(after)
+    for bit in range(1, n_space.bit_length() - 1):
+        keep, give = merge_call(keep, swapped, bit)
+        if bit == n_space.bit_length() - 2:
+            after, give = hold({key: held[key] for key in late}, give)
+            held.update(after)
+        swapped = across(give, "space", 1 << bit)
+    got = [keep, swapped]
     flipped.append(across(pack_call([held[key] for key in late]), "space", 1))
     tau = [held[key] for key in early + late] + flipped
     masks = []

time: 52.9 us -> 54.8 us (1.036)
  waiting for transfers between devices: 9.69 us -> 13.7 us
  starting transfers between devices: 21.1 us -> 18.9 us
    ppermute x14 -> x13, waiting for transfers between devices: 9.53 us -> 13.6 us  [across(): return lax.ppermute(value, axis, pairs)]
    ppermute x14 -> x13, starting transfers between devices: 15.9 us -> 13.7 us  [across(): return lax.ppermute(value, axis, pairs)]
  transfers between devices with their start and end apart: 17 -> 16, of which waited for: 8 -> 5; matrix products, arithmetic and copies ran while one was open for 3% -> 3% of each run, Pallas kernels for 31% -> 30%
where the time goes in v6:
time: 54.8 us; the launch traced here: 54.6 us
  starting transfers between devices  18.9 us (34%)
  Pallas kernels  18.8 us (34%)
  waiting for transfers between devices  13.7 us (25%)
  local copies, waits for them, and re-layouts  3 us (5%)
    pallas_call x3, Pallas kernels, plane_call(): pl.pallas_call(functools.partial(plane_kernel, plane, dirs, part is not N...  15.4 us
    ppermute x13, starting transfers between devices, across(): return lax.ppermute(value, axis, pairs)  13.7 us
    ppermute x13, waiting for transfers between devices, across(): return lax.ppermute(value, axis, pairs)  13.6 us
    ppermute x2, starting transfers between devices, from_behind(): return lax.ppermute(value, axis, pairs)  5.2 us
    unnamed x10, local copies, waits for them, and re-layouts  2.79 us
    pallas_call x1, Pallas kernels, shards(): pl.pallas_call(functools.partial(quark_kernel, masks, n_op, len(got), len...  2.23 us
  transfers between devices with their start and end apart: 16, of which 5 were waited for; matrix products, arithmetic and copies ran while one was open for 3% of the time, Pallas kernels for 30%

profile of v6, /device:TPU:0, one launch (start us, length us, event | category | flops | bytes accessed | tf_op | source)
XLA Modules:
  0.0 54.6 jit_solution(7166446043314744436)
XLA Ops:
  0.0 1.1 %dynamic-slice_bitcast_fusion = bf16[256,1,2,256]{3,2,0,1:T(2,128)(2,1)S(1)} fusion(bf16[256,16,2,256]{3,2,1,0:T(2,128)(2,1)} %bitcast.23, s32[]{:T(128)S(6)} %select_n.14), kind=kLoop, calls=%fused_computation.3 | loop fusion | bytes 524292
  1.1 0.1 reshape.10
  1.2 4.1 %collective-permute-start = (bf16[512,256]{1,0:T(8,128)(2,1)S(1)}, bf16[512,256]{1,0:T(8,128)(2,1)S(1)}, u32[]{:S(2)}, u32[]{:S(2)}) collective-permute-start(bf16[512,256]{1,0:T(8,128)(2,1)S(1)} %reshape.10), channel_id=1, source_target_pairs={{0,2},{2,0},{1,3},{3,1},{4,6},{6,4},{5,7},{7,5},{8,10},{10,8},{9,1... | collective-permute-start | bytes 786440 | tf_op jit(solution)/shard_map/ppermute | solution.py:25
  5.3 1.6 %collective-permute-start.2 = (s32[3,2,4]{2,1,0:T(2,128)}, s32[3,2,4]{2,1,0:T(2,128)S(1)}, u32[]{:S(2)}, u32[]{:S(2)}) collective-permute-start(s32[3,2,4]{2,1,0:T(2,128)} %bitcast.17), channel_id=1, source_target_pairs={{0,1},{1,0},{2,3},{3,2},{4,5},{5,4},{6,7},{7,6},{8,9},{9,8},{10,11... | collective-permute-start | bytes 296 | tf_op jit(solution)/shard_map/ppermute | solution.py:30
  6.9 0.4 collective-permute-start.1
  7.4 1.6 %copy.11 = bf16[1,2,256,3,2,256]{5,2,3,1,4,0:T(8,128)(2,1)S(1)} copy(bf16[1,2,256,3,2,256]{5,4,3,2,1,0:T(2,128)(2,1)} %param.6) | data formatting | bytes 3145728 | tf_op args[0]
  9.1 0.1 slice_bitcast_fusion
  9.2 1.1 %collective-permute-start.7 = (bf16[2,3,256,256]{3,2,1,0:T(8,128)(2,1)S(1)}, bf16[2,3,256,256]{3,2,1,0:T(8,128)(2,1)S(1)}, u32[]{:S(2)}, u32[]{:S(2)}) collective-permute-start(bf16[2,3,256,256]{3,2,1,0:T(8,128)(2,1)S(1)} %get-tuple-element.43.refs_0_), channel_id=1, source_target_pairs={{0,28},{4,0},{8,4},{12,8},{16,12},{20,16},{24,20},{28,24},{1,29},{... | collective-permute-start | bytes 2359304 | tf_op jit(solution)/shard_map/ppermute | solution.py:25
  10.3 0.8 %collective-permute-done.1.refs_1_ = s32[2,3]{1,0:T(2,128)S(1)} collective-permute-done((s32[2,3]{1,0:T(2,128)}, s32[2,3]{1,0:T(2,128)S(1)}, u32[]{:S(2)}, u32[]{:S(2)}) %collective-permute-start.1) | collective-permute-done | bytes 56 | tf_op jit(solution)/shard_map/ppermute | solution.py:30
  11.1 0.9 %phases.1.refs_2_.refs_3_ = f32[2,2,3,2,2,256]{5,4,3,2,1,0:T(2,128)S(1)} custom-call(s32[2,3]{1,0:T(2,128)S(1)} %copy-done.1, s32[2,3]{1,0:T(2,128)S(1)} %collective-permute-done.1.refs_1_, s32[3,2,4]{2,1,0:T(2,128)S(1)} %bitcast.18, s32[3,2,4]{2,1,0:T(2,128)S(1)} %collective-permute-done.2.refs_3_, s32[4]{0:T(128)S(1)} %copy-done.2), custom_call_target="tpu_custom_call" | custom-call | tf_op jit(solution)/shard_map/phases/pallas_call | solution.py:379
  12.0 5.1 %plane1_12.1.refs_4_ = f32[2,2,2,256,256]{4,3,2,1,0:T(8,128)S(1)} custom-call(bf16[2,3,256,256]{3,2,1,0:T(8,128)(2,1)S(1)} %get-tuple-element.44.refs_0_.refs_1_, f32[3,3,3,2,2,256]{5,4,3,2,1,0:T(2,128)S(1)} %bitcast.19, f32[2,2,3,2,2,256]{5,4,3,2,1,0:T(2,128)S(1)} %phases.1.refs_2_.refs_3_), custom_call_target="tpu_custom_call" | custom-call | flops 17179869184 | bytes 268435456 | tf_op jit(solution)/shard_map/plane1_12/pallas_call | solution.py:199
  17.1 0.1 collective-permute-done.refs_0_.refs_2_
  17.3 2.4 %collective-permute-start.3 = (bf16[512,256]{1,0:T(8,128)(2,1)S(1)}, bf16[512,256]{1,0:T(8,128)(2,1)S(1)}, u32[]{:S(2)}, u32[]{:S(2)}) collective-permute-start(bf16[512,256]{1,0:T(8,128)(2,1)S(1)} %collective-permute-done.refs_0_.refs_2_), channel_id=1, source_target_pairs={{0,1},{1,0},{2,3},{3,2},{4,5},{5,4},{6,7},{7,6},{8,9},{9,8},{10,11... | collective-permute-start | bytes 786440 | tf_op jit(solution)/shard_map/ppermute | solution.py:30
  19.7 1.5 %collective-permute-start.4 = (bf16[512,256]{1,0:T(8,128)(2,1)S(1)}, bf16[512,256]{1,0:T(8,128)(2,1)S(1)}, u32[]{:S(2)}, u32[]{:S(2)}) collective-permute-start(bf16[512,256]{1,0:T(8,128)(2,1)S(1)} %collective-permute-done.refs_0_.refs_2_), channel_id=1, source_target_pairs={{0,8},{4,12},{8,0},{12,4},{16,24},{20,28},{24,16},{28,20},{1,9},{5... | collective-permute-start | bytes 786440 | tf_op jit(solution)/shard_map/ppermute | solution.py:30
  21.2 1.5 %collective-permute-start.5 = (bf16[512,256]{1,0:T(8,128)(2,1)S(1)}, bf16[512,256]{1,0:T(8,128)(2,1)S(1)}, u32[]{:S(2)}, u32[]{:S(2)}) collective-permute-start(bf16[512,256]{1,0:T(8,128)(2,1)S(1)} %collective-permute-done.refs_0_.refs_2_), channel_id=1, source_target_pairs={{0,16},{4,20},{8,24},{12,28},{16,0},{20,4},{24,8},{28,12},{1,17},{... | collective-permute-start | bytes 786440 | tf_op jit(solution)/shard_map/ppermute | solution.py:30
  22.7 6.8 %plane0_120.1.refs_4_ = f32[2,2,2,256,256]{4,3,2,1,0:T(8,128)S(1)} custom-call(bf16[2,3,256,256]{3,2,1,0:T(8,128)(2,1)S(1)} %get-tuple-element.43.refs_0_, bf16[2,3,256,256]{3,2,1,0:T(8,128)(2,1)S(1)} %get-tuple-element.44.refs_0_.refs_1_, f32[3,3,3,2,2,256]{5,4,3,2,1,0:T(2,128)S(1)} %bitcast.20, f32[2,2,3,2,2,256]{5,4,3,2,1,0:T(2,128)S(1)} %phases.1.refs_2_.refs_3_, ...), custom_call_target="tpu_custom_call" | custom-call | flops 17179869184 | bytes 268435456 | tf_op jit(solution)/shard_map/plane0_120/pallas_call | solution.py:199
  29.5 3.5 %plane1_0.1 = (f32[4,2,2,32,256]{4,3,2,1,0:T(8,128)S(1)}, bf16[4,2,2,32,256]{4,3,2,1,0:T(8,128)(2,1)S(1)}) custom-call(bf16[2,3,256,256]{3,2,1,0:T(8,128)(2,1)S(1)} %get-tuple-element.44.refs_0_.refs_1_, bf16[2,3,256,256]{3,2,1,0:T(8,128)(2,1)S(1)} %collective-permute-done.7.refs_1_, f32[3,3,3,2,2,256]{5,4,3,2,1,0:T(2,128)S(1)} %bitcast.21, ...), custom_call_target="tpu_custom_call" | custom-call | flops 17179869184 | bytes 268435456 | tf_op jit(solution)/shard_map/plane1_0/pallas_call | solution.py:199
  33.1 0.1 collective-permute-start.8
  33.2 0.2 collective-permute-done.5.refs_3_.refs_5_
  33.4 1.8 %collective-permute-start.10 = (bf16[512,256]{1,0:T(8,128)(2,1)S(1)}, bf16[512,256]{1,0:T(8,128)(2,1)S(1)}, u32[]{:S(2)}, u32[]{:S(2)}) collective-permute-start(bf16[512,256]{1,0:T(8,128)(2,1)S(1)} %collective-permute-done.4.refs_2_.refs_4_), channel_id=1, source_target_pairs={{0,1},{1,0},{2,3},{3,2},{4,5},{5,4},{6,7},{7,6},{8,9},{9,8},{10,11... | collective-permute-start | bytes 786440 | tf_op jit(solution)/shard_map/ppermute | solution.py:30
  35.2 1.5 %collective-permute-start.11 = (bf16[512,256]{1,0:T(8,128)(2,1)S(1)}, bf16[512,256]{1,0:T(8,128)(2,1)S(1)}, u32[]{:S(2)}, u32[]{:S(2)}) collective-permute-start(bf16[512,256]{1,0:T(8,128)(2,1)S(1)} %collective-permute-done.3.refs_1_.refs_3_), channel_id=1, source_target_pairs={{0,16},{4,20},{8,24},{12,28},{16,0},{20,4},{24,8},{28,12},{1,17},{... | collective-permute-start | bytes 786440 | tf_op jit(solution)/shard_map/ppermute | solution.py:30
  36.7 1.5 %collective-permute-start.12 = (bf16[512,256]{1,0:T(8,128)(2,1)S(1)}, bf16[512,256]{1,0:T(8,128)(2,1)S(1)}, u32[]{:S(2)}, u32[]{:S(2)}) collective-permute-start(bf16[512,256]{1,0:T(8,128)(2,1)S(1)} %collective-permute-done.5.refs_3_.refs_5_), channel_id=1, source_target_pairs={{0,8},{4,12},{8,0},{12,4},{16,24},{20,28},{24,16},{28,20},{1,9},{5... | collective-permute-start | bytes 786440 | tf_op jit(solution)/shard_map/ppermute | solution.py:30
  38.2 0.1 merge_bit1.1
  38.3 0.6 %collective-permute-start.9 = (bf16[2,2,2,32,256]{4,3,2,1,0:T(8,128)(2,1)S(1)}, bf16[2,2,2,32,256]{4,3,2,1,0:T(8,128)(2,1)S(1)}, u32[]{:S(2)}, u32[]{:S(2)}) collective-permute-start(bf16[2,2,2,32,256]{4,3,2,1,0:T(8,128)(2,1)S(1)} %get-tuple-element.30), channel_id=1, source_target_pairs={{0,8},{4,12},{8,0},{12,4},{16,24},{20,28},{24,16},{28,20},{1,9},{5... | collective-permute-start | bytes 393224 | tf_op jit(solution)/shard_map/ppermute | solution.py:30
  38.9 0.1 pack_pieces.2
  39.0 0.1 collective-permute-start.14
  39.0 8.6 %collective-permute-done.9.got_ref = bf16[2,2,2,32,256]{4,3,2,1,0:T(8,128)(2,1)S(1)} collective-permute-done((bf16[2,2,2,32,256]{4,3,2,1,0:T(8,128)(2,1)S(1)}, bf16[2,2,2,32,256]{4,3,2,1,0:T(8,128)(2,1)S(1)}, u32[]{:S(2)}, u32[]{:S(2)}) %collective-permute-start.9) | collective-permute-done | bytes 131104 | tf_op jit(solution)/shard_map/ppermute | solution.py:30
  47.7 0.1 pack_pieces.3
  47.8 0.1 collective-permute-start.15
  47.9 0.6 %collective-permute-start.13 = (bf16[1,2,2,32,256]{4,3,2,1,0:T(8,128)(2,1)S(1)}, bf16[1,2,2,32,256]{4,3,2,1,0:T(8,128)(2,1)S(1)}, u32[]{:S(2)}, u32[]{:S(2)}) collective-permute-start(bf16[1,2,2,32,256]{4,3,2,1,0:T(8,128)(2,1)S(1)} %get-tuple-element.37), channel_id=1, source_target_pairs={{0,16},{4,20},{8,24},{12,28},{16,0},{20,4},{24,8},{28,12},{1,17},{... | collective-permute-start | bytes 196616 | tf_op jit(solution)/shard_map/ppermute | solution.py:30
  48.4 3.9 %collective-permute-done.13.refs_1_ = bf16[1,2,2,32,256]{4,3,2,1,0:T(8,128)(2,1)S(1)} collective-permute-done((bf16[1,2,2,32,256]{4,3,2,1,0:T(8,128)(2,1)S(1)}, bf16[1,2,2,32,256]{4,3,2,1,0:T(8,128)(2,1)S(1)}, u32[]{:S(2)}, u32[]{:S(2)}) %collective-permute-start.13) | collective-permute-done | bytes 65568 | tf_op jit(solution)/shard_map/ppermute | solution.py:30
  52.4 2.2 %quark_products.1 = f32[2,16,2,32,256]{4,3,2,1,0:T(8,128)} custom-call(f32[1,2,2,32,256]{4,3,2,1,0:T(8,128)S(1)} %get-tuple-element.31.refs_0_, bf16[1,2,2,32,256]{4,3,2,1,0:T(8,128)(2,1)S(1)} %collective-permute-done.13.refs_1_, bf16[512,256]{1,0:T(8,128)(2,1)S(1)} %collective-permute-done.refs_0_.refs_2_, ...), custom_call_target="tpu_custom_call" | custom-call | flops 536870912 | bytes 7340032 | tf_op jit(solution)/shard_map/quark_products/pallas_call | solution.py:440
  (21 shorter events, 0.1 us)
Async XLA Ops:
  1.2 16.0 %collective-permute-start = (bf16[512,256]{1,0:T(8,128)(2,1)S(1)}, bf16[512,256]{1,0:T(8,128)(2,1)S(1)}, u32[]{:S(2)}, u32[]{:S(2)}) collective-permute-start(bf16[512,256]{1,0:T(8,128)(2,1)S(1)} %reshape.10), channel_id=1, source_target_pairs={{0,2},{2,0},{1,3},{3,1},{4,6},{6,4},{5,7},{7,5},{8,10},{10,8},{9,1... | collective-permute-start | bytes 786440 | tf_op jit(solution)/shard_map/ppermute | solution.py:25
  5.3 5.7 %collective-permute-start.2 = (s32[3,2,4]{2,1,0:T(2,128)}, s32[3,2,4]{2,1,0:T(2,128)S(1)}, u32[]{:S(2)}, u32[]{:S(2)}) collective-permute-start(s32[3,2,4]{2,1,0:T(2,128)} %bitcast.17), channel_id=1, source_target_pairs={{0,1},{1,0},{2,3},{3,2},{4,5},{5,4},{6,7},{7,6},{8,9},{9,8},{10,11... | collective-permute-start | bytes 296 | tf_op jit(solution)/shard_map/ppermute | solution.py:30
  6.9 4.1 %collective-permute-start.1 = (s32[2,3]{1,0:T(2,128)}, s32[2,3]{1,0:T(2,128)S(1)}, u32[]{:S(2)}, u32[]{:S(2)}) collective-permute-start(s32[2,3]{1,0:T(2,128)} %refs_0_.1), channel_id=1, source_target_pairs={{0,1},{1,0},{2,3},{3,2},{4,5},{5,4},{6,7},{7,6},{8,9},{9,8},{10,11... | collective-permute-start | bytes 80 | tf_op jit(solution)/shard_map/ppermute | solution.py:30
  9.0 2.0 %copy-start = (s32[4,2,3]{0,1,2:T(2,128)S(1)}, s32[4,2,3]{0,1,2:T(2,128)}, u32[]{:S(2)}) copy-start(s32[4,2,3]{0,1,2:T(2,128)} %param.9) | copy-start | bytes 292
  9.0 2.0 %copy-start.1 = (s32[2,3]{1,0:T(2,128)S(1)}, s32[2,3]{1,0:T(2,128)}, u32[]{:S(2)}) copy-start(s32[2,3]{1,0:T(2,128)} %refs_0_.1) | copy-start | bytes 76
  9.0 2.0 %copy-start.2 = (s32[4]{0:T(128)S(1)}, s32[4]{0:T(128)}, u32[]{:S(2)}) copy-start(s32[4]{0:T(128)} %refs_4_.1) | copy-start | bytes 52
  9.1 3.0 %copy-start.3 = (f32[1,3,3,3,2,2,256]{6,5,4,3,2,1,0:T(2,128)S(1)}, f32[1,3,3,3,2,2,256]{6,5,4,3,2,1,0:T(2,128)}, u32[]{:S(2)}) copy-start(f32[1,3,3,3,2,2,256]{6,5,4,3,2,1,0:T(2,128)} %param.7) | copy-start | bytes 331780
  9.2 20.3 %collective-permute-start.7 = (bf16[2,3,256,256]{3,2,1,0:T(8,128)(2,1)S(1)}, bf16[2,3,256,256]{3,2,1,0:T(8,128)(2,1)S(1)}, u32[]{:S(2)}, u32[]{:S(2)}) collective-permute-start(bf16[2,3,256,256]{3,2,1,0:T(8,128)(2,1)S(1)} %get-tuple-element.43.refs_0_), channel_id=1, source_target_pairs={{0,28},{4,0},{8,4},{12,8},{16,12},{20,16},{24,20},{28,24},{1,29},{... | collective-permute-start | bytes 2359304 | tf_op jit(solution)/shard_map/ppermute | solution.py:25
  17.3 15.9 %collective-permute-start.3 = (bf16[512,256]{1,0:T(8,128)(2,1)S(1)}, bf16[512,256]{1,0:T(8,128)(2,1)S(1)}, u32[]{:S(2)}, u32[]{:S(2)}) collective-permute-start(bf16[512,256]{1,0:T(8,128)(2,1)S(1)} %collective-permute-done.refs_0_.refs_2_), channel_id=1, source_target_pairs={{0,1},{1,0},{2,3},{3,2},{4,5},{5,4},{6,7},{7,6},{8,9},{9,8},{10,11... | collective-permute-start | bytes 786440 | tf_op jit(solution)/shard_map/ppermute | solution.py:30
  19.7 13.4 %collective-permute-start.4 = (bf16[512,256]{1,0:T(8,128)(2,1)S(1)}, bf16[512,256]{1,0:T(8,128)(2,1)S(1)}, u32[]{:S(2)}, u32[]{:S(2)}) collective-permute-start(bf16[512,256]{1,0:T(8,128)(2,1)S(1)} %collective-permute-done.refs_0_.refs_2_), channel_id=1, source_target_pairs={{0,8},{4,12},{8,0},{12,4},{16,24},{20,28},{24,16},{28,20},{1,9},{5... | collective-permute-start | bytes 786440 | tf_op jit(solution)/shard_map/ppermute | solution.py:30
  21.2 12.2 %collective-permute-start.5 = (bf16[512,256]{1,0:T(8,128)(2,1)S(1)}, bf16[512,256]{1,0:T(8,128)(2,1)S(1)}, u32[]{:S(2)}, u32[]{:S(2)}) collective-permute-start(bf16[512,256]{1,0:T(8,128)(2,1)S(1)} %collective-permute-done.refs_0_.refs_2_), channel_id=1, source_target_pairs={{0,16},{4,20},{8,24},{12,28},{16,0},{20,4},{24,8},{28,12},{1,17},{... | collective-permute-start | bytes 786440 | tf_op jit(solution)/shard_map/ppermute | solution.py:30
  22.7 10.7 %collective-permute-start.6 = (bf16[512,256]{1,0:T(8,128)(2,1)S(1)}, bf16[512,256]{1,0:T(8,128)(2,1)S(1)}, u32[]{:S(2)}, u32[]{:S(2)}) collective-permute-start(bf16[512,256]{1,0:T(8,128)(2,1)S(1)} %collective-permute-done.refs_0_.refs_2_), channel_id=1, source_target_pairs={{0,25},{1,24},{4,29},{5,28},{8,17},{9,16},{12,21},{13,20},{16,9},{... | collective-permute-start | bytes 786440 | tf_op jit(solution)/shard_map/ppermute | solution.py:39
  33.1 5.1 %collective-permute-start.8 = (bf16[4,2,2,32,256]{4,3,2,1,0:T(8,128)(2,1)S(1)}, bf16[4,2,2,32,256]{4,3,2,1,0:T(8,128)(2,1)S(1)}, u32[]{:S(2)}, u32[]{:S(2)}) collective-permute-start(bf16[4,2,2,32,256]{4,3,2,1,0:T(8,128)(2,1)S(1)} %get-tuple-element.28), channel_id=1, source_target_pairs={{0,4},{4,0},{8,12},{12,8},{16,20},{20,16},{24,28},{28,24},{1,5},{5... | collective-permute-start | bytes 786440 | tf_op jit(solution)/shard_map/ppermute | solution.py:30
  33.4 14.3 %collective-permute-start.10 = (bf16[512,256]{1,0:T(8,128)(2,1)S(1)}, bf16[512,256]{1,0:T(8,128)(2,1)S(1)}, u32[]{:S(2)}, u32[]{:S(2)}) collective-permute-start(bf16[512,256]{1,0:T(8,128)(2,1)S(1)} %collective-permute-done.4.refs_2_.refs_4_), channel_id=1, source_target_pairs={{0,1},{1,0},{2,3},{3,2},{4,5},{5,4},{6,7},{7,6},{8,9},{9,8},{10,11... | collective-permute-start | bytes 786440 | tf_op jit(solution)/shard_map/ppermute | solution.py:30
  35.2 12.5 %collective-permute-start.11 = (bf16[512,256]{1,0:T(8,128)(2,1)S(1)}, bf16[512,256]{1,0:T(8,128)(2,1)S(1)}, u32[]{:S(2)}, u32[]{:S(2)}) collective-permute-start(bf16[512,256]{1,0:T(8,128)(2,1)S(1)} %collective-permute-done.3.refs_1_.refs_3_), channel_id=1, source_target_pairs={{0,16},{4,20},{8,24},{12,28},{16,0},{20,4},{24,8},{28,12},{1,17},{... | collective-permute-start | bytes 786440 | tf_op jit(solution)/shard_map/ppermute | solution.py:30
  36.7 11.0 %collective-permute-start.12 = (bf16[512,256]{1,0:T(8,128)(2,1)S(1)}, bf16[512,256]{1,0:T(8,128)(2,1)S(1)}, u32[]{:S(2)}, u32[]{:S(2)}) collective-permute-start(bf16[512,256]{1,0:T(8,128)(2,1)S(1)} %collective-permute-done.5.refs_3_.refs_5_), channel_id=1, source_target_pairs={{0,8},{4,12},{8,0},{12,4},{16,24},{20,28},{24,16},{28,20},{1,9},{5... | collective-permute-start | bytes 786440 | tf_op jit(solution)/shard_map/ppermute | solution.py:30
  38.3 9.4 %collective-permute-start.9 = (bf16[2,2,2,32,256]{4,3,2,1,0:T(8,128)(2,1)S(1)}, bf16[2,2,2,32,256]{4,3,2,1,0:T(8,128)(2,1)S(1)}, u32[]{:S(2)}, u32[]{:S(2)}) collective-permute-start(bf16[2,2,2,32,256]{4,3,2,1,0:T(8,128)(2,1)S(1)} %get-tuple-element.30), channel_id=1, source_target_pairs={{0,8},{4,12},{8,0},{12,4},{16,24},{20,28},{24,16},{28,20},{1,9},{5... | collective-permute-start | bytes 393224 | tf_op jit(solution)/shard_map/ppermute | solution.py:30
  39.0 13.4 %collective-permute-start.14 = (bf16[4,512,256]{2,1,0:T(8,128)(2,1)S(1)}, bf16[4,512,256]{2,1,0:T(8,128)(2,1)S(1)}, u32[]{:S(2)}, u32[]{:S(2)}) collective-permute-start(bf16[4,512,256]{2,1,0:T(8,128)(2,1)S(1)} %pack_pieces.2), channel_id=1, source_target_pairs={{0,4},{4,0},{8,12},{12,8},{16,20},{20,16},{24,28},{28,24},{1,5},{5... | collective-permute-start | bytes 3145736 | tf_op jit(solution)/shard_map/ppermute | solution.py:30
  47.8 4.6 %collective-permute-start.15 = (bf16[4,512,256]{2,1,0:T(8,128)(2,1)S(1)}, bf16[4,512,256]{2,1,0:T(8,128)(2,1)S(1)}, u32[]{:S(2)}, u32[]{:S(2)}) collective-permute-start(bf16[4,512,256]{2,1,0:T(8,128)(2,1)S(1)} %pack_pieces.3), channel_id=1, source_target_pairs={{0,4},{4,0},{8,12},{12,8},{16,20},{20,16},{24,28},{28,24},{1,5},{5... | collective-permute-start | bytes 3145736 | tf_op jit(solution)/shard_map/ppermute | solution.py:30
  47.9 4.5 %collective-permute-start.13 = (bf16[1,2,2,32,256]{4,3,2,1,0:T(8,128)(2,1)S(1)}, bf16[1,2,2,32,256]{4,3,2,1,0:T(8,128)(2,1)S(1)}, u32[]{:S(2)}, u32[]{:S(2)}) collective-permute-start(bf16[1,2,2,32,256]{4,3,2,1,0:T(8,128)(2,1)S(1)} %get-tuple-element.37), channel_id=1, source_target_pairs={{0,16},{4,20},{8,24},{12,28},{16,0},{20,4},{24,8},{28,12},{1,17},{... | collective-permute-start | bytes 196616 | tf_op jit(solution)/shard_map/ppermute | solution.py:30

commit v7 on v5

--- a/solution.py
+++ b/solution.py
@@ -407,27 +407,31 @@
     link = links[0]
     last = planes - 1
     corner = tuple(range(len(dims)))
-    partial = plane_call(last, (1, 2), vecs[last], None, link, phi)
+    partial = None
+    for plane in range(last):
+        partial = plane_call(plane, (1, 2, 0), vecs[plane], vecs[plane + 1], link, phi, partial)
     held, partial = hold({(): own_piece}, partial)
     stage(held, 1)
     if len(dims) > 2:
         far = diagonal(held[()], n_space, n_op)
-    for plane in range(last):
-        partial = plane_call(plane, (1, 2, 0), vecs[plane], vecs[plane + 1], link, phi, partial)
+    partial = plane_call(last, (1, 2), vecs[last], None, link, phi, partial)
     keep, give = plane_call(last, (0,), vecs[last], upper, link, phi, partial, n_space)
     swapped = across(give, "space", 1)
-    early = list(held)
     if len(dims) > 2:
         held[corner] = far
+    early = list(held)
     held, keep = hold(held, keep)
-    flipped = [across(pack_call([held[key] for key in early]), "space", 1)]
     for size in range(2, len(dims) if len(dims) > 2 else 3):
         stage(held, size)
     late = [key for key in held if key not in early]
+    ready, swapped = hold({key: held[key] for key in early}, swapped)
+    flipped = [across(pack_call(list(ready.values())), "space", 1)]
     merged = merge_call(keep, swapped)
-    got = [merged[0]] + [across(arr, "space", 2 * mask) for mask, arr in enumerate(merged[1:], 1)]
+    flipped, merged = lax.optimization_barrier((flipped, merged))
+    got = [across(merged[mask], "space", 2 * mask) for mask in range(n_space // 2 - 1, 0, -1)]
     after, got = hold({key: held[key] for key in late}, got)
     held.update(after)
+    got.insert(0, merged[0])
     flipped.append(across(pack_call([held[key] for key in late]), "space", 1))
     tau = [held[key] for key in early + late] + flipped
     masks = []

time: 52.9 us -> 52.6 us (level)
  starting transfers between devices: 21.1 us -> 20 us
  waiting for transfers between devices: 9.69 us -> 10.4 us
    ppermute x14, starting transfers between devices: 15.9 us -> 13.2 us  [across(): return lax.ppermute(value, axis, pairs)]
    ppermute x1, starting transfers between devices: 0.01 us -> 2.6 us  [diagonal(): return lax.ppermute(value, ('space', 'op'), pairs)]
    ppermute x2, starting transfers between devices: 5.2 us -> 4.17 us  [from_behind(): return lax.ppermute(value, axis, pairs)]
    ppermute x2, waiting for transfers between devices: 0.15 us -> 0.83 us  [from_behind(): return lax.ppermute(value, axis, pairs)]
  transfers between devices with their start and end apart: 17 -> 17, of which waited for: 8 -> 8; matrix products, arithmetic and copies ran while one was open for 3% -> 6% of each run, Pallas kernels for 31% -> 31%
where the time goes in v7:
time: 52.6 us; the launch traced here: 52.4 us
  starting transfers between devices  20 us (38%)
  Pallas kernels  18.8 us (36%)
  waiting for transfers between devices  10.4 us (20%)
  local copies, waits for them, and re-layouts  3 us (6%)
    pallas_call x3, Pallas kernels, plane_call(): pl.pallas_call(functools.partial(plane_kernel, plane, dirs, part is not N...  15.4 us
    ppermute x14, starting transfers between devices, across(): return lax.ppermute(value, axis, pairs)  13.2 us
    ppermute x14, waiting for transfers between devices, across(): return lax.ppermute(value, axis, pairs)  9.61 us
    ppermute x2, starting transfers between devices, from_behind(): return lax.ppermute(value, axis, pairs)  4.17 us
    unnamed x10, local copies, waits for them, and re-layouts  2.79 us
    ppermute x1, starting transfers between devices, diagonal(): return lax.ppermute(value, ('space', 'op'), pairs)  2.6 us
    pallas_call x1, Pallas kernels, shards(): pl.pallas_call(functools.partial(quark_kernel, masks, n_op, len(got), len...  2.26 us
  transfers between devices with their start and end apart: 17, of which 8 were waited for; matrix products, arithmetic and copies ran while one was open for 6% of the time, Pallas kernels for 31%

profile of v7, /device:TPU:0, one launch (start us, length us, event | category | flops | bytes accessed | tf_op | source)
XLA Modules:
  0.0 52.4 jit_solution(12870633241819736285)
XLA Ops:
  0.0 3.0 %collective-permute-start.1 = (s32[2,3]{1,0:T(2,128)}, s32[2,3]{1,0:T(2,128)S(1)}, u32[]{:S(2)}, u32[]{:S(2)}) collective-permute-start(s32[2,3]{1,0:T(2,128)} %refs_0_.1), channel_id=1, source_target_pairs={{0,1},{1,0},{2,3},{3,2},{4,5},{5,4},{6,7},{7,6},{8,9},{9,8},{10,11... | collective-permute-start | bytes 80 | tf_op jit(solution)/shard_map/ppermute | solution.py:30
  3.1 1.1 %dynamic-slice_bitcast_fusion = bf16[256,1,2,256]{3,2,0,1:T(2,128)(2,1)S(1)} fusion(bf16[256,16,2,256]{3,2,1,0:T(2,128)(2,1)} %bitcast.23, s32[]{:T(128)S(6)} %select_n.14), kind=kLoop, calls=%fused_computation.3 | loop fusion | bytes 524292
  4.2 0.1 reshape.10
  4.3 3.1 %collective-permute-start = (bf16[512,256]{1,0:T(8,128)(2,1)S(1)}, bf16[512,256]{1,0:T(8,128)(2,1)S(1)}, u32[]{:S(2)}, u32[]{:S(2)}) collective-permute-start(bf16[512,256]{1,0:T(8,128)(2,1)S(1)} %reshape.10), channel_id=1, source_target_pairs={{0,2},{2,0},{1,3},{3,1},{4,6},{6,4},{5,7},{7,5},{8,10},{10,8},{9,1... | collective-permute-start | bytes 786440 | tf_op jit(solution)/shard_map/ppermute | solution.py:25
  7.4 1.6 %copy.11 = bf16[1,2,256,3,2,256]{5,2,3,1,4,0:T(8,128)(2,1)S(1)} copy(bf16[1,2,256,3,2,256]{5,4,3,2,1,0:T(2,128)(2,1)} %param.6) | data formatting | bytes 3145728 | tf_op args[0]
  9.1 0.1 slice_bitcast_fusion
  9.2 1.1 %collective-permute-start.7 = (bf16[2,3,256,256]{3,2,1,0:T(8,128)(2,1)S(1)}, bf16[2,3,256,256]{3,2,1,0:T(8,128)(2,1)S(1)}, u32[]{:S(2)}, u32[]{:S(2)}) collective-permute-start(bf16[2,3,256,256]{3,2,1,0:T(8,128)(2,1)S(1)} %get-tuple-element.68.refs_0_), channel_id=1, source_target_pairs={{0,28},{4,0},{8,4},{12,8},{16,12},{20,16},{24,20},{28,24},{1,29},{... | collective-permute-start | bytes 2359304 | tf_op jit(solution)/shard_map/ppermute | solution.py:25
  10.3 0.9 %phases.1.refs_3_.refs_2_ = f32[2,2,3,2,2,256]{5,4,3,2,1,0:T(2,128)S(1)} custom-call(s32[2,3]{1,0:T(2,128)S(1)} %copy-done.1, s32[2,3]{1,0:T(2,128)S(1)} %collective-permute-done.1.refs_1_, s32[3,2,4]{2,1,0:T(2,128)S(1)} %bitcast.18, s32[3,2,4]{2,1,0:T(2,128)S(1)} %collective-permute-done.2.refs_3_, s32[4]{0:T(128)S(1)} %copy-done.2), custom_call_target="tpu_custom_call" | custom-call | tf_op jit(solution)/shard_map/phases/pallas_call | solution.py:383
  11.3 6.6 %plane0_120.1.refs_3_ = f32[2,2,2,256,256]{4,3,2,1,0:T(8,128)S(1)} custom-call(bf16[2,3,256,256]{3,2,1,0:T(8,128)(2,1)S(1)} %get-tuple-element.68.refs_0_, bf16[2,3,256,256]{3,2,1,0:T(8,128)(2,1)S(1)} %get-tuple-element.67.refs_1_.refs_0_, f32[3,3,3,2,2,256]{5,4,3,2,1,0:T(2,128)S(1)} %bitcast.19, f32[2,2,3,2,2,256]{5,4,3,2,1,0:T(2,128)S(1)} %phases.1.refs_3_.refs_2_), custom_call_target="tpu_custom_call" | custom-call | flops 17179869184 | bytes 268435456 | tf_op jit(solution)/shard_map/plane0_120/pallas_call | solution.py:199
  17.9 0.8 %collective-permute-done.refs_0_.refs_4_ = bf16[512,256]{1,0:T(8,128)(2,1)S(1)} collective-permute-done((bf16[512,256]{1,0:T(8,128)(2,1)S(1)}, bf16[512,256]{1,0:T(8,128)(2,1)S(1)}, u32[]{:S(2)}, u32[]{:S(2)}) %collective-permute-start) | collective-permute-done | bytes 262176 | tf_op jit(solution)/shard_map/ppermute | solution.py:25
  18.7 2.6 %collective-permute-start.6 = (bf16[512,256]{1,0:T(8,128)(2,1)S(1)}, bf16[512,256]{1,0:T(8,128)(2,1)S(1)}, u32[]{:S(2)}, u32[]{:S(2)}) collective-permute-start(bf16[512,256]{1,0:T(8,128)(2,1)S(1)} %collective-permute-done.refs_0_.refs_4_), channel_id=1, source_target_pairs={{0,25},{1,24},{4,29},{5,28},{8,17},{9,16},{12,21},{13,20},{16,9},{... | collective-permute-start | bytes 786440 | tf_op jit(solution)/shard_map/ppermute | solution.py:39
  21.3 0.5 collective-permute-start.5
  21.8 0.6 %collective-permute-start.4 = (bf16[512,256]{1,0:T(8,128)(2,1)S(1)}, bf16[512,256]{1,0:T(8,128)(2,1)S(1)}, u32[]{:S(2)}, u32[]{:S(2)}) collective-permute-start(bf16[512,256]{1,0:T(8,128)(2,1)S(1)} %collective-permute-done.refs_0_.refs_4_), channel_id=1, source_target_pairs={{0,8},{4,12},{8,0},{12,4},{16,24},{20,28},{24,16},{28,20},{1,9},{5... | collective-permute-start | bytes 786440 | tf_op jit(solution)/shard_map/ppermute | solution.py:30
  22.5 1.2 %collective-permute-start.3 = (bf16[512,256]{1,0:T(8,128)(2,1)S(1)}, bf16[512,256]{1,0:T(8,128)(2,1)S(1)}, u32[]{:S(2)}, u32[]{:S(2)}) collective-permute-start(bf16[512,256]{1,0:T(8,128)(2,1)S(1)} %collective-permute-done.refs_0_.refs_4_), channel_id=1, source_target_pairs={{0,1},{1,0},{2,3},{3,2},{4,5},{5,4},{6,7},{7,6},{8,9},{9,8},{10,11... | collective-permute-start | bytes 786440 | tf_op jit(solution)/shard_map/ppermute | solution.py:30
  23.7 5.2 %plane1_12.1.refs_4_ = f32[2,2,2,256,256]{4,3,2,1,0:T(8,128)S(1)} custom-call(bf16[2,3,256,256]{3,2,1,0:T(8,128)(2,1)S(1)} %get-tuple-element.67.refs_1_.refs_0_, f32[3,3,3,2,2,256]{5,4,3,2,1,0:T(2,128)S(1)} %bitcast.20, f32[2,2,3,2,2,256]{5,4,3,2,1,0:T(2,128)S(1)} %phases.1.refs_3_.refs_2_, f32[2,2,2,256,256]{4,3,2,1,0:T(8,128)S(1)} %plane0_120.1.refs_3_), custom_call_target="tpu_custom_call" | custom-call | flops 17179869184 | bytes 268435456 | tf_op jit(solution)/shard_map/plane1_12/pallas_call | solution.py:199
  28.9 3.5 %plane1_0.1 = (f32[4,2,2,32,256]{4,3,2,1,0:T(8,128)S(1)}, bf16[4,2,2,32,256]{4,3,2,1,0:T(8,128)(2,1)S(1)}) custom-call(bf16[2,3,256,256]{3,2,1,0:T(8,128)(2,1)S(1)} %get-tuple-element.67.refs_1_.refs_0_, bf16[2,3,256,256]{3,2,1,0:T(8,128)(2,1)S(1)} %collective-permute-done.7.refs_1_, f32[3,3,3,2,2,256]{5,4,3,2,1,0:T(2,128)S(1)} %bitcast.21, ...), custom_call_target="tpu_custom_call" | custom-call | flops 17179869184 | bytes 268435456 | tf_op jit(solution)/shard_map/plane1_0/pallas_call | solution.py:199
  32.5 0.9 %collective-permute-done.5.refs_3_.refs_7_ = bf16[512,256]{1,0:T(8,128)(2,1)S(1)} collective-permute-done((bf16[512,256]{1,0:T(8,128)(2,1)S(1)}, bf16[512,256]{1,0:T(8,128)(2,1)S(1)}, u32[]{:S(2)}, u32[]{:S(2)}) %collective-permute-start.5) | collective-permute-done | bytes 262176 | tf_op jit(solution)/shard_map/ppermute | solution.py:30
  33.5 0.6 %collective-permute-done.8.got_ref = bf16[4,2,2,32,256]{4,3,2,1,0:T(8,128)(2,1)S(1)} collective-permute-done((bf16[4,2,2,32,256]{4,3,2,1,0:T(8,128)(2,1)S(1)}, bf16[4,2,2,32,256]{4,3,2,1,0:T(8,128)(2,1)S(1)}, u32[]{:S(2)}, u32[]{:S(2)}) %collective-permute-start.8) | collective-permute-done | bytes 262176 | tf_op jit(solution)/shard_map/ppermute | solution.py:30
  34.0 0.1 pack_pieces.2
  34.1 0.2 collective-permute-start.9
  34.3 1.6 %collective-permute-start.11 = (bf16[512,256]{1,0:T(8,128)(2,1)S(1)}, bf16[512,256]{1,0:T(8,128)(2,1)S(1)}, u32[]{:S(2)}, u32[]{:S(2)}) collective-permute-start(bf16[512,256]{1,0:T(8,128)(2,1)S(1)} %collective-permute-done.3.refs_1_.refs_5_), channel_id=1, source_target_pairs={{0,16},{4,20},{8,24},{12,28},{16,0},{20,4},{24,8},{28,12},{1,17},{... | collective-permute-start | bytes 786440 | tf_op jit(solution)/shard_map/ppermute | solution.py:30
  35.9 0.7 %collective-permute-start.10 = (bf16[512,256]{1,0:T(8,128)(2,1)S(1)}, bf16[512,256]{1,0:T(8,128)(2,1)S(1)}, u32[]{:S(2)}, u32[]{:S(2)}) collective-permute-start(bf16[512,256]{1,0:T(8,128)(2,1)S(1)} %collective-permute-done.4.refs_2_.refs_6_), channel_id=1, source_target_pairs={{0,1},{1,0},{2,3},{3,2},{4,5},{5,4},{6,7},{7,6},{8,9},{9,8},{10,11... | collective-permute-start | bytes 786440 | tf_op jit(solution)/shard_map/ppermute | solution.py:30
  36.6 1.5 %collective-permute-start.12 = (bf16[512,256]{1,0:T(8,128)(2,1)S(1)}, bf16[512,256]{1,0:T(8,128)(2,1)S(1)}, u32[]{:S(2)}, u32[]{:S(2)}) collective-permute-start(bf16[512,256]{1,0:T(8,128)(2,1)S(1)} %collective-permute-done.5.refs_3_.refs_7_), channel_id=1, source_target_pairs={{0,8},{4,12},{8,0},{12,4},{16,24},{20,28},{24,16},{28,20},{1,9},{5... | collective-permute-start | bytes 786440 | tf_op jit(solution)/shard_map/ppermute | solution.py:30
  38.1 1.6 %collective-permute-start.13 = (bf16[128,256]{1,0:T(8,128)(2,1)S(1)}, bf16[128,256]{1,0:T(8,128)(2,1)S(1)}, u32[]{:S(2)}, u32[]{:S(2)}) collective-permute-start(bf16[128,256]{1,0:T(8,128)(2,1)S(1)} %get-tuple-element.57), channel_id=1, source_target_pairs={{0,24},{4,28},{8,16},{12,20},{16,8},{20,12},{24,0},{28,4},{1,25},{... | collective-permute-start | bytes 196616 | tf_op jit(solution)/shard_map/ppermute | solution.py:30
  39.7 0.5 collective-permute-start.14
  40.2 3.2 %collective-permute-done.11.refs_1_.refs_10_ = bf16[512,256]{1,0:T(8,128)(2,1)S(1)} collective-permute-done((bf16[512,256]{1,0:T(8,128)(2,1)S(1)}, bf16[512,256]{1,0:T(8,128)(2,1)S(1)}, u32[]{:S(2)}, u32[]{:S(2)}) %collective-permute-start.11) | collective-permute-done | bytes 262176 | tf_op jit(solution)/shard_map/ppermute | solution.py:30
  43.5 1.7 %collective-permute-start.15 = (bf16[128,256]{1,0:T(8,128)(2,1)S(1)}, bf16[128,256]{1,0:T(8,128)(2,1)S(1)}, u32[]{:S(2)}, u32[]{:S(2)}) collective-permute-start(bf16[128,256]{1,0:T(8,128)(2,1)S(1)} %get-tuple-element.59), channel_id=1, source_target_pairs={{0,8},{4,12},{8,0},{12,4},{16,24},{20,28},{24,16},{28,20},{1,9},{5... | collective-permute-start | bytes 196616 | tf_op jit(solution)/shard_map/ppermute | solution.py:30
  45.2 0.3 collective-permute-done.12.refs_2_.refs_11_
  45.5 1.3 %collective-permute-done.13.refs_1_ = bf16[128,256]{1,0:T(8,128)(2,1)S(1)} collective-permute-done((bf16[128,256]{1,0:T(8,128)(2,1)S(1)}, bf16[128,256]{1,0:T(8,128)(2,1)S(1)}, u32[]{:S(2)}, u32[]{:S(2)}) %collective-permute-start.13) | collective-permute-done | bytes 65568 | tf_op jit(solution)/shard_map/ppermute | solution.py:30
  46.7 1.0 %collective-permute-done.15.refs_3_ = bf16[128,256]{1,0:T(8,128)(2,1)S(1)} collective-permute-done((bf16[128,256]{1,0:T(8,128)(2,1)S(1)}, bf16[128,256]{1,0:T(8,128)(2,1)S(1)}, u32[]{:S(2)}, u32[]{:S(2)}) %collective-permute-start.15) | collective-permute-done | bytes 65568 | tf_op jit(solution)/shard_map/ppermute | solution.py:30
  47.9 2.3 %collective-permute-done.16.refs_13_ = bf16[3,512,256]{2,1,0:T(8,128)(2,1)S(1)} collective-permute-done((bf16[3,512,256]{2,1,0:T(8,128)(2,1)S(1)}, bf16[3,512,256]{2,1,0:T(8,128)(2,1)S(1)}, u32[]{:S(2)}, u32[]{:S(2)}) %collective-permute-start.16) | collective-permute-done | bytes 786464 | tf_op jit(solution)/shard_map/ppermute | solution.py:30
  50.1 2.3 %quark_products.1 = f32[2,16,2,32,256]{4,3,2,1,0:T(8,128)} custom-call(f32[128,256]{1,0:T(8,128)S(1)} %get-tuple-element.56.refs_0_, bf16[128,256]{1,0:T(8,128)(2,1)S(1)} %collective-permute-done.13.refs_1_, bf16[128,256]{1,0:T(8,128)(2,1)S(1)} %collective-permute-done.14.refs_2_, bf16[128,256]{1,0:T(8,128)(2,1)S(1)} %collective-permute-done.15.refs_3_, ...), custom_call_target="tpu_custom_call" | custom-call | flops 536870912 | bytes 7340032 | tf_op jit(solution)/shard_map/quark_products/pallas_call | solution.py:445
  (22 shorter events, 0.4 us)
Async XLA Ops:
  0.0 10.3 %collective-permute-start.1 = (s32[2,3]{1,0:T(2,128)}, s32[2,3]{1,0:T(2,128)S(1)}, u32[]{:S(2)}, u32[]{:S(2)}) collective-permute-start(s32[2,3]{1,0:T(2,128)} %refs_0_.1), channel_id=1, source_target_pairs={{0,1},{1,0},{2,3},{3,2},{4,5},{5,4},{6,7},{7,6},{8,9},{9,8},{10,11... | collective-permute-start | bytes 80 | tf_op jit(solution)/shard_map/ppermute | solution.py:30
  3.0 7.3 %collective-permute-start.2 = (s32[3,2,4]{2,1,0:T(2,128)}, s32[3,2,4]{2,1,0:T(2,128)S(1)}, u32[]{:S(2)}, u32[]{:S(2)}) collective-permute-start(s32[3,2,4]{2,1,0:T(2,128)} %bitcast.17), channel_id=1, source_target_pairs={{0,1},{1,0},{2,3},{3,2},{4,5},{5,4},{6,7},{7,6},{8,9},{9,8},{10,11... | collective-permute-start | bytes 296 | tf_op jit(solution)/shard_map/ppermute | solution.py:30
  4.3 14.4 %collective-permute-start = (bf16[512,256]{1,0:T(8,128)(2,1)S(1)}, bf16[512,256]{1,0:T(8,128)(2,1)S(1)}, u32[]{:S(2)}, u32[]{:S(2)}) collective-permute-start(bf16[512,256]{1,0:T(8,128)(2,1)S(1)} %reshape.10), channel_id=1, source_target_pairs={{0,2},{2,0},{1,3},{3,1},{4,6},{6,4},{5,7},{7,5},{8,10},{10,8},{9,1... | collective-permute-start | bytes 786440 | tf_op jit(solution)/shard_map/ppermute | solution.py:25
  9.0 1.3 %copy-start = (s32[4,2,3]{0,1,2:T(2,128)S(1)}, s32[4,2,3]{0,1,2:T(2,128)}, u32[]{:S(2)}) copy-start(s32[4,2,3]{0,1,2:T(2,128)} %param.9) | copy-start | bytes 292
  9.0 1.3 %copy-start.1 = (s32[2,3]{1,0:T(2,128)S(1)}, s32[2,3]{1,0:T(2,128)}, u32[]{:S(2)}) copy-start(s32[2,3]{1,0:T(2,128)} %refs_0_.1) | copy-start | bytes 76
  9.0 1.3 %copy-start.2 = (s32[4]{0:T(128)S(1)}, s32[4]{0:T(128)}, u32[]{:S(2)}) copy-start(s32[4]{0:T(128)} %refs_4_.1) | copy-start | bytes 52
  9.1 2.2 %copy-start.3 = (f32[1,3,3,3,2,2,256]{6,5,4,3,2,1,0:T(2,128)S(1)}, f32[1,3,3,3,2,2,256]{6,5,4,3,2,1,0:T(2,128)}, u32[]{:S(2)}) copy-start(f32[1,3,3,3,2,2,256]{6,5,4,3,2,1,0:T(2,128)} %param.7) | copy-start | bytes 331780
  9.2 19.7 %collective-permute-start.7 = (bf16[2,3,256,256]{3,2,1,0:T(8,128)(2,1)S(1)}, bf16[2,3,256,256]{3,2,1,0:T(8,128)(2,1)S(1)}, u32[]{:S(2)}, u32[]{:S(2)}) collective-permute-start(bf16[2,3,256,256]{3,2,1,0:T(8,128)(2,1)S(1)} %get-tuple-element.68.refs_0_), channel_id=1, source_target_pairs={{0,28},{4,0},{8,4},{12,8},{16,12},{20,16},{24,20},{28,24},{1,29},{... | collective-permute-start | bytes 2359304 | tf_op jit(solution)/shard_map/ppermute | solution.py:25
  18.7 13.8 %collective-permute-start.6 = (bf16[512,256]{1,0:T(8,128)(2,1)S(1)}, bf16[512,256]{1,0:T(8,128)(2,1)S(1)}, u32[]{:S(2)}, u32[]{:S(2)}) collective-permute-start(bf16[512,256]{1,0:T(8,128)(2,1)S(1)} %collective-permute-done.refs_0_.refs_4_), channel_id=1, source_target_pairs={{0,25},{1,24},{4,29},{5,28},{8,17},{9,16},{12,21},{13,20},{16,9},{... | collective-permute-start | bytes 786440 | tf_op jit(solution)/shard_map/ppermute | solution.py:39
  21.3 12.1 %collective-permute-start.5 = (bf16[512,256]{1,0:T(8,128)(2,1)S(1)}, bf16[512,256]{1,0:T(8,128)(2,1)S(1)}, u32[]{:S(2)}, u32[]{:S(2)}) collective-permute-start(bf16[512,256]{1,0:T(8,128)(2,1)S(1)} %collective-permute-done.refs_0_.refs_4_), channel_id=1, source_target_pairs={{0,16},{4,20},{8,24},{12,28},{16,0},{20,4},{24,8},{28,12},{1,17},{... | collective-permute-start | bytes 786440 | tf_op jit(solution)/shard_map/ppermute | solution.py:30
  21.8 11.6 %collective-permute-start.4 = (bf16[512,256]{1,0:T(8,128)(2,1)S(1)}, bf16[512,256]{1,0:T(8,128)(2,1)S(1)}, u32[]{:S(2)}, u32[]{:S(2)}) collective-permute-start(bf16[512,256]{1,0:T(8,128)(2,1)S(1)} %collective-permute-done.refs_0_.refs_4_), channel_id=1, source_target_pairs={{0,8},{4,12},{8,0},{12,4},{16,24},{20,28},{24,16},{28,20},{1,9},{5... | collective-permute-start | bytes 786440 | tf_op jit(solution)/shard_map/ppermute | solution.py:30
  22.5 11.0 %collective-permute-start.3 = (bf16[512,256]{1,0:T(8,128)(2,1)S(1)}, bf16[512,256]{1,0:T(8,128)(2,1)S(1)}, u32[]{:S(2)}, u32[]{:S(2)}) collective-permute-start(bf16[512,256]{1,0:T(8,128)(2,1)S(1)} %collective-permute-done.refs_0_.refs_4_), channel_id=1, source_target_pairs={{0,1},{1,0},{2,3},{3,2},{4,5},{5,4},{6,7},{7,6},{8,9},{9,8},{10,11... | collective-permute-start | bytes 786440 | tf_op jit(solution)/shard_map/ppermute | solution.py:30
  32.4 1.6 %collective-permute-start.8 = (bf16[4,2,2,32,256]{4,3,2,1,0:T(8,128)(2,1)S(1)}, bf16[4,2,2,32,256]{4,3,2,1,0:T(8,128)(2,1)S(1)}, u32[]{:S(2)}, u32[]{:S(2)}) collective-permute-start(bf16[4,2,2,32,256]{4,3,2,1,0:T(8,128)(2,1)S(1)} %get-tuple-element.44), channel_id=1, source_target_pairs={{0,4},{4,0},{8,12},{12,8},{16,20},{20,16},{24,28},{28,24},{1,5},{5... | collective-permute-start | bytes 786440 | tf_op jit(solution)/shard_map/ppermute | solution.py:30
  34.1 4.0 %collective-permute-start.9 = (bf16[5,512,256]{2,1,0:T(8,128)(2,1)S(1)}, bf16[5,512,256]{2,1,0:T(8,128)(2,1)S(1)}, u32[]{:S(2)}, u32[]{:S(2)}) collective-permute-start(bf16[5,512,256]{2,1,0:T(8,128)(2,1)S(1)} %pack_pieces.2), channel_id=1, source_target_pairs={{0,4},{4,0},{8,12},{12,8},{16,20},{20,16},{24,28},{28,24},{1,5},{5... | collective-permute-start | bytes 3932168 | tf_op jit(solution)/shard_map/ppermute | solution.py:30
  34.3 9.1 %collective-permute-start.11 = (bf16[512,256]{1,0:T(8,128)(2,1)S(1)}, bf16[512,256]{1,0:T(8,128)(2,1)S(1)}, u32[]{:S(2)}, u32[]{:S(2)}) collective-permute-start(bf16[512,256]{1,0:T(8,128)(2,1)S(1)} %collective-permute-done.3.refs_1_.refs_5_), channel_id=1, source_target_pairs={{0,16},{4,20},{8,24},{12,28},{16,0},{20,4},{24,8},{28,12},{1,17},{... | collective-permute-start | bytes 786440 | tf_op jit(solution)/shard_map/ppermute | solution.py:30
  35.9 9.2 %collective-permute-start.10 = (bf16[512,256]{1,0:T(8,128)(2,1)S(1)}, bf16[512,256]{1,0:T(8,128)(2,1)S(1)}, u32[]{:S(2)}, u32[]{:S(2)}) collective-permute-start(bf16[512,256]{1,0:T(8,128)(2,1)S(1)} %collective-permute-done.4.refs_2_.refs_6_), channel_id=1, source_target_pairs={{0,1},{1,0},{2,3},{3,2},{4,5},{5,4},{6,7},{7,6},{8,9},{9,8},{10,11... | collective-permute-start | bytes 786440 | tf_op jit(solution)/shard_map/ppermute | solution.py:30
  36.6 8.9 %collective-permute-start.12 = (bf16[512,256]{1,0:T(8,128)(2,1)S(1)}, bf16[512,256]{1,0:T(8,128)(2,1)S(1)}, u32[]{:S(2)}, u32[]{:S(2)}) collective-permute-start(bf16[512,256]{1,0:T(8,128)(2,1)S(1)} %collective-permute-done.5.refs_3_.refs_7_), channel_id=1, source_target_pairs={{0,8},{4,12},{8,0},{12,4},{16,24},{20,28},{24,16},{28,20},{1,9},{5... | collective-permute-start | bytes 786440 | tf_op jit(solution)/shard_map/ppermute | solution.py:30
  38.1 8.6 %collective-permute-start.13 = (bf16[128,256]{1,0:T(8,128)(2,1)S(1)}, bf16[128,256]{1,0:T(8,128)(2,1)S(1)}, u32[]{:S(2)}, u32[]{:S(2)}) collective-permute-start(bf16[128,256]{1,0:T(8,128)(2,1)S(1)} %get-tuple-element.57), channel_id=1, source_target_pairs={{0,24},{4,28},{8,16},{12,20},{16,8},{20,12},{24,0},{28,4},{1,25},{... | collective-permute-start | bytes 196616 | tf_op jit(solution)/shard_map/ppermute | solution.py:30
  39.7 7.0 %collective-permute-start.14 = (bf16[128,256]{1,0:T(8,128)(2,1)S(1)}, bf16[128,256]{1,0:T(8,128)(2,1)S(1)}, u32[]{:S(2)}, u32[]{:S(2)}) collective-permute-start(bf16[128,256]{1,0:T(8,128)(2,1)S(1)} %get-tuple-element.58), channel_id=1, source_target_pairs={{0,16},{4,20},{8,24},{12,28},{16,0},{20,4},{24,8},{28,12},{1,17},{... | collective-permute-start | bytes 196616 | tf_op jit(solution)/shard_map/ppermute | solution.py:30
  43.5 4.3 %collective-permute-start.15 = (bf16[128,256]{1,0:T(8,128)(2,1)S(1)}, bf16[128,256]{1,0:T(8,128)(2,1)S(1)}, u32[]{:S(2)}, u32[]{:S(2)}) collective-permute-start(bf16[128,256]{1,0:T(8,128)(2,1)S(1)} %get-tuple-element.59), channel_id=1, source_target_pairs={{0,8},{4,12},{8,0},{12,4},{16,24},{20,28},{24,16},{28,20},{1,9},{5... | collective-permute-start | bytes 196616 | tf_op jit(solution)/shard_map/ppermute | solution.py:30
  47.8 2.4 %collective-permute-start.16 = (bf16[3,512,256]{2,1,0:T(8,128)(2,1)S(1)}, bf16[3,512,256]{2,1,0:T(8,128)(2,1)S(1)}, u32[]{:S(2)}, u32[]{:S(2)}) collective-permute-start(bf16[3,512,256]{2,1,0:T(8,128)(2,1)S(1)} %pack_pieces.3), channel_id=1, source_target_pairs={{0,4},{4,0},{8,12},{12,8},{16,20},{20,16},{24,28},{28,24},{1,5},{5... | collective-permute-start | bytes 2359304 | tf_op jit(solution)/shard_map/ppermute | solution.py:30

commit v8 on v7

--- a/solution.py
+++ b/solution.py
@@ -255,12 +255,10 @@
     )(*arrs)
 
 
-def quark_kernel(masks, n_op, n_got, n_tau, n_h, *refs):
-    got_refs = refs[:n_got]
-    tau_refs = refs[n_got : n_got + n_tau]
-    out_ref, left_ref = refs[n_got + n_tau :]
-    my_space, my_op = lax.axis_index("space"), lax.axis_index("op")
-    _, n_pair, _, own, n_b = out_ref.shape
+def left_kernel(n_h, *refs):
+    got_refs, left_ref = refs[:-1], refs[-1]
+    rows, n_b = got_refs[0].shape
+    own = rows // (2 * n_h)
     row = lax.broadcasted_iota(jnp.int32, (n_b, 2 * n_b), 0)
     col = lax.broadcasted_iota(jnp.int32, (n_b, 2 * n_b), 1)
     even = (col == 2 * row).astype(jnp.bfloat16)
@@ -277,6 +275,26 @@
         jnp.concatenate(swap, 0).astype(jnp.bfloat16), odd, preferred_element_type=jnp.float32
     )
     left_ref[...] = left.astype(jnp.bfloat16)
+
+
+def left_call(got, n_h):
+    rows, n_b = got[0].shape
+    vmem = pl.BlockSpec(memory_space=pltpu.VMEM)
+    return pl.pallas_call(
+        functools.partial(left_kernel, n_h),
+        in_specs=[vmem] * len(got),
+        out_specs=vmem,
+        out_shape=jax.ShapeDtypeStruct((rows, 2 * n_b), jnp.bfloat16),
+        compiler_params=pltpu.CompilerParams(vmem_limit_bytes=8 * 2**20),
+        cost_estimate=pl.CostEstimate(flops=2**34, bytes_accessed=2**24, transcendentals=0),
+        name="left_operand",
+    )(*got)
+
+
+def quark_kernel(masks, n_op, left_ref, *refs):
+    tau_refs, out_ref = refs[:-1], refs[-1]
+    my_space, my_op = lax.axis_index("space"), lax.axis_index("op")
+    n_h, n_pair, _, own, n_b = out_ref.shape
     tau = []
     for ref in tau_refs:
         tau += [ref.at[which] for which in range(ref.shape[0])] if len(ref.shape) == 3 else [ref]
@@ -407,14 +425,13 @@
     link = links[0]
     last = planes - 1
     corner = tuple(range(len(dims)))
-    partial = None
-    for plane in range(last):
-        partial = plane_call(plane, (1, 2, 0), vecs[plane], vecs[plane + 1], link, phi, partial)
+    partial = plane_call(last, (1, 2), vecs[last], None, link, phi)
     held, partial = hold({(): own_piece}, partial)
     stage(held, 1)
     if len(dims) > 2:
         far = diagonal(held[()], n_space, n_op)
-    partial = plane_call(last, (1, 2), vecs[last], None, link, phi, partial)
+    for plane in range(last):
+        partial = plane_call(plane, (1, 2, 0), vecs[plane], vecs[plane + 1], link, phi, partial)
     keep, give = plane_call(last, (0,), vecs[last], upper, link, phi, partial, n_space)
     swapped = across(give, "space", 1)
     if len(dims) > 2:
@@ -429,8 +446,6 @@
     merged = merge_call(keep, swapped)
     flipped, merged = lax.optimization_barrier((flipped, merged))
     got = [across(merged[mask], "space", 2 * mask) for mask in range(n_space // 2 - 1, 0, -1)]
-    after, got = hold({key: held[key] for key in late}, got)
-    held.update(after)
     got.insert(0, merged[0])
     flipped.append(across(pack_call([held[key] for key in late]), "space", 1))
     tau = [held[key] for key in early + late] + flipped
@@ -443,19 +458,16 @@
             masks.append((mask["space"], mask["op"]))
 
     lines = pl.pallas_call(
-        functools.partial(quark_kernel, masks, n_op, len(got), len(tau), n_h),
-        in_specs=[vmem] * (len(got) + len(tau)),
+        functools.partial(quark_kernel, masks, n_op),
+        in_specs=[vmem] * (1 + len(tau)),
         out_specs=vmem,
         out_shape=jax.ShapeDtypeStruct((n_h, SPINS, 2, own, n_b), jnp.float32),
-        scratch_shapes=[
-            pltpu.VMEM((n_h * 2 * own, 2 * n_b), jnp.bfloat16),
-        ],
         compiler_params=pltpu.CompilerParams(vmem_limit_bytes=VMEM_BYTES),
         cost_estimate=pl.CostEstimate(
             flops=2 * SPINS * n_h * 2 * own * 2 * n_b * n_b, bytes_accessed=7 * 2**20, transcendentals=0
         ),
         name="quark_products",
-    )(*got, *tau)
+    )(left_call(got, n_h), *tau)
     return lines.reshape(1, n_h, 4, 4, 2, own, n_b)
 
 

time: 52.6 us -> 52.2 us (level)
  waiting for transfers between devices: 10.4 us -> 8.52 us
  starting transfers between devices: 20 us -> 21.5 us
    ppermute x14, starting transfers between devices: 13.2 us -> 16.3 us  [across(): return lax.ppermute(value, axis, pairs)]
    ppermute x1, starting transfers between devices: 2.6 us -> 0.01 us  [diagonal(): return lax.ppermute(value, ('space', 'op'), pairs)]
    ppermute x14, waiting for transfers between devices: 9.61 us -> 8.37 us  [across(): return lax.ppermute(value, axis, pairs)]
    ppermute x2, starting transfers between devices: 4.17 us -> 5.2 us  [from_behind(): return lax.ppermute(value, axis, pairs)]
    ppermute x2, waiting for transfers between devices: 0.83 us -> 0.15 us  [from_behind(): return lax.ppermute(value, axis, pairs)]
    pallas_call x1 -> x2, Pallas kernels: 2.26 us -> 2.3 us  [the longest x1 2.05 us: shards(): pl.pallas_call(functools.partial(quark_kernel, masks, n_op), in_specs=[vm...]
  transfers between devices with their start and end apart: 17 -> 17, of which waited for: 8 -> 10; matrix products, arithmetic and copies ran while one was open for 6% -> 3% of each run, Pallas kernels for 31% -> 32%
where the time goes in v8:
time: 52.2 us; the launch traced here: 52.1 us
  starting transfers between devices  21.5 us (41%)
  Pallas kernels  18.8 us (36%)
  waiting for transfers between devices  8.52 us (16%)
  local copies, waits for them, and re-layouts  3 us (6%)
    ppermute x14, starting transfers between devices, across(): return lax.ppermute(value, axis, pairs)  16.3 us
    pallas_call x3, Pallas kernels, plane_call(): pl.pallas_call(functools.partial(plane_kernel, plane, dirs, part is not N...  15.4 us
    ppermute x14, waiting for transfers between devices, across(): return lax.ppermute(value, axis, pairs)  8.37 us
    ppermute x2, starting transfers between devices, from_behind(): return lax.ppermute(value, axis, pairs)  5.2 us
    unnamed x10, local copies, waits for them, and re-layouts  2.79 us
    pallas_call x1, Pallas kernels, shards(): pl.pallas_call(functools.partial(quark_kernel, masks, n_op), in_specs=[vm...  2.05 us
  transfers between devices with their start and end apart: 17, of which 10 were waited for; matrix products, arithmetic and copies ran while one was open for 3% of the time, Pallas kernels for 32%

profile of v8, /device:TPU:0, one launch (start us, length us, event | category | flops | bytes accessed | tf_op | source)
XLA Modules:
  0.0 52.1 jit_solution(10031126967323811207)
XLA Ops:
  0.0 1.1 %dynamic-slice_bitcast_fusion = bf16[256,1,2,256]{3,2,0,1:T(2,128)(2,1)S(1)} fusion(bf16[256,16,2,256]{3,2,1,0:T(2,128)(2,1)} %bitcast.23, s32[]{:T(128)S(6)} %select_n.14), kind=kLoop, calls=%fused_computation.3 | loop fusion | bytes 524292
  1.2 4.1 %collective-permute-start = (bf16[512,256]{1,0:T(8,128)(2,1)S(1)}, bf16[512,256]{1,0:T(8,128)(2,1)S(1)}, u32[]{:S(2)}, u32[]{:S(2)}) collective-permute-start(bf16[512,256]{1,0:T(8,128)(2,1)S(1)} %reshape.10), channel_id=1, source_target_pairs={{0,2},{2,0},{1,3},{3,1},{4,6},{6,4},{5,7},{7,5},{8,10},{10,8},{9,1... | collective-permute-start | bytes 786440 | tf_op jit(solution)/shard_map/ppermute | solution.py:25
  5.3 1.6 %collective-permute-start.2 = (s32[3,2,4]{2,1,0:T(2,128)}, s32[3,2,4]{2,1,0:T(2,128)S(1)}, u32[]{:S(2)}, u32[]{:S(2)}) collective-permute-start(s32[3,2,4]{2,1,0:T(2,128)} %bitcast.17), channel_id=1, source_target_pairs={{0,1},{1,0},{2,3},{3,2},{4,5},{5,4},{6,7},{7,6},{8,9},{9,8},{10,11... | collective-permute-start | bytes 296 | tf_op jit(solution)/shard_map/ppermute | solution.py:30
  6.9 0.4 collective-permute-start.1
  7.4 1.6 %copy.11 = bf16[1,2,256,3,2,256]{5,2,3,1,4,0:T(8,128)(2,1)S(1)} copy(bf16[1,2,256,3,2,256]{5,4,3,2,1,0:T(2,128)(2,1)} %param.6) | data formatting | bytes 3145728 | tf_op args[0]
  9.2 1.1 %collective-permute-start.7 = (bf16[2,3,256,256]{3,2,1,0:T(8,128)(2,1)S(1)}, bf16[2,3,256,256]{3,2,1,0:T(8,128)(2,1)S(1)}, u32[]{:S(2)}, u32[]{:S(2)}) collective-permute-start(bf16[2,3,256,256]{3,2,1,0:T(8,128)(2,1)S(1)} %get-tuple-element.55.refs_0_), channel_id=1, source_target_pairs={{0,28},{4,0},{8,4},{12,8},{16,12},{20,16},{24,20},{28,24},{1,29},{... | collective-permute-start | bytes 2359304 | tf_op jit(solution)/shard_map/ppermute | solution.py:25
  10.3 0.8 %collective-permute-done.1.refs_1_ = s32[2,3]{1,0:T(2,128)S(1)} collective-permute-done((s32[2,3]{1,0:T(2,128)}, s32[2,3]{1,0:T(2,128)S(1)}, u32[]{:S(2)}, u32[]{:S(2)}) %collective-permute-start.1) | collective-permute-done | bytes 56 | tf_op jit(solution)/shard_map/ppermute | solution.py:30
  11.1 0.9 %phases.1.refs_2_.refs_3_ = f32[2,2,3,2,2,256]{5,4,3,2,1,0:T(2,128)S(1)} custom-call(s32[2,3]{1,0:T(2,128)S(1)} %copy-done.1, s32[2,3]{1,0:T(2,128)S(1)} %collective-permute-done.1.refs_1_, s32[3,2,4]{2,1,0:T(2,128)S(1)} %bitcast.18, s32[3,2,4]{2,1,0:T(2,128)S(1)} %collective-permute-done.2.refs_3_, s32[4]{0:T(128)S(1)} %copy-done.2), custom_call_target="tpu_custom_call" | custom-call | tf_op jit(solution)/shard_map/phases/pallas_call | solution.py:401
  12.0 5.1 %plane1_12.1.refs_4_ = f32[2,2,2,256,256]{4,3,2,1,0:T(8,128)S(1)} custom-call(bf16[2,3,256,256]{3,2,1,0:T(8,128)(2,1)S(1)} %get-tuple-element.56.refs_0_.refs_1_, f32[3,3,3,2,2,256]{5,4,3,2,1,0:T(2,128)S(1)} %bitcast.19, f32[2,2,3,2,2,256]{5,4,3,2,1,0:T(2,128)S(1)} %phases.1.refs_2_.refs_3_), custom_call_target="tpu_custom_call" | custom-call | flops 17179869184 | bytes 268435456 | tf_op jit(solution)/shard_map/plane1_12/pallas_call | solution.py:199
  17.1 0.1 collective-permute-done.refs_0_
  17.3 2.4 %collective-permute-start.3 = (bf16[512,256]{1,0:T(8,128)(2,1)S(1)}, bf16[512,256]{1,0:T(8,128)(2,1)S(1)}, u32[]{:S(2)}, u32[]{:S(2)}) collective-permute-start(bf16[512,256]{1,0:T(8,128)(2,1)S(1)} %collective-permute-done.refs_0_), channel_id=1, source_target_pairs={{0,1},{1,0},{2,3},{3,2},{4,5},{5,4},{6,7},{7,6},{8,9},{9,8},{10,11... | collective-permute-start | bytes 786440 | tf_op jit(solution)/shard_map/ppermute | solution.py:30
  19.7 1.5 %collective-permute-start.4 = (bf16[512,256]{1,0:T(8,128)(2,1)S(1)}, bf16[512,256]{1,0:T(8,128)(2,1)S(1)}, u32[]{:S(2)}, u32[]{:S(2)}) collective-permute-start(bf16[512,256]{1,0:T(8,128)(2,1)S(1)} %collective-permute-done.refs_0_), channel_id=1, source_target_pairs={{0,8},{4,12},{8,0},{12,4},{16,24},{20,28},{24,16},{28,20},{1,9},{5... | collective-permute-start | bytes 786440 | tf_op jit(solution)/shard_map/ppermute | solution.py:30
  21.2 1.5 %collective-permute-start.5 = (bf16[512,256]{1,0:T(8,128)(2,1)S(1)}, bf16[512,256]{1,0:T(8,128)(2,1)S(1)}, u32[]{:S(2)}, u32[]{:S(2)}) collective-permute-start(bf16[512,256]{1,0:T(8,128)(2,1)S(1)} %collective-permute-done.refs_0_), channel_id=1, source_target_pairs={{0,16},{4,20},{8,24},{12,28},{16,0},{20,4},{24,8},{28,12},{1,17},{... | collective-permute-start | bytes 786440 | tf_op jit(solution)/shard_map/ppermute | solution.py:30
  22.7 6.8 %plane0_120.1.refs_4_ = f32[2,2,2,256,256]{4,3,2,1,0:T(8,128)S(1)} custom-call(bf16[2,3,256,256]{3,2,1,0:T(8,128)(2,1)S(1)} %get-tuple-element.55.refs_0_, bf16[2,3,256,256]{3,2,1,0:T(8,128)(2,1)S(1)} %get-tuple-element.56.refs_0_.refs_1_, f32[3,3,3,2,2,256]{5,4,3,2,1,0:T(2,128)S(1)} %bitcast.20, f32[2,2,3,2,2,256]{5,4,3,2,1,0:T(2,128)S(1)} %phases.1.refs_2_.refs_3_, ...), custom_call_target="tpu_custom_call" | custom-call | flops 17179869184 | bytes 268435456 | tf_op jit(solution)/shard_map/plane0_120/pallas_call | solution.py:199
  29.5 3.5 %plane1_0.1 = (f32[4,2,2,32,256]{4,3,2,1,0:T(8,128)S(1)}, bf16[4,2,2,32,256]{4,3,2,1,0:T(8,128)(2,1)S(1)}) custom-call(bf16[2,3,256,256]{3,2,1,0:T(8,128)(2,1)S(1)} %get-tuple-element.56.refs_0_.refs_1_, bf16[2,3,256,256]{3,2,1,0:T(8,128)(2,1)S(1)} %collective-permute-done.7.refs_1_, f32[3,3,3,2,2,256]{5,4,3,2,1,0:T(2,128)S(1)} %bitcast.21, ...), custom_call_target="tpu_custom_call" | custom-call | flops 17179869184 | bytes 268435456 | tf_op jit(solution)/shard_map/plane1_0/pallas_call | solution.py:199
  33.2 0.2 collective-permute-done.5.refs_3_
  33.4 1.3 %collective-permute-done.8.got_ref = bf16[4,2,2,32,256]{4,3,2,1,0:T(8,128)(2,1)S(1)} collective-permute-done((bf16[4,2,2,32,256]{4,3,2,1,0:T(8,128)(2,1)S(1)}, bf16[4,2,2,32,256]{4,3,2,1,0:T(8,128)(2,1)S(1)}, u32[]{:S(2)}, u32[]{:S(2)}) %collective-permute-start.8) | collective-permute-done | bytes 262176 | tf_op jit(solution)/shard_map/ppermute | solution.py:30
  34.8 0.2 collective-permute-start.9
  35.0 2.0 %collective-permute-start.13 = (bf16[512,256]{1,0:T(8,128)(2,1)S(1)}, bf16[512,256]{1,0:T(8,128)(2,1)S(1)}, u32[]{:S(2)}, u32[]{:S(2)}) collective-permute-start(bf16[512,256]{1,0:T(8,128)(2,1)S(1)} %collective-permute-done.4.refs_2_), channel_id=1, source_target_pairs={{0,1},{1,0},{2,3},{3,2},{4,5},{5,4},{6,7},{7,6},{8,9},{9,8},{10,11... | collective-permute-start | bytes 786440 | tf_op jit(solution)/shard_map/ppermute | solution.py:30
  36.9 1.5 %collective-permute-start.14 = (bf16[512,256]{1,0:T(8,128)(2,1)S(1)}, bf16[512,256]{1,0:T(8,128)(2,1)S(1)}, u32[]{:S(2)}, u32[]{:S(2)}) collective-permute-start(bf16[512,256]{1,0:T(8,128)(2,1)S(1)} %collective-permute-done.3.refs_1_), channel_id=1, source_target_pairs={{0,16},{4,20},{8,24},{12,28},{16,0},{20,4},{24,8},{28,12},{1,17},{... | collective-permute-start | bytes 786440 | tf_op jit(solution)/shard_map/ppermute | solution.py:30
  38.4 1.5 %collective-permute-start.15 = (bf16[512,256]{1,0:T(8,128)(2,1)S(1)}, bf16[512,256]{1,0:T(8,128)(2,1)S(1)}, u32[]{:S(2)}, u32[]{:S(2)}) collective-permute-start(bf16[512,256]{1,0:T(8,128)(2,1)S(1)} %collective-permute-done.5.refs_3_), channel_id=1, source_target_pairs={{0,8},{4,12},{8,0},{12,4},{16,24},{20,28},{24,16},{28,20},{1,9},{5... | collective-permute-start | bytes 786440 | tf_op jit(solution)/shard_map/ppermute | solution.py:30
  40.0 0.5 %collective-permute-start.10 = (bf16[128,256]{1,0:T(8,128)(2,1)S(1)}, bf16[128,256]{1,0:T(8,128)(2,1)S(1)}, u32[]{:S(2)}, u32[]{:S(2)}) collective-permute-start(bf16[128,256]{1,0:T(8,128)(2,1)S(1)} %get-tuple-element.51), channel_id=1, source_target_pairs={{0,24},{4,28},{8,16},{12,20},{16,8},{20,12},{24,0},{28,4},{1,25},{... | collective-permute-start | bytes 196616 | tf_op jit(solution)/shard_map/ppermute | solution.py:30
  40.5 1.5 %collective-permute-start.11 = (bf16[128,256]{1,0:T(8,128)(2,1)S(1)}, bf16[128,256]{1,0:T(8,128)(2,1)S(1)}, u32[]{:S(2)}, u32[]{:S(2)}) collective-permute-start(bf16[128,256]{1,0:T(8,128)(2,1)S(1)} %get-tuple-element.52), channel_id=1, source_target_pairs={{0,16},{4,20},{8,24},{12,28},{16,0},{20,4},{24,8},{28,12},{1,17},{... | collective-permute-start | bytes 196616 | tf_op jit(solution)/shard_map/ppermute | solution.py:30
  42.1 1.7 %collective-permute-done.13.refs_0_.refs_5_ = bf16[512,256]{1,0:T(8,128)(2,1)S(1)} collective-permute-done((bf16[512,256]{1,0:T(8,128)(2,1)S(1)}, bf16[512,256]{1,0:T(8,128)(2,1)S(1)}, u32[]{:S(2)}, u32[]{:S(2)}) %collective-permute-start.13) | collective-permute-done | bytes 262176 | tf_op jit(solution)/shard_map/ppermute | solution.py:30
  43.7 1.5 %collective-permute-start.12 = (bf16[128,256]{1,0:T(8,128)(2,1)S(1)}, bf16[128,256]{1,0:T(8,128)(2,1)S(1)}, u32[]{:S(2)}, u32[]{:S(2)}) collective-permute-start(bf16[128,256]{1,0:T(8,128)(2,1)S(1)} %get-tuple-element.53), channel_id=1, source_target_pairs={{0,8},{4,12},{8,0},{12,4},{16,24},{20,28},{24,16},{28,20},{1,9},{5... | collective-permute-start | bytes 196616 | tf_op jit(solution)/shard_map/ppermute | solution.py:30
  45.2 1.4 %collective-permute-done.14.refs_1_.refs_6_ = bf16[512,256]{1,0:T(8,128)(2,1)S(1)} collective-permute-done((bf16[512,256]{1,0:T(8,128)(2,1)S(1)}, bf16[512,256]{1,0:T(8,128)(2,1)S(1)}, u32[]{:S(2)}, u32[]{:S(2)}) %collective-permute-start.14) | collective-permute-done | bytes 262176 | tf_op jit(solution)/shard_map/ppermute | solution.py:30
  46.6 1.0 %collective-permute-done.15.refs_2_.refs_7_ = bf16[512,256]{1,0:T(8,128)(2,1)S(1)} collective-permute-done((bf16[512,256]{1,0:T(8,128)(2,1)S(1)}, bf16[512,256]{1,0:T(8,128)(2,1)S(1)}, u32[]{:S(2)}, u32[]{:S(2)}) %collective-permute-start.15) | collective-permute-done | bytes 262176 | tf_op jit(solution)/shard_map/ppermute | solution.py:30
  47.8 0.7 %collective-permute-done.10.refs_1_ = bf16[128,256]{1,0:T(8,128)(2,1)S(1)} collective-permute-done((bf16[128,256]{1,0:T(8,128)(2,1)S(1)}, bf16[128,256]{1,0:T(8,128)(2,1)S(1)}, u32[]{:S(2)}, u32[]{:S(2)}) %collective-permute-start.10) | collective-permute-done | bytes 65568 | tf_op jit(solution)/shard_map/ppermute | solution.py:30
  48.4 0.8 %collective-permute-done.12.refs_3_ = bf16[128,256]{1,0:T(8,128)(2,1)S(1)} collective-permute-done((bf16[128,256]{1,0:T(8,128)(2,1)S(1)}, bf16[128,256]{1,0:T(8,128)(2,1)S(1)}, u32[]{:S(2)}, u32[]{:S(2)}) %collective-permute-start.12) | collective-permute-done | bytes 65568 | tf_op jit(solution)/shard_map/ppermute | solution.py:30
  49.2 0.3 left_operand.1.left_ref
  49.5 0.5 collective-permute-done.16.refs_9_
  50.0 2.0 %quark_products.1 = f32[2,16,2,32,256]{4,3,2,1,0:T(8,128)} custom-call(bf16[128,512]{1,0:T(8,128)(2,1)S(1)} %left_operand.1.left_ref, bf16[512,256]{1,0:T(8,128)(2,1)S(1)} %collective-permute-done.refs_0_, bf16[512,256]{1,0:T(8,128)(2,1)S(1)} %collective-permute-done.3.refs_1_, bf16[512,256]{1,0:T(8,128)(2,1)S(1)} %collective-permute-done.4.refs_2_, ...), custom_call_target="tpu_custom_call" | custom-call | flops 536870912 | bytes 7340032 | tf_op jit(solution)/shard_map/quark_products/pallas_call | solution.py:460
  (23 shorter events, 0.6 us)
Async XLA Ops:
  1.2 16.0 %collective-permute-start = (bf16[512,256]{1,0:T(8,128)(2,1)S(1)}, bf16[512,256]{1,0:T(8,128)(2,1)S(1)}, u32[]{:S(2)}, u32[]{:S(2)}) collective-permute-start(bf16[512,256]{1,0:T(8,128)(2,1)S(1)} %reshape.10), channel_id=1, source_target_pairs={{0,2},{2,0},{1,3},{3,1},{4,6},{6,4},{5,7},{7,5},{8,10},{10,8},{9,1... | collective-permute-start | bytes 786440 | tf_op jit(solution)/shard_map/ppermute | solution.py:25
  5.3 5.7 %collective-permute-start.2 = (s32[3,2,4]{2,1,0:T(2,128)}, s32[3,2,4]{2,1,0:T(2,128)S(1)}, u32[]{:S(2)}, u32[]{:S(2)}) collective-permute-start(s32[3,2,4]{2,1,0:T(2,128)} %bitcast.17), channel_id=1, source_target_pairs={{0,1},{1,0},{2,3},{3,2},{4,5},{5,4},{6,7},{7,6},{8,9},{9,8},{10,11... | collective-permute-start | bytes 296 | tf_op jit(solution)/shard_map/ppermute | solution.py:30
  6.9 4.1 %collective-permute-start.1 = (s32[2,3]{1,0:T(2,128)}, s32[2,3]{1,0:T(2,128)S(1)}, u32[]{:S(2)}, u32[]{:S(2)}) collective-permute-start(s32[2,3]{1,0:T(2,128)} %refs_0_.1), channel_id=1, source_target_pairs={{0,1},{1,0},{2,3},{3,2},{4,5},{5,4},{6,7},{7,6},{8,9},{9,8},{10,11... | collective-permute-start | bytes 80 | tf_op jit(solution)/shard_map/ppermute | solution.py:30
  9.0 2.0 %copy-start = (s32[4,2,3]{0,1,2:T(2,128)S(1)}, s32[4,2,3]{0,1,2:T(2,128)}, u32[]{:S(2)}) copy-start(s32[4,2,3]{0,1,2:T(2,128)} %param.9) | copy-start | bytes 292
  9.0 2.0 %copy-start.1 = (s32[2,3]{1,0:T(2,128)S(1)}, s32[2,3]{1,0:T(2,128)}, u32[]{:S(2)}) copy-start(s32[2,3]{1,0:T(2,128)} %refs_0_.1) | copy-start | bytes 76
  9.0 2.0 %copy-start.2 = (s32[4]{0:T(128)S(1)}, s32[4]{0:T(128)}, u32[]{:S(2)}) copy-start(s32[4]{0:T(128)} %refs_4_.1) | copy-start | bytes 52
  9.1 3.0 %copy-start.3 = (f32[1,3,3,3,2,2,256]{6,5,4,3,2,1,0:T(2,128)S(1)}, f32[1,3,3,3,2,2,256]{6,5,4,3,2,1,0:T(2,128)}, u32[]{:S(2)}) copy-start(f32[1,3,3,3,2,2,256]{6,5,4,3,2,1,0:T(2,128)} %param.7) | copy-start | bytes 331780
  9.2 20.3 %collective-permute-start.7 = (bf16[2,3,256,256]{3,2,1,0:T(8,128)(2,1)S(1)}, bf16[2,3,256,256]{3,2,1,0:T(8,128)(2,1)S(1)}, u32[]{:S(2)}, u32[]{:S(2)}) collective-permute-start(bf16[2,3,256,256]{3,2,1,0:T(8,128)(2,1)S(1)} %get-tuple-element.55.refs_0_), channel_id=1, source_target_pairs={{0,28},{4,0},{8,4},{12,8},{16,12},{20,16},{24,20},{28,24},{1,29},{... | collective-permute-start | bytes 2359304 | tf_op jit(solution)/shard_map/ppermute | solution.py:25
  17.3 15.9 %collective-permute-start.3 = (bf16[512,256]{1,0:T(8,128)(2,1)S(1)}, bf16[512,256]{1,0:T(8,128)(2,1)S(1)}, u32[]{:S(2)}, u32[]{:S(2)}) collective-permute-start(bf16[512,256]{1,0:T(8,128)(2,1)S(1)} %collective-permute-done.refs_0_), channel_id=1, source_target_pairs={{0,1},{1,0},{2,3},{3,2},{4,5},{5,4},{6,7},{7,6},{8,9},{9,8},{10,11... | collective-permute-start | bytes 786440 | tf_op jit(solution)/shard_map/ppermute | solution.py:30
  19.7 13.4 %collective-permute-start.4 = (bf16[512,256]{1,0:T(8,128)(2,1)S(1)}, bf16[512,256]{1,0:T(8,128)(2,1)S(1)}, u32[]{:S(2)}, u32[]{:S(2)}) collective-permute-start(bf16[512,256]{1,0:T(8,128)(2,1)S(1)} %collective-permute-done.refs_0_), channel_id=1, source_target_pairs={{0,8},{4,12},{8,0},{12,4},{16,24},{20,28},{24,16},{28,20},{1,9},{5... | collective-permute-start | bytes 786440 | tf_op jit(solution)/shard_map/ppermute | solution.py:30
  21.2 12.2 %collective-permute-start.5 = (bf16[512,256]{1,0:T(8,128)(2,1)S(1)}, bf16[512,256]{1,0:T(8,128)(2,1)S(1)}, u32[]{:S(2)}, u32[]{:S(2)}) collective-permute-start(bf16[512,256]{1,0:T(8,128)(2,1)S(1)} %collective-permute-done.refs_0_), channel_id=1, source_target_pairs={{0,16},{4,20},{8,24},{12,28},{16,0},{20,4},{24,8},{28,12},{1,17},{... | collective-permute-start | bytes 786440 | tf_op jit(solution)/shard_map/ppermute | solution.py:30
  22.7 10.7 %collective-permute-start.6 = (bf16[512,256]{1,0:T(8,128)(2,1)S(1)}, bf16[512,256]{1,0:T(8,128)(2,1)S(1)}, u32[]{:S(2)}, u32[]{:S(2)}) collective-permute-start(bf16[512,256]{1,0:T(8,128)(2,1)S(1)} %collective-permute-done.refs_0_), channel_id=1, source_target_pairs={{0,25},{1,24},{4,29},{5,28},{8,17},{9,16},{12,21},{13,20},{16,9},{... | collective-permute-start | bytes 786440 | tf_op jit(solution)/shard_map/ppermute | solution.py:39
  33.1 1.6 %collective-permute-start.8 = (bf16[4,2,2,32,256]{4,3,2,1,0:T(8,128)(2,1)S(1)}, bf16[4,2,2,32,256]{4,3,2,1,0:T(8,128)(2,1)S(1)}, u32[]{:S(2)}, u32[]{:S(2)}) collective-permute-start(bf16[4,2,2,32,256]{4,3,2,1,0:T(8,128)(2,1)S(1)} %get-tuple-element.38), channel_id=1, source_target_pairs={{0,4},{4,0},{8,12},{12,8},{16,20},{20,16},{24,28},{28,24},{1,5},{5... | collective-permute-start | bytes 786440 | tf_op jit(solution)/shard_map/ppermute | solution.py:30
  34.8 5.2 %collective-permute-start.9 = (bf16[5,512,256]{2,1,0:T(8,128)(2,1)S(1)}, bf16[5,512,256]{2,1,0:T(8,128)(2,1)S(1)}, u32[]{:S(2)}, u32[]{:S(2)}) collective-permute-start(bf16[5,512,256]{2,1,0:T(8,128)(2,1)S(1)} %pack_pieces.2), channel_id=1, source_target_pairs={{0,4},{4,0},{8,12},{12,8},{16,20},{20,16},{24,28},{28,24},{1,5},{5... | collective-permute-start | bytes 3932168 | tf_op jit(solution)/shard_map/ppermute | solution.py:30
  35.0 8.8 %collective-permute-start.13 = (bf16[512,256]{1,0:T(8,128)(2,1)S(1)}, bf16[512,256]{1,0:T(8,128)(2,1)S(1)}, u32[]{:S(2)}, u32[]{:S(2)}) collective-permute-start(bf16[512,256]{1,0:T(8,128)(2,1)S(1)} %collective-permute-done.4.refs_2_), channel_id=1, source_target_pairs={{0,1},{1,0},{2,3},{3,2},{4,5},{5,4},{6,7},{7,6},{8,9},{9,8},{10,11... | collective-permute-start | bytes 786440 | tf_op jit(solution)/shard_map/ppermute | solution.py:30
  36.9 9.7 %collective-permute-start.14 = (bf16[512,256]{1,0:T(8,128)(2,1)S(1)}, bf16[512,256]{1,0:T(8,128)(2,1)S(1)}, u32[]{:S(2)}, u32[]{:S(2)}) collective-permute-start(bf16[512,256]{1,0:T(8,128)(2,1)S(1)} %collective-permute-done.3.refs_1_), channel_id=1, source_target_pairs={{0,16},{4,20},{8,24},{12,28},{16,0},{20,4},{24,8},{28,12},{1,17},{... | collective-permute-start | bytes 786440 | tf_op jit(solution)/shard_map/ppermute | solution.py:30
  38.4 9.2 %collective-permute-start.15 = (bf16[512,256]{1,0:T(8,128)(2,1)S(1)}, bf16[512,256]{1,0:T(8,128)(2,1)S(1)}, u32[]{:S(2)}, u32[]{:S(2)}) collective-permute-start(bf16[512,256]{1,0:T(8,128)(2,1)S(1)} %collective-permute-done.5.refs_3_), channel_id=1, source_target_pairs={{0,8},{4,12},{8,0},{12,4},{16,24},{20,28},{24,16},{28,20},{1,9},{5... | collective-permute-start | bytes 786440 | tf_op jit(solution)/shard_map/ppermute | solution.py:30
  40.0 8.4 %collective-permute-start.10 = (bf16[128,256]{1,0:T(8,128)(2,1)S(1)}, bf16[128,256]{1,0:T(8,128)(2,1)S(1)}, u32[]{:S(2)}, u32[]{:S(2)}) collective-permute-start(bf16[128,256]{1,0:T(8,128)(2,1)S(1)} %get-tuple-element.51), channel_id=1, source_target_pairs={{0,24},{4,28},{8,16},{12,20},{16,8},{20,12},{24,0},{28,4},{1,25},{... | collective-permute-start | bytes 196616 | tf_op jit(solution)/shard_map/ppermute | solution.py:30
  40.5 7.9 %collective-permute-start.11 = (bf16[128,256]{1,0:T(8,128)(2,1)S(1)}, bf16[128,256]{1,0:T(8,128)(2,1)S(1)}, u32[]{:S(2)}, u32[]{:S(2)}) collective-permute-start(bf16[128,256]{1,0:T(8,128)(2,1)S(1)} %get-tuple-element.52), channel_id=1, source_target_pairs={{0,16},{4,20},{8,24},{12,28},{16,0},{20,4},{24,8},{28,12},{1,17},{... | collective-permute-start | bytes 196616 | tf_op jit(solution)/shard_map/ppermute | solution.py:30
  43.7 5.5 %collective-permute-start.12 = (bf16[128,256]{1,0:T(8,128)(2,1)S(1)}, bf16[128,256]{1,0:T(8,128)(2,1)S(1)}, u32[]{:S(2)}, u32[]{:S(2)}) collective-permute-start(bf16[128,256]{1,0:T(8,128)(2,1)S(1)} %get-tuple-element.53), channel_id=1, source_target_pairs={{0,8},{4,12},{8,0},{12,4},{16,24},{20,28},{24,16},{28,20},{1,9},{5... | collective-permute-start | bytes 196616 | tf_op jit(solution)/shard_map/ppermute | solution.py:30
  47.7 2.4 %collective-permute-start.16 = (bf16[3,512,256]{2,1,0:T(8,128)(2,1)S(1)}, bf16[3,512,256]{2,1,0:T(8,128)(2,1)S(1)}, u32[]{:S(2)}, u32[]{:S(2)}) collective-permute-start(bf16[3,512,256]{2,1,0:T(8,128)(2,1)S(1)} %pack_pieces.3), channel_id=1, source_target_pairs={{0,4},{4,0},{8,12},{12,8},{16,20},{20,16},{24,28},{28,24},{1,5},{5... | collective-permute-start | bytes 2359304 | tf_op jit(solution)/shard_map/ppermute | solution.py:30

commit v9 on v8

--- a/solution.py
+++ b/solution.py
@@ -441,10 +441,8 @@
     for size in range(2, len(dims) if len(dims) > 2 else 3):
         stage(held, size)
     late = [key for key in held if key not in early]
-    ready, swapped = hold({key: held[key] for key in early}, swapped)
-    flipped = [across(pack_call(list(ready.values())), "space", 1)]
+    flipped = [across(pack_call([held[key] for key in early]), "space", 1)]
     merged = merge_call(keep, swapped)
-    flipped, merged = lax.optimization_barrier((flipped, merged))
     got = [across(merged[mask], "space", 2 * mask) for mask in range(n_space // 2 - 1, 0, -1)]
     got.insert(0, merged[0])
     flipped.append(across(pack_call([held[key] for key in late]), "space", 1))

time: 52.2 us -> 51.1 us (0.979)
  waiting for transfers between devices: 8.52 us -> 7.67 us
    ppermute x14, waiting for transfers between devices: 8.37 us -> 7.52 us  [across(): return lax.ppermute(value, axis, pairs)]
  transfers between devices with their start and end apart: 17 -> 17, of which waited for: 10 -> 8; matrix products, arithmetic and copies ran while one was open for 3% -> 3% of each run, Pallas kernels for 32% -> 33%
where the time goes in v9:
time: 51.1 us; the launch traced here: 51 us
  starting transfers between devices  21.2 us (41%)
  Pallas kernels  18.8 us (37%)
  waiting for transfers between devices  7.67 us (15%)
  local copies, waits for them, and re-layouts  3 us (6%)
    ppermute x14, starting transfers between devices, across(): return lax.ppermute(value, axis, pairs)  16 us
    pallas_call x3, Pallas kernels, plane_call(): pl.pallas_call(functools.partial(plane_kernel, plane, dirs, part is not N...  15.4 us
    ppermute x14, waiting for transfers between devices, across(): return lax.ppermute(value, axis, pairs)  7.52 us
    ppermute x2, starting transfers between devices, from_behind(): return lax.ppermute(value, axis, pairs)  5.2 us
    unnamed x10, local copies, waits for them, and re-layouts  2.79 us
    pallas_call x1, Pallas kernels, shards(): pl.pallas_call(functools.partial(quark_kernel, masks, n_op), in_specs=[vm...  2.05 us
  transfers between devices with their start and end apart: 17, of which 8 were waited for; matrix products, arithmetic and copies ran while one was open for 3% of the time, Pallas kernels for 33%

profile of v9, /device:TPU:0, one launch (start us, length us, event | category | flops | bytes accessed | tf_op | source)
XLA Modules:
  0.0 51.0 jit_solution(11088446562054368069)
XLA Ops:
  0.0 1.1 %dynamic-slice_bitcast_fusion = bf16[256,1,2,256]{3,2,0,1:T(2,128)(2,1)S(1)} fusion(bf16[256,16,2,256]{3,2,1,0:T(2,128)(2,1)} %bitcast.23, s32[]{:T(128)S(6)} %select_n.14), kind=kLoop, calls=%fused_computation.3 | loop fusion | bytes 524292
  1.1 0.1 reshape.10
  1.2 4.1 %collective-permute-start = (bf16[512,256]{1,0:T(8,128)(2,1)S(1)}, bf16[512,256]{1,0:T(8,128)(2,1)S(1)}, u32[]{:S(2)}, u32[]{:S(2)}) collective-permute-start(bf16[512,256]{1,0:T(8,128)(2,1)S(1)} %reshape.10), channel_id=1, source_target_pairs={{0,2},{2,0},{1,3},{3,1},{4,6},{6,4},{5,7},{7,5},{8,10},{10,8},{9,1... | collective-permute-start | bytes 786440 | tf_op jit(solution)/shard_map/ppermute | solution.py:25
  5.3 1.6 %collective-permute-start.2 = (s32[3,2,4]{2,1,0:T(2,128)}, s32[3,2,4]{2,1,0:T(2,128)S(1)}, u32[]{:S(2)}, u32[]{:S(2)}) collective-permute-start(s32[3,2,4]{2,1,0:T(2,128)} %bitcast.17), channel_id=1, source_target_pairs={{0,1},{1,0},{2,3},{3,2},{4,5},{5,4},{6,7},{7,6},{8,9},{9,8},{10,11... | collective-permute-start | bytes 296 | tf_op jit(solution)/shard_map/ppermute | solution.py:30
  6.9 0.4 collective-permute-start.1
  7.4 1.6 %copy.11 = bf16[1,2,256,3,2,256]{5,2,3,1,4,0:T(8,128)(2,1)S(1)} copy(bf16[1,2,256,3,2,256]{5,4,3,2,1,0:T(2,128)(2,1)} %param.6) | data formatting | bytes 3145728 | tf_op args[0]
  9.1 0.1 slice_bitcast_fusion
  9.2 1.1 %collective-permute-start.7 = (bf16[2,3,256,256]{3,2,1,0:T(8,128)(2,1)S(1)}, bf16[2,3,256,256]{3,2,1,0:T(8,128)(2,1)S(1)}, u32[]{:S(2)}, u32[]{:S(2)}) collective-permute-start(bf16[2,3,256,256]{3,2,1,0:T(8,128)(2,1)S(1)} %get-tuple-element.33.refs_0_), channel_id=1, source_target_pairs={{0,28},{4,0},{8,4},{12,8},{16,12},{20,16},{24,20},{28,24},{1,29},{... | collective-permute-start | bytes 2359304 | tf_op jit(solution)/shard_map/ppermute | solution.py:25
  10.3 0.8 %collective-permute-done.1.refs_1_ = s32[2,3]{1,0:T(2,128)S(1)} collective-permute-done((s32[2,3]{1,0:T(2,128)}, s32[2,3]{1,0:T(2,128)S(1)}, u32[]{:S(2)}, u32[]{:S(2)}) %collective-permute-start.1) | collective-permute-done | bytes 56 | tf_op jit(solution)/shard_map/ppermute | solution.py:30
  11.1 0.9 %phases.1.refs_2_.refs_3_ = f32[2,2,3,2,2,256]{5,4,3,2,1,0:T(2,128)S(1)} custom-call(s32[2,3]{1,0:T(2,128)S(1)} %copy-done.1, s32[2,3]{1,0:T(2,128)S(1)} %collective-permute-done.1.refs_1_, s32[3,2,4]{2,1,0:T(2,128)S(1)} %bitcast.18, s32[3,2,4]{2,1,0:T(2,128)S(1)} %collective-permute-done.2.refs_3_, s32[4]{0:T(128)S(1)} %copy-done.2), custom_call_target="tpu_custom_call" | custom-call | tf_op jit(solution)/shard_map/phases/pallas_call | solution.py:401
  12.0 5.1 %plane1_12.1.refs_4_ = f32[2,2,2,256,256]{4,3,2,1,0:T(8,128)S(1)} custom-call(bf16[2,3,256,256]{3,2,1,0:T(8,128)(2,1)S(1)} %get-tuple-element.34.refs_0_.refs_1_, f32[3,3,3,2,2,256]{5,4,3,2,1,0:T(2,128)S(1)} %bitcast.19, f32[2,2,3,2,2,256]{5,4,3,2,1,0:T(2,128)S(1)} %phases.1.refs_2_.refs_3_), custom_call_target="tpu_custom_call" | custom-call | flops 17179869184 | bytes 268435456 | tf_op jit(solution)/shard_map/plane1_12/pallas_call | solution.py:199
  17.1 0.1 collective-permute-done.refs_0_
  17.3 2.4 %collective-permute-start.3 = (bf16[512,256]{1,0:T(8,128)(2,1)S(1)}, bf16[512,256]{1,0:T(8,128)(2,1)S(1)}, u32[]{:S(2)}, u32[]{:S(2)}) collective-permute-start(bf16[512,256]{1,0:T(8,128)(2,1)S(1)} %collective-permute-done.refs_0_), channel_id=1, source_target_pairs={{0,1},{1,0},{2,3},{3,2},{4,5},{5,4},{6,7},{7,6},{8,9},{9,8},{10,11... | collective-permute-start | bytes 786440 | tf_op jit(solution)/shard_map/ppermute | solution.py:30
  19.7 1.5 %collective-permute-start.4 = (bf16[512,256]{1,0:T(8,128)(2,1)S(1)}, bf16[512,256]{1,0:T(8,128)(2,1)S(1)}, u32[]{:S(2)}, u32[]{:S(2)}) collective-permute-start(bf16[512,256]{1,0:T(8,128)(2,1)S(1)} %collective-permute-done.refs_0_), channel_id=1, source_target_pairs={{0,8},{4,12},{8,0},{12,4},{16,24},{20,28},{24,16},{28,20},{1,9},{5... | collective-permute-start | bytes 786440 | tf_op jit(solution)/shard_map/ppermute | solution.py:30
  21.2 1.5 %collective-permute-start.5 = (bf16[512,256]{1,0:T(8,128)(2,1)S(1)}, bf16[512,256]{1,0:T(8,128)(2,1)S(1)}, u32[]{:S(2)}, u32[]{:S(2)}) collective-permute-start(bf16[512,256]{1,0:T(8,128)(2,1)S(1)} %collective-permute-done.refs_0_), channel_id=1, source_target_pairs={{0,16},{4,20},{8,24},{12,28},{16,0},{20,4},{24,8},{28,12},{1,17},{... | collective-permute-start | bytes 786440 | tf_op jit(solution)/shard_map/ppermute | solution.py:30
  22.7 6.8 %plane0_120.1.refs_4_ = f32[2,2,2,256,256]{4,3,2,1,0:T(8,128)S(1)} custom-call(bf16[2,3,256,256]{3,2,1,0:T(8,128)(2,1)S(1)} %get-tuple-element.33.refs_0_, bf16[2,3,256,256]{3,2,1,0:T(8,128)(2,1)S(1)} %get-tuple-element.34.refs_0_.refs_1_, f32[3,3,3,2,2,256]{5,4,3,2,1,0:T(2,128)S(1)} %bitcast.20, f32[2,2,3,2,2,256]{5,4,3,2,1,0:T(2,128)S(1)} %phases.1.refs_2_.refs_3_, ...), custom_call_target="tpu_custom_call" | custom-call | flops 17179869184 | bytes 268435456 | tf_op jit(solution)/shard_map/plane0_120/pallas_call | solution.py:199
  29.5 3.5 %plane1_0.1 = (f32[4,2,2,32,256]{4,3,2,1,0:T(8,128)S(1)}, bf16[4,2,2,32,256]{4,3,2,1,0:T(8,128)(2,1)S(1)}) custom-call(bf16[2,3,256,256]{3,2,1,0:T(8,128)(2,1)S(1)} %get-tuple-element.34.refs_0_.refs_1_, bf16[2,3,256,256]{3,2,1,0:T(8,128)(2,1)S(1)} %collective-permute-done.7.refs_1_, f32[3,3,3,2,2,256]{5,4,3,2,1,0:T(2,128)S(1)} %bitcast.21, ...), custom_call_target="tpu_custom_call" | custom-call | flops 17179869184 | bytes 268435456 | tf_op jit(solution)/shard_map/plane1_0/pallas_call | solution.py:199
  33.2 0.2 collective-permute-done.5.refs_3_
  33.4 1.8 %collective-permute-start.12 = (bf16[512,256]{1,0:T(8,128)(2,1)S(1)}, bf16[512,256]{1,0:T(8,128)(2,1)S(1)}, u32[]{:S(2)}, u32[]{:S(2)}) collective-permute-start(bf16[512,256]{1,0:T(8,128)(2,1)S(1)} %collective-permute-done.4.refs_2_), channel_id=1, source_target_pairs={{0,1},{1,0},{2,3},{3,2},{4,5},{5,4},{6,7},{7,6},{8,9},{9,8},{10,11... | collective-permute-start | bytes 786440 | tf_op jit(solution)/shard_map/ppermute | solution.py:30
  35.2 1.5 %collective-permute-start.13 = (bf16[512,256]{1,0:T(8,128)(2,1)S(1)}, bf16[512,256]{1,0:T(8,128)(2,1)S(1)}, u32[]{:S(2)}, u32[]{:S(2)}) collective-permute-start(bf16[512,256]{1,0:T(8,128)(2,1)S(1)} %collective-permute-done.3.refs_1_), channel_id=1, source_target_pairs={{0,16},{4,20},{8,24},{12,28},{16,0},{20,4},{24,8},{28,12},{1,17},{... | collective-permute-start | bytes 786440 | tf_op jit(solution)/shard_map/ppermute | solution.py:30
  36.7 1.5 %collective-permute-start.14 = (bf16[512,256]{1,0:T(8,128)(2,1)S(1)}, bf16[512,256]{1,0:T(8,128)(2,1)S(1)}, u32[]{:S(2)}, u32[]{:S(2)}) collective-permute-start(bf16[512,256]{1,0:T(8,128)(2,1)S(1)} %collective-permute-done.5.refs_3_), channel_id=1, source_target_pairs={{0,8},{4,12},{8,0},{12,4},{16,24},{20,28},{24,16},{28,20},{1,9},{5... | collective-permute-start | bytes 786440 | tf_op jit(solution)/shard_map/ppermute | solution.py:30
  38.3 0.6 %collective-permute-start.10 = (bf16[128,256]{1,0:T(8,128)(2,1)S(1)}, bf16[128,256]{1,0:T(8,128)(2,1)S(1)}, u32[]{:S(2)}, u32[]{:S(2)}) collective-permute-start(bf16[128,256]{1,0:T(8,128)(2,1)S(1)} %get-tuple-element.26), channel_id=1, source_target_pairs={{0,16},{4,20},{8,24},{12,28},{16,0},{20,4},{24,8},{28,12},{1,17},{... | collective-permute-start | bytes 196616 | tf_op jit(solution)/shard_map/ppermute | solution.py:30
  38.8 0.5 %collective-permute-start.11 = (bf16[128,256]{1,0:T(8,128)(2,1)S(1)}, bf16[128,256]{1,0:T(8,128)(2,1)S(1)}, u32[]{:S(2)}, u32[]{:S(2)}) collective-permute-start(bf16[128,256]{1,0:T(8,128)(2,1)S(1)} %get-tuple-element.27), channel_id=1, source_target_pairs={{0,8},{4,12},{8,0},{12,4},{16,24},{20,28},{24,16},{28,20},{1,9},{5... | collective-permute-start | bytes 196616 | tf_op jit(solution)/shard_map/ppermute | solution.py:30
  39.4 2.8 %collective-permute-done.12.refs_0_.refs_5_ = bf16[512,256]{1,0:T(8,128)(2,1)S(1)} collective-permute-done((bf16[512,256]{1,0:T(8,128)(2,1)S(1)}, bf16[512,256]{1,0:T(8,128)(2,1)S(1)}, u32[]{:S(2)}, u32[]{:S(2)}) %collective-permute-start.12) | collective-permute-done | bytes 262176 | tf_op jit(solution)/shard_map/ppermute | solution.py:30
  42.1 2.4 %collective-permute-start.9 = (bf16[128,256]{1,0:T(8,128)(2,1)S(1)}, bf16[128,256]{1,0:T(8,128)(2,1)S(1)}, u32[]{:S(2)}, u32[]{:S(2)}) collective-permute-start(bf16[128,256]{1,0:T(8,128)(2,1)S(1)} %get-tuple-element.25), channel_id=1, source_target_pairs={{0,24},{4,28},{8,16},{12,20},{16,8},{20,12},{24,0},{28,4},{1,25},{... | collective-permute-start | bytes 196616 | tf_op jit(solution)/shard_map/ppermute | solution.py:30
  44.6 0.1 pack_pieces.2
  44.8 0.8 %collective-permute-done.14.refs_2_.refs_7_ = bf16[512,256]{1,0:T(8,128)(2,1)S(1)} collective-permute-done((bf16[512,256]{1,0:T(8,128)(2,1)S(1)}, bf16[512,256]{1,0:T(8,128)(2,1)S(1)}, u32[]{:S(2)}, u32[]{:S(2)}) %collective-permute-start.14) | collective-permute-done | bytes 262176 | tf_op jit(solution)/shard_map/ppermute | solution.py:30
  45.7 1.2 %collective-permute-done.11.refs_3_ = bf16[128,256]{1,0:T(8,128)(2,1)S(1)} collective-permute-done((bf16[128,256]{1,0:T(8,128)(2,1)S(1)}, bf16[128,256]{1,0:T(8,128)(2,1)S(1)}, u32[]{:S(2)}, u32[]{:S(2)}) %collective-permute-start.11) | collective-permute-done | bytes 65568 | tf_op jit(solution)/shard_map/ppermute | solution.py:30
  46.9 0.6 %collective-permute-done.9.refs_1_ = bf16[128,256]{1,0:T(8,128)(2,1)S(1)} collective-permute-done((bf16[128,256]{1,0:T(8,128)(2,1)S(1)}, bf16[128,256]{1,0:T(8,128)(2,1)S(1)}, u32[]{:S(2)}, u32[]{:S(2)}) %collective-permute-start.9) | collective-permute-done | bytes 65568 | tf_op jit(solution)/shard_map/ppermute | solution.py:30
  47.6 0.3 left_operand.1.left_ref
  47.9 1.0 %collective-permute-done.16.refs_9_ = bf16[3,512,256]{2,1,0:T(8,128)(2,1)S(1)} collective-permute-done((bf16[3,512,256]{2,1,0:T(8,128)(2,1)S(1)}, bf16[3,512,256]{2,1,0:T(8,128)(2,1)S(1)}, u32[]{:S(2)}, u32[]{:S(2)}) %collective-permute-start.16) | collective-permute-done | bytes 786464 | tf_op jit(solution)/shard_map/ppermute | solution.py:30
  48.9 2.0 %quark_products.1 = f32[2,16,2,32,256]{4,3,2,1,0:T(8,128)} custom-call(bf16[128,512]{1,0:T(8,128)(2,1)S(1)} %left_operand.1.left_ref, bf16[512,256]{1,0:T(8,128)(2,1)S(1)} %collective-permute-done.refs_0_, bf16[512,256]{1,0:T(8,128)(2,1)S(1)} %collective-permute-done.3.refs_1_, bf16[512,256]{1,0:T(8,128)(2,1)S(1)} %collective-permute-done.4.refs_2_, ...), custom_call_target="tpu_custom_call" | custom-call | flops 536870912 | bytes 7340032 | tf_op jit(solution)/shard_map/quark_products/pallas_call | solution.py:458
  (23 shorter events, 0.4 us)
Async XLA Ops:
  1.2 16.0 %collective-permute-start = (bf16[512,256]{1,0:T(8,128)(2,1)S(1)}, bf16[512,256]{1,0:T(8,128)(2,1)S(1)}, u32[]{:S(2)}, u32[]{:S(2)}) collective-permute-start(bf16[512,256]{1,0:T(8,128)(2,1)S(1)} %reshape.10), channel_id=1, source_target_pairs={{0,2},{2,0},{1,3},{3,1},{4,6},{6,4},{5,7},{7,5},{8,10},{10,8},{9,1... | collective-permute-start | bytes 786440 | tf_op jit(solution)/shard_map/ppermute | solution.py:25
  5.3 5.7 %collective-permute-start.2 = (s32[3,2,4]{2,1,0:T(2,128)}, s32[3,2,4]{2,1,0:T(2,128)S(1)}, u32[]{:S(2)}, u32[]{:S(2)}) collective-permute-start(s32[3,2,4]{2,1,0:T(2,128)} %bitcast.17), channel_id=1, source_target_pairs={{0,1},{1,0},{2,3},{3,2},{4,5},{5,4},{6,7},{7,6},{8,9},{9,8},{10,11... | collective-permute-start | bytes 296 | tf_op jit(solution)/shard_map/ppermute | solution.py:30
  6.9 4.1 %collective-permute-start.1 = (s32[2,3]{1,0:T(2,128)}, s32[2,3]{1,0:T(2,128)S(1)}, u32[]{:S(2)}, u32[]{:S(2)}) collective-permute-start(s32[2,3]{1,0:T(2,128)} %refs_0_.1), channel_id=1, source_target_pairs={{0,1},{1,0},{2,3},{3,2},{4,5},{5,4},{6,7},{7,6},{8,9},{9,8},{10,11... | collective-permute-start | bytes 80 | tf_op jit(solution)/shard_map/ppermute | solution.py:30
  9.0 2.0 %copy-start = (s32[4,2,3]{0,1,2:T(2,128)S(1)}, s32[4,2,3]{0,1,2:T(2,128)}, u32[]{:S(2)}) copy-start(s32[4,2,3]{0,1,2:T(2,128)} %param.9) | copy-start | bytes 292
  9.0 2.0 %copy-start.1 = (s32[2,3]{1,0:T(2,128)S(1)}, s32[2,3]{1,0:T(2,128)}, u32[]{:S(2)}) copy-start(s32[2,3]{1,0:T(2,128)} %refs_0_.1) | copy-start | bytes 76
  9.0 2.0 %copy-start.2 = (s32[4]{0:T(128)S(1)}, s32[4]{0:T(128)}, u32[]{:S(2)}) copy-start(s32[4]{0:T(128)} %refs_4_.1) | copy-start | bytes 52
  9.1 3.0 %copy-start.3 = (f32[1,3,3,3,2,2,256]{6,5,4,3,2,1,0:T(2,128)S(1)}, f32[1,3,3,3,2,2,256]{6,5,4,3,2,1,0:T(2,128)}, u32[]{:S(2)}) copy-start(f32[1,3,3,3,2,2,256]{6,5,4,3,2,1,0:T(2,128)} %param.7) | copy-start | bytes 331780
  9.2 20.3 %collective-permute-start.7 = (bf16[2,3,256,256]{3,2,1,0:T(8,128)(2,1)S(1)}, bf16[2,3,256,256]{3,2,1,0:T(8,128)(2,1)S(1)}, u32[]{:S(2)}, u32[]{:S(2)}) collective-permute-start(bf16[2,3,256,256]{3,2,1,0:T(8,128)(2,1)S(1)} %get-tuple-element.33.refs_0_), channel_id=1, source_target_pairs={{0,28},{4,0},{8,4},{12,8},{16,12},{20,16},{24,20},{28,24},{1,29},{... | collective-permute-start | bytes 2359304 | tf_op jit(solution)/shard_map/ppermute | solution.py:25
  17.3 15.9 %collective-permute-start.3 = (bf16[512,256]{1,0:T(8,128)(2,1)S(1)}, bf16[512,256]{1,0:T(8,128)(2,1)S(1)}, u32[]{:S(2)}, u32[]{:S(2)}) collective-permute-start(bf16[512,256]{1,0:T(8,128)(2,1)S(1)} %collective-permute-done.refs_0_), channel_id=1, source_target_pairs={{0,1},{1,0},{2,3},{3,2},{4,5},{5,4},{6,7},{7,6},{8,9},{9,8},{10,11... | collective-permute-start | bytes 786440 | tf_op jit(solution)/shard_map/ppermute | solution.py:30
  19.7 13.4 %collective-permute-start.4 = (bf16[512,256]{1,0:T(8,128)(2,1)S(1)}, bf16[512,256]{1,0:T(8,128)(2,1)S(1)}, u32[]{:S(2)}, u32[]{:S(2)}) collective-permute-start(bf16[512,256]{1,0:T(8,128)(2,1)S(1)} %collective-permute-done.refs_0_), channel_id=1, source_target_pairs={{0,8},{4,12},{8,0},{12,4},{16,24},{20,28},{24,16},{28,20},{1,9},{5... | collective-permute-start | bytes 786440 | tf_op jit(solution)/shard_map/ppermute | solution.py:30
  21.2 12.2 %collective-permute-start.5 = (bf16[512,256]{1,0:T(8,128)(2,1)S(1)}, bf16[512,256]{1,0:T(8,128)(2,1)S(1)}, u32[]{:S(2)}, u32[]{:S(2)}) collective-permute-start(bf16[512,256]{1,0:T(8,128)(2,1)S(1)} %collective-permute-done.refs_0_), channel_id=1, source_target_pairs={{0,16},{4,20},{8,24},{12,28},{16,0},{20,4},{24,8},{28,12},{1,17},{... | collective-permute-start | bytes 786440 | tf_op jit(solution)/shard_map/ppermute | solution.py:30
  22.7 10.7 %collective-permute-start.6 = (bf16[512,256]{1,0:T(8,128)(2,1)S(1)}, bf16[512,256]{1,0:T(8,128)(2,1)S(1)}, u32[]{:S(2)}, u32[]{:S(2)}) collective-permute-start(bf16[512,256]{1,0:T(8,128)(2,1)S(1)} %collective-permute-done.refs_0_), channel_id=1, source_target_pairs={{0,25},{1,24},{4,29},{5,28},{8,17},{9,16},{12,21},{13,20},{16,9},{... | collective-permute-start | bytes 786440 | tf_op jit(solution)/shard_map/ppermute | solution.py:39
  33.1 5.1 %collective-permute-start.8 = (bf16[4,2,2,32,256]{4,3,2,1,0:T(8,128)(2,1)S(1)}, bf16[4,2,2,32,256]{4,3,2,1,0:T(8,128)(2,1)S(1)}, u32[]{:S(2)}, u32[]{:S(2)}) collective-permute-start(bf16[4,2,2,32,256]{4,3,2,1,0:T(8,128)(2,1)S(1)} %get-tuple-element.23), channel_id=1, source_target_pairs={{0,4},{4,0},{8,12},{12,8},{16,20},{20,16},{24,28},{28,24},{1,5},{5... | collective-permute-start | bytes 786440 | tf_op jit(solution)/shard_map/ppermute | solution.py:30
  33.4 8.7 %collective-permute-start.12 = (bf16[512,256]{1,0:T(8,128)(2,1)S(1)}, bf16[512,256]{1,0:T(8,128)(2,1)S(1)}, u32[]{:S(2)}, u32[]{:S(2)}) collective-permute-start(bf16[512,256]{1,0:T(8,128)(2,1)S(1)} %collective-permute-done.4.refs_2_), channel_id=1, source_target_pairs={{0,1},{1,0},{2,3},{3,2},{4,5},{5,4},{6,7},{7,6},{8,9},{9,8},{10,11... | collective-permute-start | bytes 786440 | tf_op jit(solution)/shard_map/ppermute | solution.py:30
  35.2 9.5 %collective-permute-start.13 = (bf16[512,256]{1,0:T(8,128)(2,1)S(1)}, bf16[512,256]{1,0:T(8,128)(2,1)S(1)}, u32[]{:S(2)}, u32[]{:S(2)}) collective-permute-start(bf16[512,256]{1,0:T(8,128)(2,1)S(1)} %collective-permute-done.3.refs_1_), channel_id=1, source_target_pairs={{0,16},{4,20},{8,24},{12,28},{16,0},{20,4},{24,8},{28,12},{1,17},{... | collective-permute-start | bytes 786440 | tf_op jit(solution)/shard_map/ppermute | solution.py:30
  36.7 8.9 %collective-permute-start.14 = (bf16[512,256]{1,0:T(8,128)(2,1)S(1)}, bf16[512,256]{1,0:T(8,128)(2,1)S(1)}, u32[]{:S(2)}, u32[]{:S(2)}) collective-permute-start(bf16[512,256]{1,0:T(8,128)(2,1)S(1)} %collective-permute-done.5.refs_3_), channel_id=1, source_target_pairs={{0,8},{4,12},{8,0},{12,4},{16,24},{20,28},{24,16},{28,20},{1,9},{5... | collective-permute-start | bytes 786440 | tf_op jit(solution)/shard_map/ppermute | solution.py:30
  38.3 7.4 %collective-permute-start.10 = (bf16[128,256]{1,0:T(8,128)(2,1)S(1)}, bf16[128,256]{1,0:T(8,128)(2,1)S(1)}, u32[]{:S(2)}, u32[]{:S(2)}) collective-permute-start(bf16[128,256]{1,0:T(8,128)(2,1)S(1)} %get-tuple-element.26), channel_id=1, source_target_pairs={{0,16},{4,20},{8,24},{12,28},{16,0},{20,4},{24,8},{28,12},{1,17},{... | collective-permute-start | bytes 196616 | tf_op jit(solution)/shard_map/ppermute | solution.py:30
  38.8 8.1 %collective-permute-start.11 = (bf16[128,256]{1,0:T(8,128)(2,1)S(1)}, bf16[128,256]{1,0:T(8,128)(2,1)S(1)}, u32[]{:S(2)}, u32[]{:S(2)}) collective-permute-start(bf16[128,256]{1,0:T(8,128)(2,1)S(1)} %get-tuple-element.27), channel_id=1, source_target_pairs={{0,8},{4,12},{8,0},{12,4},{16,24},{20,28},{24,16},{28,20},{1,9},{5... | collective-permute-start | bytes 196616 | tf_op jit(solution)/shard_map/ppermute | solution.py:30
  42.1 5.5 %collective-permute-start.9 = (bf16[128,256]{1,0:T(8,128)(2,1)S(1)}, bf16[128,256]{1,0:T(8,128)(2,1)S(1)}, u32[]{:S(2)}, u32[]{:S(2)}) collective-permute-start(bf16[128,256]{1,0:T(8,128)(2,1)S(1)} %get-tuple-element.25), channel_id=1, source_target_pairs={{0,24},{4,28},{8,16},{12,20},{16,8},{20,12},{24,0},{28,4},{1,25},{... | collective-permute-start | bytes 196616 | tf_op jit(solution)/shard_map/ppermute | solution.py:30
  44.7 4.2 %collective-permute-start.15 = (bf16[5,512,256]{2,1,0:T(8,128)(2,1)S(1)}, bf16[5,512,256]{2,1,0:T(8,128)(2,1)S(1)}, u32[]{:S(2)}, u32[]{:S(2)}) collective-permute-start(bf16[5,512,256]{2,1,0:T(8,128)(2,1)S(1)} %pack_pieces.2), channel_id=1, source_target_pairs={{0,4},{4,0},{8,12},{12,8},{16,20},{20,16},{24,28},{28,24},{1,5},{5... | collective-permute-start | bytes 3932168 | tf_op jit(solution)/shard_map/ppermute | solution.py:30
  45.6 3.3 %collective-permute-start.16 = (bf16[3,512,256]{2,1,0:T(8,128)(2,1)S(1)}, bf16[3,512,256]{2,1,0:T(8,128)(2,1)S(1)}, u32[]{:S(2)}, u32[]{:S(2)}) collective-permute-start(bf16[3,512,256]{2,1,0:T(8,128)(2,1)S(1)} %pack_pieces.3), channel_id=1, source_target_pairs={{0,4},{4,0},{8,12},{12,8},{16,20},{20,16},{24,28},{28,24},{1,5},{5... | collective-permute-start | bytes 2359304 | tf_op jit(solution)/shard_map/ppermute | solution.py:30

commit v10 on v9

--- a/solution.py
+++ b/solution.py
@@ -380,19 +380,20 @@
     my_op = lax.axis_index("op")
     my_space = lax.axis_index("space")
 
-    nums = jnp.transpose(coef_num, (2, 1, 0))
-    both = [(momenta, nums)]
-    both += [(across(momenta, "op", mask), across(nums, "op", mask)) for mask in range(1, n_op)]
-
     group = n_space * n_op
     depth = n_b * SPINS // group
     first = (my_space * n_op + my_op) * depth
     piece = lax.dynamic_slice(
         peram.reshape(n_b, SPINS, 2, n_b), (first % n_b, first // n_b, 0, 0), (depth, 1, 2, n_b)
     ).reshape(depth * 2, n_b)
+    own_piece = from_behind(piece, "tm", n_tm - 1)
+
+    momenta, coef_num, piece = lax.optimization_barrier((momenta, coef_num, piece))
+    nums = jnp.transpose(coef_num, (2, 1, 0))
+    both = [(momenta, nums)]
+    both += [(across(momenta, "op", mask), across(nums, "op", mask)) for mask in range(1, n_op)]
 
     moved = lax.optimization_barrier(jnp.transpose(eigvecs[0], (3, 0, 2, 1, 4)))
-    own_piece = from_behind(piece, "tm", n_tm - 1)
     vecs = [moved[plane] for plane in range(planes)]
     upper = from_behind(vecs[0], "space", -1)
 
@@ -425,13 +426,14 @@
     link = links[0]
     last = planes - 1
     corner = tuple(range(len(dims)))
-    partial = plane_call(last, (1, 2), vecs[last], None, link, phi)
+    partial = None
+    for plane in range(last):
+        partial = plane_call(plane, (1, 2, 0), vecs[plane], vecs[plane + 1], link, phi, partial)
     held, partial = hold({(): own_piece}, partial)
     stage(held, 1)
     if len(dims) > 2:
         far = diagonal(held[()], n_space, n_op)
-    for plane in range(last):
-        partial = plane_call(plane, (1, 2, 0), vecs[plane], vecs[plane + 1], link, phi, partial)
+    partial = plane_call(last, (1, 2), vecs[last], None, link, phi, partial)
     keep, give = plane_call(last, (0,), vecs[last], upper, link, phi, partial, n_space)
     swapped = across(give, "space", 1)
     if len(dims) > 2:

time: 51.1 us -> 50.5 us (0.988)
  starting transfers between devices: 21.2 us -> 19.7 us
  waiting for transfers between devices: 7.67 us -> 8.61 us
    ppermute x14, starting transfers between devices: 16 us -> 10.1 us  [across(): return lax.ppermute(value, axis, pairs)]
    ppermute x1, starting transfers between devices: 0.01 us -> 4.43 us  [diagonal(): return lax.ppermute(value, ('space', 'op'), pairs)]
    ppermute x14, waiting for transfers between devices: 7.52 us -> 8.6 us  [across(): return lax.ppermute(value, axis, pairs)]
  transfers between devices with their start and end apart: 17 -> 17, of which waited for: 8 -> 7; matrix products, arithmetic and copies ran while one was open for 3% -> 3% of each run, Pallas kernels for 33% -> 33%
where the time goes in v10:
time: 50.5 us; the launch traced here: 50.3 us
  starting transfers between devices  19.7 us (39%)
  Pallas kernels  18.8 us (37%)
  waiting for transfers between devices  8.61 us (17%)
  local copies, waits for them, and re-layouts  3 us (6%)
    pallas_call x3, Pallas kernels, plane_call(): pl.pallas_call(functools.partial(plane_kernel, plane, dirs, part is not N...  15.4 us
    ppermute x14, starting transfers between devices, across(): return lax.ppermute(value, axis, pairs)  10.1 us
    ppermute x14, waiting for transfers between devices, across(): return lax.ppermute(value, axis, pairs)  8.6 us
    ppermute x2, starting transfers between devices, from_behind(): return lax.ppermute(value, axis, pairs)  5.2 us
    ppermute x1, starting transfers between devices, diagonal(): return lax.ppermute(value, ('space', 'op'), pairs)  4.43 us
    unnamed x10, local copies, waits for them, and re-layouts  2.79 us
    pallas_call x1, Pallas kernels, shards(): pl.pallas_call(functools.partial(quark_kernel, masks, n_op), in_specs=[vm...  2.05 us
  transfers between devices with their start and end apart: 17, of which 7 were waited for; matrix products, arithmetic and copies ran while one was open for 3% of the time, Pallas kernels for 33%

profile of v10, /device:TPU:0, one launch (start us, length us, event | category | flops | bytes accessed | tf_op | source)
XLA Modules:
  0.0 50.3 jit_solution(4710060233283721827)
XLA Ops:
  0.0 1.1 %dynamic-slice_bitcast_fusion = bf16[256,1,2,256]{3,2,0,1:T(2,128)(2,1)S(1)} fusion(bf16[256,16,2,256]{3,2,1,0:T(2,128)(2,1)} %bitcast.23, s32[]{:T(128)S(6)} %select_n.14), kind=kLoop, calls=%fused_computation.3 | loop fusion | bytes 524292
  1.1 0.1 reshape.10
  1.2 4.1 %collective-permute-start = (bf16[512,256]{1,0:T(8,128)(2,1)S(1)}, bf16[512,256]{1,0:T(8,128)(2,1)S(1)}, u32[]{:S(2)}, u32[]{:S(2)}) collective-permute-start(bf16[512,256]{1,0:T(8,128)(2,1)S(1)} %reshape.10), channel_id=1, source_target_pairs={{0,2},{2,0},{1,3},{3,1},{4,6},{6,4},{5,7},{7,5},{8,10},{10,8},{9,1... | collective-permute-start | bytes 786440 | tf_op jit(solution)/shard_map/ppermute | solution.py:25
  5.3 1.6 %collective-permute-start.1 = (s32[2,3]{1,0:T(2,128)}, s32[2,3]{1,0:T(2,128)S(1)}, u32[]{:S(2)}, u32[]{:S(2)}) collective-permute-start(s32[2,3]{1,0:T(2,128)} %refs_0_), channel_id=1, source_target_pairs={{0,1},{1,0},{2,3},{3,2},{4,5},{5,4},{6,7},{7,6},{8,9},{9,8},{10,11... | collective-permute-start | bytes 80 | tf_op jit(solution)/shard_map/ppermute | solution.py:30
  6.9 0.4 collective-permute-start.2
  7.4 1.6 %copy.11 = bf16[1,2,256,3,2,256]{5,2,3,1,4,0:T(8,128)(2,1)S(1)} copy(bf16[1,2,256,3,2,256]{5,4,3,2,1,0:T(2,128)(2,1)} %param.6) | data formatting | bytes 3145728 | tf_op args[0]
  9.1 0.1 slice_bitcast_fusion
  9.2 1.1 %collective-permute-start.7 = (bf16[2,3,256,256]{3,2,1,0:T(8,128)(2,1)S(1)}, bf16[2,3,256,256]{3,2,1,0:T(8,128)(2,1)S(1)}, u32[]{:S(2)}, u32[]{:S(2)}) collective-permute-start(bf16[2,3,256,256]{3,2,1,0:T(8,128)(2,1)S(1)} %get-tuple-element.38.refs_0_), channel_id=1, source_target_pairs={{0,28},{4,0},{8,4},{12,8},{16,12},{20,16},{24,20},{28,24},{1,29},{... | collective-permute-start | bytes 2359304 | tf_op jit(solution)/shard_map/ppermute | solution.py:25
  10.3 0.7 %collective-permute-done.1.refs_1_ = s32[2,3]{1,0:T(2,128)S(1)} collective-permute-done((s32[2,3]{1,0:T(2,128)}, s32[2,3]{1,0:T(2,128)S(1)}, u32[]{:S(2)}, u32[]{:S(2)}) %collective-permute-start.1) | collective-permute-done | bytes 56 | tf_op jit(solution)/shard_map/ppermute | solution.py:30
  11.0 0.9 %phases.1.refs_3_.refs_2_ = f32[2,2,3,2,2,256]{5,4,3,2,1,0:T(2,128)S(1)} custom-call(s32[2,3]{1,0:T(2,128)S(1)} %copy-done.1, s32[2,3]{1,0:T(2,128)S(1)} %collective-permute-done.1.refs_1_, s32[3,2,4]{2,1,0:T(2,128)S(1)} %bitcast.18, s32[3,2,4]{2,1,0:T(2,128)S(1)} %collective-permute-done.2.refs_3_, s32[4]{0:T(128)S(1)} %copy-done.2), custom_call_target="tpu_custom_call" | custom-call | tf_op jit(solution)/shard_map/phases/pallas_call | solution.py:402
  12.0 6.6 %plane0_120.1.refs_3_ = f32[2,2,2,256,256]{4,3,2,1,0:T(8,128)S(1)} custom-call(bf16[2,3,256,256]{3,2,1,0:T(8,128)(2,1)S(1)} %get-tuple-element.38.refs_0_, bf16[2,3,256,256]{3,2,1,0:T(8,128)(2,1)S(1)} %get-tuple-element.37.refs_1_.refs_0_, f32[3,3,3,2,2,256]{5,4,3,2,1,0:T(2,128)S(1)} %bitcast.19, f32[2,2,3,2,2,256]{5,4,3,2,1,0:T(2,128)S(1)} %phases.1.refs_3_.refs_2_), custom_call_target="tpu_custom_call" | custom-call | flops 17179869184 | bytes 268435456 | tf_op jit(solution)/shard_map/plane0_120/pallas_call | solution.py:199
  18.7 4.4 %collective-permute-start.6 = (bf16[512,256]{1,0:T(8,128)(2,1)S(1)}, bf16[512,256]{1,0:T(8,128)(2,1)S(1)}, u32[]{:S(2)}, u32[]{:S(2)}) collective-permute-start(bf16[512,256]{1,0:T(8,128)(2,1)S(1)} %collective-permute-done.refs_0_), channel_id=1, source_target_pairs={{0,25},{1,24},{4,29},{5,28},{8,17},{9,16},{12,21},{13,20},{16,9},{... | collective-permute-start | bytes 786440 | tf_op jit(solution)/shard_map/ppermute | solution.py:39
  23.1 0.5 %collective-permute-start.5 = (bf16[512,256]{1,0:T(8,128)(2,1)S(1)}, bf16[512,256]{1,0:T(8,128)(2,1)S(1)}, u32[]{:S(2)}, u32[]{:S(2)}) collective-permute-start(bf16[512,256]{1,0:T(8,128)(2,1)S(1)} %collective-permute-done.refs_0_), channel_id=1, source_target_pairs={{0,16},{4,20},{8,24},{12,28},{16,0},{20,4},{24,8},{28,12},{1,17},{... | collective-permute-start | bytes 786440 | tf_op jit(solution)/shard_map/ppermute | solution.py:30
  23.6 0.5 %collective-permute-start.4 = (bf16[512,256]{1,0:T(8,128)(2,1)S(1)}, bf16[512,256]{1,0:T(8,128)(2,1)S(1)}, u32[]{:S(2)}, u32[]{:S(2)}) collective-permute-start(bf16[512,256]{1,0:T(8,128)(2,1)S(1)} %collective-permute-done.refs_0_), channel_id=1, source_target_pairs={{0,8},{4,12},{8,0},{12,4},{16,24},{20,28},{24,16},{28,20},{1,9},{5... | collective-permute-start | bytes 786440 | tf_op jit(solution)/shard_map/ppermute | solution.py:30
  24.1 0.2 collective-permute-start.3
  24.3 5.2 %plane1_12.1.refs_4_ = f32[2,2,2,256,256]{4,3,2,1,0:T(8,128)S(1)} custom-call(bf16[2,3,256,256]{3,2,1,0:T(8,128)(2,1)S(1)} %get-tuple-element.37.refs_1_.refs_0_, f32[3,3,3,2,2,256]{5,4,3,2,1,0:T(2,128)S(1)} %bitcast.20, f32[2,2,3,2,2,256]{5,4,3,2,1,0:T(2,128)S(1)} %phases.1.refs_3_.refs_2_, f32[2,2,2,256,256]{4,3,2,1,0:T(8,128)S(1)} %plane0_120.1.refs_3_), custom_call_target="tpu_custom_call" | custom-call | flops 17179869184 | bytes 268435456 | tf_op jit(solution)/shard_map/plane1_12/pallas_call | solution.py:199
  29.5 3.5 %plane1_0.1 = (f32[4,2,2,32,256]{4,3,2,1,0:T(8,128)S(1)}, bf16[4,2,2,32,256]{4,3,2,1,0:T(8,128)(2,1)S(1)}) custom-call(bf16[2,3,256,256]{3,2,1,0:T(8,128)(2,1)S(1)} %get-tuple-element.37.refs_1_.refs_0_, bf16[2,3,256,256]{3,2,1,0:T(8,128)(2,1)S(1)} %collective-permute-done.7.refs_1_, f32[3,3,3,2,2,256]{5,4,3,2,1,0:T(2,128)S(1)} %bitcast.21, ...), custom_call_target="tpu_custom_call" | custom-call | flops 17179869184 | bytes 268435456 | tf_op jit(solution)/shard_map/plane1_0/pallas_call | solution.py:199
  33.1 1.0 %collective-permute-done.5.refs_3_ = bf16[512,256]{1,0:T(8,128)(2,1)S(1)} collective-permute-done((bf16[512,256]{1,0:T(8,128)(2,1)S(1)}, bf16[512,256]{1,0:T(8,128)(2,1)S(1)}, u32[]{:S(2)}, u32[]{:S(2)}) %collective-permute-start.5) | collective-permute-done | bytes 262176 | tf_op jit(solution)/shard_map/ppermute | solution.py:30
  34.2 0.7 %collective-permute-start.13 = (bf16[512,256]{1,0:T(8,128)(2,1)S(1)}, bf16[512,256]{1,0:T(8,128)(2,1)S(1)}, u32[]{:S(2)}, u32[]{:S(2)}) collective-permute-start(bf16[512,256]{1,0:T(8,128)(2,1)S(1)} %collective-permute-done.3.refs_1_), channel_id=1, source_target_pairs={{0,16},{4,20},{8,24},{12,28},{16,0},{20,4},{24,8},{28,12},{1,17},{... | collective-permute-start | bytes 786440 | tf_op jit(solution)/shard_map/ppermute | solution.py:30
  34.9 1.8 %collective-permute-start.12 = (bf16[512,256]{1,0:T(8,128)(2,1)S(1)}, bf16[512,256]{1,0:T(8,128)(2,1)S(1)}, u32[]{:S(2)}, u32[]{:S(2)}) collective-permute-start(bf16[512,256]{1,0:T(8,128)(2,1)S(1)} %collective-permute-done.4.refs_2_), channel_id=1, source_target_pairs={{0,1},{1,0},{2,3},{3,2},{4,5},{5,4},{6,7},{7,6},{8,9},{9,8},{10,11... | collective-permute-start | bytes 786440 | tf_op jit(solution)/shard_map/ppermute | solution.py:30
  36.6 1.5 %collective-permute-start.14 = (bf16[512,256]{1,0:T(8,128)(2,1)S(1)}, bf16[512,256]{1,0:T(8,128)(2,1)S(1)}, u32[]{:S(2)}, u32[]{:S(2)}) collective-permute-start(bf16[512,256]{1,0:T(8,128)(2,1)S(1)} %collective-permute-done.5.refs_3_), channel_id=1, source_target_pairs={{0,8},{4,12},{8,0},{12,4},{16,24},{20,28},{24,16},{28,20},{1,9},{5... | collective-permute-start | bytes 786440 | tf_op jit(solution)/shard_map/ppermute | solution.py:30
  38.2 1.4 %collective-permute-start.9 = (bf16[128,256]{1,0:T(8,128)(2,1)S(1)}, bf16[128,256]{1,0:T(8,128)(2,1)S(1)}, u32[]{:S(2)}, u32[]{:S(2)}) collective-permute-start(bf16[128,256]{1,0:T(8,128)(2,1)S(1)} %get-tuple-element.29), channel_id=1, source_target_pairs={{0,24},{4,28},{8,16},{12,20},{16,8},{20,12},{24,0},{28,4},{1,25},{... | collective-permute-start | bytes 196616 | tf_op jit(solution)/shard_map/ppermute | solution.py:30
  39.6 0.7 %collective-permute-start.10 = (bf16[128,256]{1,0:T(8,128)(2,1)S(1)}, bf16[128,256]{1,0:T(8,128)(2,1)S(1)}, u32[]{:S(2)}, u32[]{:S(2)}) collective-permute-start(bf16[128,256]{1,0:T(8,128)(2,1)S(1)} %get-tuple-element.30), channel_id=1, source_target_pairs={{0,16},{4,20},{8,24},{12,28},{16,0},{20,4},{24,8},{28,12},{1,17},{... | collective-permute-start | bytes 196616 | tf_op jit(solution)/shard_map/ppermute | solution.py:30
  40.2 3.1 %collective-permute-done.13.refs_1_.refs_6_ = bf16[512,256]{1,0:T(8,128)(2,1)S(1)} collective-permute-done((bf16[512,256]{1,0:T(8,128)(2,1)S(1)}, bf16[512,256]{1,0:T(8,128)(2,1)S(1)}, u32[]{:S(2)}, u32[]{:S(2)}) %collective-permute-start.13) | collective-permute-done | bytes 262176 | tf_op jit(solution)/shard_map/ppermute | solution.py:30
  43.3 0.6 %collective-permute-start.11 = (bf16[128,256]{1,0:T(8,128)(2,1)S(1)}, bf16[128,256]{1,0:T(8,128)(2,1)S(1)}, u32[]{:S(2)}, u32[]{:S(2)}) collective-permute-start(bf16[128,256]{1,0:T(8,128)(2,1)S(1)} %get-tuple-element.31), channel_id=1, source_target_pairs={{0,8},{4,12},{8,0},{12,4},{16,24},{20,28},{24,16},{28,20},{1,9},{5... | collective-permute-start | bytes 196616 | tf_op jit(solution)/shard_map/ppermute | solution.py:30
  44.0 0.1 pack_pieces.2
  44.1 1.7 %collective-permute-done.14.refs_2_.refs_7_ = bf16[512,256]{1,0:T(8,128)(2,1)S(1)} collective-permute-done((bf16[512,256]{1,0:T(8,128)(2,1)S(1)}, bf16[512,256]{1,0:T(8,128)(2,1)S(1)}, u32[]{:S(2)}, u32[]{:S(2)}) %collective-permute-start.14) | collective-permute-done | bytes 262176 | tf_op jit(solution)/shard_map/ppermute | solution.py:30
  45.9 0.9 %collective-permute-done.9.refs_1_ = bf16[128,256]{1,0:T(8,128)(2,1)S(1)} collective-permute-done((bf16[128,256]{1,0:T(8,128)(2,1)S(1)}, bf16[128,256]{1,0:T(8,128)(2,1)S(1)}, u32[]{:S(2)}, u32[]{:S(2)}) %collective-permute-start.9) | collective-permute-done | bytes 65568 | tf_op jit(solution)/shard_map/ppermute | solution.py:30
  46.8 0.8 %collective-permute-done.11.refs_3_ = bf16[128,256]{1,0:T(8,128)(2,1)S(1)} collective-permute-done((bf16[128,256]{1,0:T(8,128)(2,1)S(1)}, bf16[128,256]{1,0:T(8,128)(2,1)S(1)}, u32[]{:S(2)}, u32[]{:S(2)}) %collective-permute-start.11) | collective-permute-done | bytes 65568 | tf_op jit(solution)/shard_map/ppermute | solution.py:30
  47.6 0.3 left_operand.1.left_ref
  47.9 0.4 collective-permute-done.16.refs_9_
  48.3 2.0 %quark_products.1 = f32[2,16,2,32,256]{4,3,2,1,0:T(8,128)} custom-call(bf16[128,512]{1,0:T(8,128)(2,1)S(1)} %left_operand.1.left_ref, bf16[512,256]{1,0:T(8,128)(2,1)S(1)} %collective-permute-done.refs_0_, bf16[512,256]{1,0:T(8,128)(2,1)S(1)} %collective-permute-done.3.refs_1_, bf16[512,256]{1,0:T(8,128)(2,1)S(1)} %collective-permute-done.4.refs_2_, ...), custom_call_target="tpu_custom_call" | custom-call | flops 536870912 | bytes 7340032 | tf_op jit(solution)/shard_map/quark_products/pallas_call | solution.py:460
  (23 shorter events, 0.4 us)
Async XLA Ops:
  1.2 17.4 %collective-permute-start = (bf16[512,256]{1,0:T(8,128)(2,1)S(1)}, bf16[512,256]{1,0:T(8,128)(2,1)S(1)}, u32[]{:S(2)}, u32[]{:S(2)}) collective-permute-start(bf16[512,256]{1,0:T(8,128)(2,1)S(1)} %reshape.10), channel_id=1, source_target_pairs={{0,2},{2,0},{1,3},{3,1},{4,6},{6,4},{5,7},{7,5},{8,10},{10,8},{9,1... | collective-permute-start | bytes 786440 | tf_op jit(solution)/shard_map/ppermute | solution.py:25
  5.3 5.7 %collective-permute-start.1 = (s32[2,3]{1,0:T(2,128)}, s32[2,3]{1,0:T(2,128)S(1)}, u32[]{:S(2)}, u32[]{:S(2)}) collective-permute-start(s32[2,3]{1,0:T(2,128)} %refs_0_), channel_id=1, source_target_pairs={{0,1},{1,0},{2,3},{3,2},{4,5},{5,4},{6,7},{7,6},{8,9},{9,8},{10,11... | collective-permute-start | bytes 80 | tf_op jit(solution)/shard_map/ppermute | solution.py:30
  6.9 4.1 %collective-permute-start.2 = (s32[3,2,4]{2,1,0:T(2,128)}, s32[3,2,4]{2,1,0:T(2,128)S(1)}, u32[]{:S(2)}, u32[]{:S(2)}) collective-permute-start(s32[3,2,4]{2,1,0:T(2,128)} %bitcast.17), channel_id=1, source_target_pairs={{0,1},{1,0},{2,3},{3,2},{4,5},{5,4},{6,7},{7,6},{8,9},{9,8},{10,11... | collective-permute-start | bytes 296 | tf_op jit(solution)/shard_map/ppermute | solution.py:30
  9.0 2.0 %copy-start = (s32[4,2,3]{0,1,2:T(2,128)S(1)}, s32[4,2,3]{0,1,2:T(2,128)}, u32[]{:S(2)}) copy-start(s32[4,2,3]{0,1,2:T(2,128)} %param.9) | copy-start | bytes 292
  9.0 2.0 %copy-start.1 = (s32[2,3]{1,0:T(2,128)S(1)}, s32[2,3]{1,0:T(2,128)}, u32[]{:S(2)}) copy-start(s32[2,3]{1,0:T(2,128)} %refs_0_) | copy-start | bytes 76
  9.0 2.0 %copy-start.2 = (s32[4]{0:T(128)S(1)}, s32[4]{0:T(128)}, u32[]{:S(2)}) copy-start(s32[4]{0:T(128)} %refs_4_.1) | copy-start | bytes 52
  9.1 2.9 %copy-start.3 = (f32[1,3,3,3,2,2,256]{6,5,4,3,2,1,0:T(2,128)S(1)}, f32[1,3,3,3,2,2,256]{6,5,4,3,2,1,0:T(2,128)}, u32[]{:S(2)}) copy-start(f32[1,3,3,3,2,2,256]{6,5,4,3,2,1,0:T(2,128)} %param.7) | copy-start | bytes 331780
  9.2 20.3 %collective-permute-start.7 = (bf16[2,3,256,256]{3,2,1,0:T(8,128)(2,1)S(1)}, bf16[2,3,256,256]{3,2,1,0:T(8,128)(2,1)S(1)}, u32[]{:S(2)}, u32[]{:S(2)}) collective-permute-start(bf16[2,3,256,256]{3,2,1,0:T(8,128)(2,1)S(1)} %get-tuple-element.38.refs_0_), channel_id=1, source_target_pairs={{0,28},{4,0},{8,4},{12,8},{16,12},{20,16},{24,20},{28,24},{1,29},{... | collective-permute-start | bytes 2359304 | tf_op jit(solution)/shard_map/ppermute | solution.py:25
  18.7 14.5 %collective-permute-start.6 = (bf16[512,256]{1,0:T(8,128)(2,1)S(1)}, bf16[512,256]{1,0:T(8,128)(2,1)S(1)}, u32[]{:S(2)}, u32[]{:S(2)}) collective-permute-start(bf16[512,256]{1,0:T(8,128)(2,1)S(1)} %collective-permute-done.refs_0_), channel_id=1, source_target_pairs={{0,25},{1,24},{4,29},{5,28},{8,17},{9,16},{12,21},{13,20},{16,9},{... | collective-permute-start | bytes 786440 | tf_op jit(solution)/shard_map/ppermute | solution.py:39
  23.1 11.1 %collective-permute-start.5 = (bf16[512,256]{1,0:T(8,128)(2,1)S(1)}, bf16[512,256]{1,0:T(8,128)(2,1)S(1)}, u32[]{:S(2)}, u32[]{:S(2)}) collective-permute-start(bf16[512,256]{1,0:T(8,128)(2,1)S(1)} %collective-permute-done.refs_0_), channel_id=1, source_target_pairs={{0,16},{4,20},{8,24},{12,28},{16,0},{20,4},{24,8},{28,12},{1,17},{... | collective-permute-start | bytes 786440 | tf_op jit(solution)/shard_map/ppermute | solution.py:30
  23.6 10.5 %collective-permute-start.4 = (bf16[512,256]{1,0:T(8,128)(2,1)S(1)}, bf16[512,256]{1,0:T(8,128)(2,1)S(1)}, u32[]{:S(2)}, u32[]{:S(2)}) collective-permute-start(bf16[512,256]{1,0:T(8,128)(2,1)S(1)} %collective-permute-done.refs_0_), channel_id=1, source_target_pairs={{0,8},{4,12},{8,0},{12,4},{16,24},{20,28},{24,16},{28,20},{1,9},{5... | collective-permute-start | bytes 786440 | tf_op jit(solution)/shard_map/ppermute | solution.py:30
  24.1 10.0 %collective-permute-start.3 = (bf16[512,256]{1,0:T(8,128)(2,1)S(1)}, bf16[512,256]{1,0:T(8,128)(2,1)S(1)}, u32[]{:S(2)}, u32[]{:S(2)}) collective-permute-start(bf16[512,256]{1,0:T(8,128)(2,1)S(1)} %collective-permute-done.refs_0_), channel_id=1, source_target_pairs={{0,1},{1,0},{2,3},{3,2},{4,5},{5,4},{6,7},{7,6},{8,9},{9,8},{10,11... | collective-permute-start | bytes 786440 | tf_op jit(solution)/shard_map/ppermute | solution.py:30
  33.1 5.1 %collective-permute-start.8 = (bf16[4,2,2,32,256]{4,3,2,1,0:T(8,128)(2,1)S(1)}, bf16[4,2,2,32,256]{4,3,2,1,0:T(8,128)(2,1)S(1)}, u32[]{:S(2)}, u32[]{:S(2)}) collective-permute-start(bf16[4,2,2,32,256]{4,3,2,1,0:T(8,128)(2,1)S(1)} %get-tuple-element.27), channel_id=1, source_target_pairs={{0,4},{4,0},{8,12},{12,8},{16,20},{20,16},{24,28},{28,24},{1,5},{5... | collective-permute-start | bytes 786440 | tf_op jit(solution)/shard_map/ppermute | solution.py:30
  34.2 9.2 %collective-permute-start.13 = (bf16[512,256]{1,0:T(8,128)(2,1)S(1)}, bf16[512,256]{1,0:T(8,128)(2,1)S(1)}, u32[]{:S(2)}, u32[]{:S(2)}) collective-permute-start(bf16[512,256]{1,0:T(8,128)(2,1)S(1)} %collective-permute-done.3.refs_1_), channel_id=1, source_target_pairs={{0,16},{4,20},{8,24},{12,28},{16,0},{20,4},{24,8},{28,12},{1,17},{... | collective-permute-start | bytes 786440 | tf_op jit(solution)/shard_map/ppermute | solution.py:30
  34.9 9.2 %collective-permute-start.12 = (bf16[512,256]{1,0:T(8,128)(2,1)S(1)}, bf16[512,256]{1,0:T(8,128)(2,1)S(1)}, u32[]{:S(2)}, u32[]{:S(2)}) collective-permute-start(bf16[512,256]{1,0:T(8,128)(2,1)S(1)} %collective-permute-done.4.refs_2_), channel_id=1, source_target_pairs={{0,1},{1,0},{2,3},{3,2},{4,5},{5,4},{6,7},{7,6},{8,9},{9,8},{10,11... | collective-permute-start | bytes 786440 | tf_op jit(solution)/shard_map/ppermute | solution.py:30
  36.6 9.2 %collective-permute-start.14 = (bf16[512,256]{1,0:T(8,128)(2,1)S(1)}, bf16[512,256]{1,0:T(8,128)(2,1)S(1)}, u32[]{:S(2)}, u32[]{:S(2)}) collective-permute-start(bf16[512,256]{1,0:T(8,128)(2,1)S(1)} %collective-permute-done.5.refs_3_), channel_id=1, source_target_pairs={{0,8},{4,12},{8,0},{12,4},{16,24},{20,28},{24,16},{28,20},{1,9},{5... | collective-permute-start | bytes 786440 | tf_op jit(solution)/shard_map/ppermute | solution.py:30
  38.2 8.6 %collective-permute-start.9 = (bf16[128,256]{1,0:T(8,128)(2,1)S(1)}, bf16[128,256]{1,0:T(8,128)(2,1)S(1)}, u32[]{:S(2)}, u32[]{:S(2)}) collective-permute-start(bf16[128,256]{1,0:T(8,128)(2,1)S(1)} %get-tuple-element.29), channel_id=1, source_target_pairs={{0,24},{4,28},{8,16},{12,20},{16,8},{20,12},{24,0},{28,4},{1,25},{... | collective-permute-start | bytes 196616 | tf_op jit(solution)/shard_map/ppermute | solution.py:30
  39.6 7.2 %collective-permute-start.10 = (bf16[128,256]{1,0:T(8,128)(2,1)S(1)}, bf16[128,256]{1,0:T(8,128)(2,1)S(1)}, u32[]{:S(2)}, u32[]{:S(2)}) collective-permute-start(bf16[128,256]{1,0:T(8,128)(2,1)S(1)} %get-tuple-element.30), channel_id=1, source_target_pairs={{0,16},{4,20},{8,24},{12,28},{16,0},{20,4},{24,8},{28,12},{1,17},{... | collective-permute-start | bytes 196616 | tf_op jit(solution)/shard_map/ppermute | solution.py:30
  43.3 4.3 %collective-permute-start.11 = (bf16[128,256]{1,0:T(8,128)(2,1)S(1)}, bf16[128,256]{1,0:T(8,128)(2,1)S(1)}, u32[]{:S(2)}, u32[]{:S(2)}) collective-permute-start(bf16[128,256]{1,0:T(8,128)(2,1)S(1)} %get-tuple-element.31), channel_id=1, source_target_pairs={{0,8},{4,12},{8,0},{12,4},{16,24},{20,28},{24,16},{28,20},{1,9},{5... | collective-permute-start | bytes 196616 | tf_op jit(solution)/shard_map/ppermute | solution.py:30
  44.0 4.2 %collective-permute-start.15 = (bf16[5,512,256]{2,1,0:T(8,128)(2,1)S(1)}, bf16[5,512,256]{2,1,0:T(8,128)(2,1)S(1)}, u32[]{:S(2)}, u32[]{:S(2)}) collective-permute-start(bf16[5,512,256]{2,1,0:T(8,128)(2,1)S(1)} %pack_pieces.2), channel_id=1, source_target_pairs={{0,4},{4,0},{8,12},{12,8},{16,20},{20,16},{24,28},{28,24},{1,5},{5... | collective-permute-start | bytes 3932168 | tf_op jit(solution)/shard_map/ppermute | solution.py:30
  45.9 2.4 %collective-permute-start.16 = (bf16[3,512,256]{2,1,0:T(8,128)(2,1)S(1)}, bf16[3,512,256]{2,1,0:T(8,128)(2,1)S(1)}, u32[]{:S(2)}, u32[]{:S(2)}) collective-permute-start(bf16[3,512,256]{2,1,0:T(8,128)(2,1)S(1)} %pack_pieces.3), channel_id=1, source_target_pairs={{0,4},{4,0},{8,12},{12,8},{16,20},{20,16},{24,28},{28,24},{1,5},{5... | collective-permute-start | bytes 2359304 | tf_op jit(solution)/shard_map/ppermute | solution.py:30
